TPU v7x, 128 devices: a whole 4x4x4 slice. The times are simulated.
128 devices in a mesh: passage: 2 (over x_hi), brick: 64 (over z, y, x_lo, core).
Axes of the slice: x: 4 (x_hi: 2, x_lo: 2; x = x_hi * 2 + x_lo), y: 4, z: 4, core: 2. Of those that a mesh axis runs over, the one named last changes fastest.
Arguments:
- jac_blocks: bfloat16 [2, 25, 64, 8192], P('passage', None, None, 'brick'), may hold values from -6 to 6
- psi_start: float32 [2, 10, 64, 64, 128], P('passage', None, 'brick'), may hold values from -6 to 6
- source: float32 [2, 10, 64, 64, 128], P('passage', None, 'brick'), may hold values from -6 to 6
- pseudo_step: float32 [2, 64, 64, 128], P('passage', 'brick'), may hold values from 0.1 to 0.4
- dissipation: float32 [2, 64, 64, 128], P('passage', 'brick'), may hold values from 0.04 to 0.15
- freq_volume: float32 [2, 64, 64, 128], P('passage', 'brick'), may hold values from 0.2 to 2
- normals: float32 [2, 3, 64, 64], P('passage', None, 'brick'), may hold values from -6 to 6
- face_owner: int32 [2, 4096, 1], P('passage', 'brick'), may hold values from 0 to 63; in each aligned block of 64 rows (0 to 63, 64 to 127, ..., all dimensions but the last counted through in order) at most 4 rows name the same one
- face_slot: int32 [2, 4096], P('passage', 'brick'), may hold values from 0 to 255
Outputs:
- adjoint: float32 [2, 10, 64, 64, 128], P('passage', None, 'brick')
- sensitivity: float32 [2, 6, 16384], P('passage', None, 'brick')
Inputs may be any that keep to these rules, and one draw needn't show every extreme that they name: `face_owner`: in the 64 faces of one device (aligned blocks of the rows), no brick is named by more than 4 faces, and in some block some brick is named by exactly 4.
All inputs are finite; a program needn't handle non-finite values.
Results may differ from a plain program's by a relative error of at most 0.0003.
Values may be sent and summed in bfloat16 or wider, within the bound.
No kernel may reach another device: no remote copies, remote signals or barrier semaphores. Data moves between devices by JAX's collectives and lax.ppermute only.
A program may use at most 64 MiB of HBM per device.

v0:
```python
import math

import jax
import jax.numpy as jnp
from jax import lax
from jax.sharding import PartitionSpec as P

NODE_DEV = 256
SWEEPS = 2
ND = 1
BLADES = 36


def padded(value, sides, width, wrap):
    for axis, dim in sides:
        peers, length = (lax.axis_size(axis), value.shape[dim])
        up = [(i, (i + 1) % peers) for i in range(peers if wrap else peers - 1)]
        down = [(j, i) for i, j in up]
        last = lax.slice_in_dim(value, length - width, length, axis=dim)
        initial = lax.slice_in_dim(value, 0, width, axis=dim)
        before = lax.ppermute(last, axis, up)
        after = lax.ppermute(initial, axis, down)
        value = jnp.concatenate([before, value, after], axis=dim)
    return value


def rotate(rim, turn):
    cosine = math.cos(turn)
    sine = math.sin(turn)
    real_part = rim[:, :5]
    imag_part = rim[:, 5:]
    return jnp.concatenate(
        [real_part * cosine - imag_part * sine, real_part * sine + imag_part * cosine], axis=1
    )


def transpose_apply(tiles, diff):
    total_real = jnp.zeros_like(diff[:, :5])
    total_imag = jnp.zeros_like(diff[:, :5])
    for row_index in range(5):
        column = tiles[:, row_index * 5 : row_index * 5 + 5].astype(jnp.float32)
        total_real = total_real + column * diff[:, row_index : row_index + 1]
        total_imag = total_imag + column * diff[:, 5 + row_index : 6 + row_index]
    return jnp.concatenate([total_real, total_imag], axis=1)


def advance(
    state,
    source,
    pseudo_step,
    dissipation,
    freq_volume,
    convect_fn,
    cycle_index,
    passes,
    phase_angle,
):
    padded_i = padded(state, (("brick", 2),), 1, False)
    padded_j = padded(state.astype(jnp.bfloat16), (("passage", 3),), 1, True).astype(state.dtype)
    below_rim = padded_j[:, :, :, :1]
    above_rim = padded_j[:, :, :, -1:]
    below_rim = jnp.where(cycle_index == 0, rotate(below_rim, -phase_angle), below_rim)
    above_rim = jnp.where(cycle_index == passes - 1, rotate(above_rim, phase_angle), above_rim)
    fixed_j = jnp.concatenate([below_rim, state, above_rim], axis=3)
    padded_k = jnp.pad(state, ((0, 0), (0, 0), (0, 0), (0, 0), (1, 1)))
    beside = padded_i[:, :, 2:] + padded_i[:, :, :-2]
    beside = beside + fixed_j[:, :, :, 2:] + fixed_j[:, :, :, :-2]
    beside = beside + padded_k[..., 2:] + padded_k[..., :-2]
    diff = 0.5 * (padded_i[:, :, 2:] - padded_i[:, :, :-2])
    convect = convect_fn(diff)
    omega = freq_volume[:, None]
    spin = jnp.concatenate([omega * state[:, 5:], -omega * state[:, :5]], axis=1)
    resid = convect + spin + dissipation[:, None] * (6.0 * state - beside) - source
    return state - pseudo_step[:, None] * resid


def body(
    jac_blocks,
    psi_start,
    source,
    pseudo_step,
    dissipation,
    freq_volume,
    normals,
    face_owner,
    face_slot,
):
    passes = lax.axis_size("passage")
    cycle_index = lax.axis_index("passage")
    bricks = lax.axis_size("brick")
    planes = psi_start.shape[2]
    width_j = psi_start.shape[3]
    width_k = psi_start.shape[4]
    phase_angle = 2.0 * math.pi * ND * passes / BLADES

    def convect_fn(diff):
        flattened = diff.reshape(1, 10, planes, width_j * width_k)
        spread = lax.all_to_all(flattened, "brick", split_axis=3, concat_axis=2, tiled=True)
        products = transpose_apply(jac_blocks, spread)
        returned = lax.all_to_all(products, "brick", split_axis=2, concat_axis=3, tiled=True)
        return returned.reshape(1, 10, planes, width_j, width_k)

    state = psi_start
    for sweep in range(SWEEPS):
        state = advance(
            state,
            source,
            pseudo_step,
            dissipation,
            freq_volume,
            convect_fn,
            cycle_index,
            passes,
            phase_angle,
        )
    wall_state = state[0, :, :, :, 0]
    face_normals = normals[0]
    values = jnp.concatenate(
        [face_normals * wall_state[1:4], face_normals * wall_state[6:9]], axis=0
    )
    values = values.reshape(6, planes * width_j)
    owners = face_owner[0, :, 0]
    slots = face_slot[0]
    node_ids = owners * NODE_DEV + slots
    local_terms = jnp.zeros((6, NODE_DEV * bricks), jnp.float32).at[:, node_ids].add(values)
    summed = lax.psum_scatter(local_terms, "brick", scatter_dimension=1, tiled=True)
    sensitivity = summed[None]
    return (state, sensitivity)


def solution(mesh):
    placed = (
        P("passage", None, None, "brick"),
        P("passage", None, "brick", None, None),
        P("passage", None, "brick", None, None),
        P("passage", "brick", None, None),
        P("passage", "brick", None, None),
        P("passage", "brick", None, None),
        P("passage", None, "brick", None),
        P("passage", "brick", None),
        P("passage", "brick"),
    )
    return jax.shard_map(
        body,
        mesh=mesh,
        in_specs=placed,
        out_specs=(P("passage", None, "brick", None, None), P("passage", None, "brick")),
        check_vma=False,
    )
```

profile of v0, /device:TPU:1, one launch (start us, length us, event | category | flops | bytes accessed | tf_op | source)
XLA Modules:
  0.0 551.5 jit_solution(5108275818433556031)
XLA Ops:
  7.2 3.3 collective-permute-start
  10.5 3.1 collective-permute-start.1
  14.8 2.8 collective-permute-start.2
  21.6 6.4 %copy.214 = f32[1,10,1,8192]{1,2,0,3:T(1,128)} copy(f32[1,10,1,8192]{3,2,1,0:T(1,128)S(1)} %bitcast.85) | data formatting | bytes 655360 | tf_op jit(solution)/shard_map/reshape | solution.py:97
  28.4 38.4 %reduce = f32[8192,10]{1,0:T(8,128)} reduce(f32[8192,1,1,10]{3,2,1,0:T(1,128)} %bitcast.79, f32[]{:T(128)} %broadcast.92), dimensions={1,2}, to_apply=%bitcast.74.reduce_sub_computation | reduce | bytes 655364
  66.9 5.8 %reshape.331 = f32[64,1,1280]{2,1,0:T(1,128)} reshape(f32[8192,10]{1,0:T(8,128)} %reduce) | data formatting | bytes 655360
  72.7 12.3 %all-to-all-start = ((f32[64,1,1280]{2,1,0:T(1,128)}), f32[64,1,1280]{2,1,0:T(1,128)S(1)}, u32[]{:S(2)}, u32[]{:S(2)}) async-start(f32[64,1,1280]{2,1,0:T(1,128)} %reshape.331), calls=%async_computation | async-start | bytes 655360 | tf_op jit(solution)/shard_map/all_to_all | solution.py:98
  85.1 10.6 %all-to-all-done = f32[64,1,1280]{2,1,0:T(1,128)S(1)} async-done(((f32[64,1,1280]{2,1,0:T(1,128)}), f32[64,1,1280]{2,1,0:T(1,128)S(1)}, u32[]{:S(2)}, u32[]{:S(2)}) %all-to-all-start) | async-done | bytes 327712 | tf_op jit(solution)/shard_map/all_to_all | solution.py:98
  97.1 7.9 %reshape.332 = f32[8192,1,1,10]{3,2,1,0:T(1,128)} reshape(f32[64,1280]{1,0:T(8,128)S(1)} %reduce.1) | data formatting | bytes 655360
  105.0 7.9 %copy.215 = f32[1,10,1,8192]{3,0,1,2:T(1,128)S(1)} copy(f32[1,10,1,8192]{1,2,0,3:T(1,128)} %bitcast.80) | data formatting | bytes 655360 | tf_op jit(solution)/shard_map/all_to_all | solution.py:98
  114.2 4.5 all-to-all-start.1
  118.8 10.8 %all-to-all-done.1 = f32[1,10,64,128]{3,0,1,2:T(1,128)S(1)} async-done(((f32[1,10,64,128]{3,0,1,2:T(1,128)}), f32[1,10,64,128]{3,0,1,2:T(1,128)S(1)}, u32[]{:S(2)}, u32[]{:S(2)}) %all-to-all-start.1) | async-done | bytes 327712 | tf_op jit(solution)/shard_map/all_to_all | solution.py:100
  134.0 3.2 collective-permute-start.5
  141.3 6.4 %copy.230 = f32[1,10,1,8192]{1,2,0,3:T(1,128)} copy(f32[1,10,1,8192]{3,2,1,0:T(1,128)S(1)} %bitcast.86) | data formatting | bytes 655360 | tf_op jit(solution)/shard_map/reshape | solution.py:97
  147.7 38.4 %reduce.2 = f32[8192,10]{1,0:T(8,128)} reduce(f32[8192,1,1,10]{3,2,1,0:T(1,128)} %bitcast.81, f32[]{:T(128)} %broadcast.92), dimensions={1,2}, to_apply=%bitcast.76.reduce_sub_computation | reduce | bytes 655364
  186.1 5.8 %reshape.333 = f32[64,1,1280]{2,1,0:T(1,128)} reshape(f32[8192,10]{1,0:T(8,128)} %reduce.2) | data formatting | bytes 655360
  191.9 8.8 %all-to-all-start.2 = ((f32[64,1,1280]{2,1,0:T(1,128)}), f32[64,1,1280]{2,1,0:T(1,128)S(1)}, u32[]{:S(2)}, u32[]{:S(2)}) async-start(f32[64,1,1280]{2,1,0:T(1,128)} %reshape.333), calls=%async_computation.2 | async-start | bytes 655360 | tf_op jit(solution)/shard_map/all_to_all | solution.py:98
  200.8 10.6 %all-to-all-done.2 = f32[64,1,1280]{2,1,0:T(1,128)S(1)} async-done(((f32[64,1,1280]{2,1,0:T(1,128)}), f32[64,1,1280]{2,1,0:T(1,128)S(1)}, u32[]{:S(2)}, u32[]{:S(2)}) %all-to-all-start.2) | async-done | bytes 327712 | tf_op jit(solution)/shard_map/all_to_all | solution.py:98
  212.9 7.9 %reshape.334 = f32[8192,1,1,10]{3,2,1,0:T(1,128)} reshape(f32[64,1280]{1,0:T(8,128)S(1)} %reduce.3) | data formatting | bytes 655360
  220.7 7.9 %copy.231 = f32[1,10,1,8192]{3,0,1,2:T(1,128)S(1)} copy(f32[1,10,1,8192]{1,2,0,3:T(1,128)} %bitcast.82) | data formatting | bytes 655360 | tf_op jit(solution)/shard_map/all_to_all | solution.py:98
  229.9 4.8 all-to-all-start.3
  234.8 10.7 %all-to-all-done.3 = f32[1,10,64,128]{3,0,1,2:T(1,128)S(1)} async-done(((f32[1,10,64,128]{3,0,1,2:T(1,128)}), f32[1,10,64,128]{3,0,1,2:T(1,128)S(1)}, u32[]{:S(2)}, u32[]{:S(2)}) %all-to-all-start.3) | async-done | bytes 327712 | tf_op jit(solution)/shard_map/all_to_all | solution.py:100
  247.8 4.5 scatter_custom_fusion
  253.2 290.0 %reduce-scatter.2.cloned.1.call-done = f32[6,256]{0,1:T(8,128)} async-done(((f32[6,16384]{0,1:T(8,128)}), f32[6,256]{0,1:T(8,128)}) %reduce-scatter.2.cloned.1.call-update) | async-done | bytes 6160 | tf_op jit(solution)/shard_map/reduce_scatter | solution.py:126
  (71 shorter events, 24.3 us)
Async XLA Ops:
  7.2 14.3 %collective-permute-start = (f32[1,10,1,64,128]{4,3,2,1,0:T(8,128)}, f32[1,10,1,64,128]{4,3,2,1,0:T(8,128)S(1)}, u32[]{:S(2)}, u32[]{:S(2)}) collective-permute-start(f32[1,10,1,64,128]{4,3,2,1,0:T(8,128)} %param.10), channel_id=1, source_target_pairs={{1,0},{2,1},{3,2},{4,3},{5,4},{6,5},{7,6},{8,7},{9,8},{10,9},{11,1... | collective-permute-start | bytes 983048 | tf_op jit(solution)/shard_map/ppermute | solution.py:22
  10.5 11.0 %collective-permute-start.1 = (f32[1,10,1,64,128]{4,3,2,1,0:T(8,128)}, f32[1,10,1,64,128]{4,3,2,1,0:T(8,128)S(1)}, u32[]{:S(2)}, u32[]{:S(2)}) collective-permute-start(f32[1,10,1,64,128]{4,3,2,1,0:T(8,128)} %param.10), channel_id=1, source_target_pairs={{0,1},{1,2},{2,3},{3,4},{4,5},{5,6},{6,7},{7,8},{8,9},{9,10},{10,1... | collective-permute-start | bytes 983048 | tf_op jit(solution)/shard_map/ppermute | solution.py:21
  14.8 70.3 %collective-permute-start.2 = (bf16[1,10,1,1,128]{4,1,3,2,0:T(8,128)(2,1)S(1)}, bf16[1,10,1,1,128]{4,1,3,2,0:T(8,128)(2,1)S(1)}, u32[]{:S(2)}, u32[]{:S(2)}) collective-permute-start(bf16[1,10,1,1,128]{4,1,3,2,0:T(8,128)(2,1)S(1)} %get-tuple-element.66), channel_id=1, source_target_pairs={{0,64},{64,0},{1,65},{65,1},{2,66},{66,2},{3,67},{67,3},{4,68},{68... | collective-permute-start | bytes 7688 | tf_op jit(solution)/shard_map/ppermute | solution.py:21
  17.6 67.5 %collective-permute-start.3 = (bf16[1,10,1,1,128]{4,1,3,2,0:T(8,128)(2,1)S(1)}, bf16[1,10,1,1,128]{4,1,3,2,0:T(8,128)(2,1)S(1)}, u32[]{:S(2)}, u32[]{:S(2)}) collective-permute-start(bf16[1,10,1,1,128]{4,1,3,2,0:T(8,128)(2,1)S(1)} %get-tuple-element.67), channel_id=1, source_target_pairs={{64,0},{0,64},{65,1},{1,65},{66,2},{2,66},{67,3},{3,67},{68,4},{4,... | collective-permute-start | bytes 7688 | tf_op jit(solution)/shard_map/ppermute | solution.py:22
  21.5 63.5 %copy-start.6 = (s32[1,64]{1,0:T(1,128)S(1)}, s32[1,64]{1,0:T(1,128)}, u32[]{:S(2)}) copy-start(s32[1,64]{1,0:T(1,128)} %param.17) | copy-start | bytes 772
  21.5 63.5 %copy-start.7 = (s32[1,64,1]{1,2,0:T(1,128)S(1)}, s32[1,64,1]{1,2,0:T(1,128)}, u32[]{:S(2)}) copy-start(s32[1,64,1]{1,2,0:T(1,128)} %param.16) | copy-start | bytes 772
  66.9 46.1 %copy-start = (bf16[1,25,64,128]{3,2,1,0:T(8,128)(2,1)S(1)}, bf16[1,25,64,128]{3,2,1,0:T(8,128)(2,1)}, u32[]{:S(2)}) copy-start(bf16[1,25,64,128]{3,2,1,0:T(8,128)(2,1)} %param.9) | copy-start | bytes 1228804
  72.7 56.9 %copy-start.1 = (f32[1,10,1,64,128]{4,3,2,1,0:T(8,128)S(1)}, f32[1,10,1,64,128]{4,3,2,1,0:T(8,128)}, u32[]{:S(2)}) copy-start(f32[1,10,1,64,128]{4,3,2,1,0:T(8,128)} %param.11) | copy-start | bytes 983044
  72.7 56.9 %copy-start.3 = (f32[1,1,64,128]{3,2,1,0:T(8,128)S(1)}, f32[1,1,64,128]{3,2,1,0:T(8,128)}, u32[]{:S(2)}) copy-start(f32[1,1,64,128]{3,2,1,0:T(8,128)} %param.13) | copy-start | bytes 98308
  72.7 56.9 %copy-start.4 = (f32[1,1,64,128]{3,2,1,0:T(8,128)S(1)}, f32[1,1,64,128]{3,2,1,0:T(8,128)}, u32[]{:S(2)}) copy-start(f32[1,1,64,128]{3,2,1,0:T(8,128)} %param.12) | copy-start | bytes 98308
  72.7 23.0 %all-to-all-start = ((f32[64,1,1280]{2,1,0:T(1,128)}), f32[64,1,1280]{2,1,0:T(1,128)S(1)}, u32[]{:S(2)}, u32[]{:S(2)}) async-start(f32[64,1,1280]{2,1,0:T(1,128)} %reshape.331), calls=%async_computation | async-start | bytes 655360 | tf_op jit(solution)/shard_map/all_to_all | solution.py:98
  97.1 43.2 %copy-start.2 = (f32[1,1,64,128]{3,2,1,0:T(8,128)S(1)}, f32[1,1,64,128]{3,2,1,0:T(8,128)}, u32[]{:S(2)}) copy-start(f32[1,1,64,128]{3,2,1,0:T(8,128)} %param.14) | copy-start | bytes 98308
  114.2 15.3 %all-to-all-start.1 = ((f32[1,10,64,128]{3,0,1,2:T(1,128)}), f32[1,10,64,128]{3,0,1,2:T(1,128)S(1)}, u32[]{:S(2)}, u32[]{:S(2)}) async-start(f32[1,10,64,128]{3,0,1,2:T(1,128)} %copy.216), calls=%async_computation.1 | async-start | bytes 655360 | tf_op jit(solution)/shard_map/all_to_all | solution.py:100
  131.6 9.7 %collective-permute-start.4 = (f32[1,10,1,64,128]{4,3,2,1,0:T(8,128)S(1)}, f32[1,10,1,64,128]{4,3,2,1,0:T(8,128)S(1)}, u32[]{:S(2)}, u32[]{:S(2)}) collective-permute-start(f32[1,10,1,64,128]{4,3,2,1,0:T(8,128)S(1)} %copy.228), channel_id=1, source_target_pairs={{1,0},{2,1},{3,2},{4,3},{5,4},{6,5},{7,6},{8,7},{9,8},{10,9},{11,1... | collective-permute-start | bytes 983048 | tf_op jit(solution)/shard_map/ppermute | solution.py:22
  134.0 7.3 %collective-permute-start.5 = (f32[1,10,1,64,128]{4,3,2,1,0:T(8,128)S(1)}, f32[1,10,1,64,128]{4,3,2,1,0:T(8,128)S(1)}, u32[]{:S(2)}, u32[]{:S(2)}) collective-permute-start(f32[1,10,1,64,128]{4,3,2,1,0:T(8,128)S(1)} %copy.228), channel_id=1, source_target_pairs={{0,1},{1,2},{2,3},{3,4},{4,5},{5,6},{6,7},{7,8},{8,9},{9,10},{10,1... | collective-permute-start | bytes 983048 | tf_op jit(solution)/shard_map/ppermute | solution.py:21
  137.2 63.5 %collective-permute-start.6 = (bf16[1,10,1,1,128]{4,1,3,2,0:T(8,128)(2,1)S(1)}, bf16[1,10,1,1,128]{4,1,3,2,0:T(8,128)(2,1)S(1)}, u32[]{:S(2)}, u32[]{:S(2)}) collective-permute-start(bf16[1,10,1,1,128]{4,1,3,2,0:T(8,128)(2,1)S(1)} %get-tuple-element.64), channel_id=1, source_target_pairs={{0,64},{64,0},{1,65},{65,1},{2,66},{66,2},{3,67},{67,3},{4,68},{68... | collective-permute-start | bytes 7688 | tf_op jit(solution)/shard_map/ppermute | solution.py:21
  139.8 61.0 %collective-permute-start.7 = (bf16[1,10,1,1,128]{4,1,3,2,0:T(8,128)(2,1)S(1)}, bf16[1,10,1,1,128]{4,1,3,2,0:T(8,128)(2,1)S(1)}, u32[]{:S(2)}, u32[]{:S(2)}) collective-permute-start(bf16[1,10,1,1,128]{4,1,3,2,0:T(8,128)(2,1)S(1)} %get-tuple-element.65), channel_id=1, source_target_pairs={{64,0},{0,64},{65,1},{1,65},{66,2},{2,66},{67,3},{3,67},{68,4},{4,... | collective-permute-start | bytes 7688 | tf_op jit(solution)/shard_map/ppermute | solution.py:22
  191.9 19.5 %all-to-all-start.2 = ((f32[64,1,1280]{2,1,0:T(1,128)}), f32[64,1,1280]{2,1,0:T(1,128)S(1)}, u32[]{:S(2)}, u32[]{:S(2)}) async-start(f32[64,1,1280]{2,1,0:T(1,128)} %reshape.333), calls=%async_computation.2 | async-start | bytes 655360 | tf_op jit(solution)/shard_map/all_to_all | solution.py:98
  212.8 34.8 %copy-start.5 = (f32[1,3,1,64]{3,2,1,0:T(1,128)S(1)}, f32[1,3,1,64]{3,2,1,0:T(1,128)}, u32[]{:S(2)}) copy-start(f32[1,3,1,64]{3,2,1,0:T(1,128)} %param.15) | copy-start | bytes 2308
  229.9 15.6 %all-to-all-start.3 = ((f32[1,10,64,128]{3,0,1,2:T(1,128)}), f32[1,10,64,128]{3,0,1,2:T(1,128)S(1)}, u32[]{:S(2)}, u32[]{:S(2)}) async-start(f32[1,10,64,128]{3,0,1,2:T(1,128)} %copy.232), calls=%async_computation.3 | async-start | bytes 655360 | tf_op jit(solution)/shard_map/all_to_all | solution.py:100
  234.7 308.4 %reduce-scatter.2.cloned.1.call-start = ((), (), s32[]{:S(2)}) async-start(), calls=%async_computation.5 | async-start | bytes 8519680 | tf_op jit(solution)/shard_map/reduce_scatter | solution.py:126
Sparse Core Ops, SparseCore 0:
  252.5 290.6 reduce-scatter.1
where the time goes:
time: 557 us; the launch traced here: 552 us
  waiting for transfers between devices  333 us (60%)
  other arithmetic  91.8 us (16%)
  local copies, waits for them, and re-layouts  63.8 us (11%)
  starting transfers between devices  48.5 us (9%)
  between operations  14.4 us (3%)
    reduce_scatter x1, waiting for transfers between devices, body(): lax.psum_scatter(local_terms, 'brick', scatter_dimension=1, tiled=True)  290 us
    unnamed x2, other arithmetic  76.9 us
    unnamed x25, local copies, waits for them, and re-layouts  32.6 us
    all_to_all x2, waiting for transfers between devices, convect_fn(): lax.all_to_all(products, 'brick', split_axis=2, concat_axis=3, tiled=True)  21.5 us
    all_to_all x2, waiting for transfers between devices, convect_fn(): lax.all_to_all(flattened, 'brick', split_axis=3, concat_axis=2, tiled=True)  21.2 us
    all_to_all x2, starting transfers between devices, convect_fn(): lax.all_to_all(flattened, 'brick', split_axis=3, concat_axis=2, tiled=True)  21.1 us
    all_to_all x2, local copies, waits for them, and re-layouts, convect_fn(): lax.all_to_all(flattened, 'brick', split_axis=3, concat_axis=2, tiled=True)  15.8 us
    reshape x2, local copies, waits for them, and re-layouts, convect_fn(): flattened = diff.reshape(1, 10, planes, width_j * width_k)  12.7 us
  transfers between devices with their start and end apart: 13, of which 6 were waited for; matrix products, arithmetic and copies ran while one was open for 20% of the time, Pallas kernels for 0%

commit v1 on v0

v1 whole, which is shorter than its diff:
```python
import functools
import math

import jax
import jax.numpy as jnp
from jax import lax
from jax.experimental import pallas as pl
from jax.experimental.pallas import tpu as pltpu
from jax.sharding import PartitionSpec as P

NODE_DEV = 256
CAP = 4
ND = 1
BLADES = 36
ROWS = 32
SLOT_ROW = 25
VMEM_BYTES = 40 * 1024 * 1024
F32 = jnp.float32
BF16 = jnp.bfloat16


def lanes(shape):
    return lax.broadcasted_iota(jnp.int32, shape, len(shape) - 1)


def rows(shape):
    return lax.broadcasted_iota(jnp.int32, shape, len(shape) - 2)


def prep_kernel(
    jac_ref, low_ref, high_ref, owner_ref, slot_ref, normals_ref, send_ref, rim_ref, weight_ref, route_ref, wide
):
    faces = owner_ref.shape[0]
    planes = jac_ref.shape[1]
    rim_ref[...] = jnp.zeros_like(rim_ref)
    for c in range(10):
        rim_ref[0, c : c + 1, :] = low_ref[0, c, 0, 0:1, :]
        rim_ref[1, c : c + 1, :] = high_ref[0, c, 0, 7:8, :]

    square = (faces, faces)
    eye = rows(square) == lanes(square)
    owner_col = owner_ref[...].astype(F32)
    owner_row = jnp.sum(jnp.where(eye, owner_col, 0.0), axis=0, keepdims=True)
    slot_col = jnp.sum(jnp.where(eye, slot_ref[...].astype(F32), 0.0), axis=1, keepdims=True)
    earlier = (owner_col == owner_row) & (lanes(square) < rows(square))
    rank = jnp.sum(jnp.where(earlier, 1.0, 0.0), axis=1, keepdims=True)
    route = jnp.where(rows(square).astype(F32) == owner_row, 1.0, 0.0)
    route_ref[...] = route
    lane = lanes((faces, 128))
    table = jnp.where(lane.astype(F32) == rank, slot_col + 1.0, 0.0)
    slots = jnp.dot(route.astype(BF16), table.astype(BF16), preferred_element_type=F32)
    weight = jnp.zeros((faces, 128), F32)
    for d in range(3):
        normal = jnp.sum(jnp.where(eye, normals_ref[d], 0.0), axis=1, keepdims=True)
        hit = ((lane % 8) == d) | ((lane % 8) == d + 3)
        weight = jnp.where(hit, normal, weight)
    weight_ref[...] = jnp.where((lane // 8).astype(F32) == rank, weight, 0.0)

    for e in range(25):
        wide[e * planes : (e + 1) * planes, :] = jac_ref[e].astype(F32)
    wide[SLOT_ROW * planes : (SLOT_ROW + 1) * planes, :] = slots
    wide[(SLOT_ROW + 1) * planes : ROWS * planes, :] = jnp.zeros(((ROWS - SLOT_ROW - 1) * planes, 128), F32)
    for i in range(planes):
        send_ref[i] = wide[pl.ds(i, ROWS, stride=planes), :].astype(BF16)


def sweep_block(b, blocks, passage, phase, u_ref, lo_ref, hi_ref, rim_ref, tile, source_ref, step_ref, diss_ref, freq_ref):
    at = slice(8 * b, 8 * b + 8)
    shape = (8, 128)
    row, lane = rows(shape), lanes(shape)
    u = [u_ref[c, at, :] for c in range(10)]

    def rotated(rim, turn, turned):
        cosine = jnp.where(turned, math.cos(turn), 1.0)
        sine = jnp.where(turned, math.sin(turn), 0.0)
        re = [rim[n] * cosine - rim[5 + n] * sine for n in range(5)]
        im = [rim[n] * sine + rim[5 + n] * cosine for n in range(5)]
        return re + im

    if b == 0:
        before = rotated([rim_ref[1, c : c + 1, :] for c in range(10)], -phase, passage == 0)
    else:
        before = [u_ref[c, 8 * b - 1 : 8 * b, :] for c in range(10)]
    if b == blocks - 1:
        after = rotated([rim_ref[0, c : c + 1, :] for c in range(10)], phase, passage == 1)
    else:
        after = [u_ref[c, 8 * b + 8 : 8 * b + 9, :] for c in range(10)]

    diff = []
    beside = []
    for c in range(10):
        lo, hi = lo_ref[c, at, :], hi_ref[c, at, :]
        diff.append(0.5 * (hi - lo))
        down = jnp.where(row == 0, before[c], pltpu.roll(u[c], 1, axis=0))
        up = jnp.where(row == 7, after[c], pltpu.roll(u[c], 7, axis=0))
        left = jnp.where(lane == 0, 0.0, pltpu.roll(u[c], 1, axis=1))
        right = jnp.where(lane == 127, 0.0, pltpu.roll(u[c], 127, axis=1))
        beside.append(hi + lo + up + down + right + left)
    conv = [None] * 10
    for n in range(5):
        for m in range(5):
            t = tile(5 * n + m)
            re, im = t * diff[n], t * diff[5 + n]
            conv[m] = re if n == 0 else conv[m] + re
            conv[5 + m] = im if n == 0 else conv[5 + m] + im
    step, diss, omega = step_ref[at, :], diss_ref[at, :], freq_ref[at, :]
    new = []
    for c in range(10):
        spin = omega * u[c + 5] if c < 5 else -(omega * u[c - 5])
        resid = conv[c] + spin + diss * (6.0 * u[c] - beside[c]) - source_ref[c, at, :]
        new.append(u[c] - step * resid)
    return new


def first_kernel(
    phase, recv_ref, u_ref, lo_ref, hi_ref, rim_ref, source_ref, step_ref, diss_ref, freq_ref,
    out_ref, tiles_ref, slots_ref, rim_out_ref, wide,
):
    passage = lax.axis_index("passage")
    width = u_ref.shape[1]
    for j in range(width):
        wide[j * ROWS : (j + 1) * ROWS, :] = recv_ref[j].astype(F32)
    slots_ref[...] = wide[pl.ds(SLOT_ROW, width, stride=ROWS), :]
    for e in range(25):
        tiles_ref[e] = wide[pl.ds(e, width, stride=ROWS), :].astype(BF16)
    rim_out_ref[...] = jnp.zeros_like(rim_out_ref)
    blocks = width // 8
    for b in range(blocks):
        new = sweep_block(
            b, blocks, passage, phase, u_ref, lo_ref, hi_ref, rim_ref,
            lambda e: wide[pl.ds(8 * b * ROWS + e, 8, stride=ROWS), :],
            source_ref, step_ref, diss_ref, freq_ref,
        )
        for c in range(10):
            out_ref[c, 8 * b : 8 * b + 8, :] = new[c]
            if b == 0:
                rim_out_ref[0, c : c + 1, :] = new[c][0:1]
            if b == blocks - 1:
                rim_out_ref[1, c : c + 1, :] = new[c][7:8]


def second_kernel(
    phase, tiles_ref, u_ref, lo_ref, hi_ref, rim_ref, source_ref, step_ref, diss_ref, freq_ref, weight_ref, route_ref,
    out_ref, send_ref,
):
    passage = lax.axis_index("passage")
    width = u_ref.shape[1]
    blocks = width // 8
    for b in range(blocks):
        new = sweep_block(
            b, blocks, passage, phase, u_ref, lo_ref, hi_ref, rim_ref,
            lambda e: tiles_ref[e, 8 * b : 8 * b + 8, :].astype(F32),
            source_ref, step_ref, diss_ref, freq_ref,
        )
        for c in range(10):
            out_ref[c, 8 * b : 8 * b + 8, :] = new[c]
    lane = lanes((width, 128)) % 8
    wall = jnp.zeros((width, 128), F32)
    for k, c in enumerate((1, 2, 3, 6, 7, 8)):
        wall = jnp.where(lane == k, out_ref[c, :, 0:1], wall)
    routed = jnp.dot(
        route_ref[...], weight_ref[...] * wall, precision=lax.Precision.HIGHEST, preferred_element_type=F32
    )
    for q in range(send_ref.shape[0]):
        send_ref[q] = routed[q : q + 1, :]


def nodes_kernel(recv_ref, slots_ref, out_ref, dense):
    peers = slots_ref.shape[0]
    for q in range(peers):
        dense[q : q + 1, :] = recv_ref[q]
    total = jnp.zeros((8, NODE_DEV), F32)
    node = lanes((peers, NODE_DEV)).astype(F32) + 1.0
    turned = dense[...].T
    for r in range(CAP):
        hit = jnp.where(slots_ref[:, r : r + 1] == node, 1.0, 0.0)
        total = total + jnp.dot(
            turned[8 * r : 8 * r + 8, :], hit, precision=lax.Precision.HIGHEST, preferred_element_type=F32
        )
    out_ref[...] = total[0:6, :]


def kernel_call(body, out, scratch=(), ins=None):
    options = {} if ins is None else {"grid": (1,), "in_specs": ins[0], "out_specs": ins[1]}
    if ins is None:
        whole = pl.BlockSpec(memory_space=pltpu.VMEM)
        options = {"out_specs": [whole] * len(out)}
    return pl.pallas_call(
        body,
        out_shape=[jax.ShapeDtypeStruct(s, d) for s, d in out],
        scratch_shapes=list(scratch),
        compiler_params=pltpu.CompilerParams(vmem_limit_bytes=VMEM_BYTES),
        **options,
    )


def planes_beside(state, bricks):
    up = [(i, i + 1) for i in range(bricks - 1)]
    down = [(j, i) for i, j in up]
    return lax.ppermute(state, "brick", up), lax.ppermute(state, "brick", down)


def swapped(rim, passes):
    return lax.ppermute(rim, "passage", [(i, (i + 1) % passes) for i in range(passes)])


def body(
    jac_blocks,
    psi_start,
    source,
    pseudo_step,
    dissipation,
    freq_volume,
    normals,
    face_owner,
    face_slot,
):
    passes = lax.axis_size("passage")
    bricks = lax.axis_size("brick")
    width, depth = psi_start.shape[3], psi_start.shape[4]
    phase = 2.0 * math.pi * ND * passes / BLADES
    field = (10, width, depth)
    rim = (2, 16, depth)

    def whole(shape):
        return pl.BlockSpec(shape, lambda _: (0,) * len(shape))

    psi = psi_start.reshape(field)
    jac = jac_blocks.reshape(25, bricks, depth)
    source = source.reshape(field)
    scalars = [a.reshape(width, depth) for a in (pseudo_step, dissipation, freq_volume)]

    lo, hi = planes_beside(psi, bricks)
    edge = (1, 10, 1, 8, depth)
    last = width // 8 - 1
    outs = [((bricks, ROWS, depth), BF16), (rim, F32), ((width, 128), F32), ((bricks, width), F32)]
    send, rims, weight, route = kernel_call(
        prep_kernel,
        outs,
        [pltpu.VMEM((ROWS * bricks, depth), F32)],
        (
            [
                whole(jac.shape),
                pl.BlockSpec(edge, lambda _: (0, 0, 0, 0, 0)),
                pl.BlockSpec(edge, lambda _: (0, 0, 0, last, 0)),
                whole((width, 1)),
                whole((1, width)),
                whole((3, 1, width)),
            ],
            [whole(s) for s, _ in outs],
        ),
    )(jac, psi_start, psi_start, face_owner.reshape(width, 1), face_slot, normals.reshape(3, 1, width))
    recv = lax.all_to_all(send, "brick", 0, 0, tiled=True)
    rims = swapped(rims, passes)

    state, tiles, slots, rims = kernel_call(
        functools.partial(first_kernel, phase),
        [(field, F32), ((25, width, depth), BF16), ((bricks, 128), F32), (rim, F32)],
        [pltpu.VMEM((ROWS * width, depth), F32)],
    )(recv, psi, lo, hi, rims, source, *scalars)

    lo, hi = planes_beside(state, bricks)
    rims = swapped(rims, passes)
    state, routed = kernel_call(
        functools.partial(second_kernel, phase), [(field, F32), ((bricks, 1, 128), F32)]
    )(tiles, state, lo, hi, rims, source, *scalars, weight, route)

    arrived = lax.all_to_all(routed, "brick", 0, 0, tiled=True)
    (sensitivity,) = kernel_call(
        nodes_kernel, [((6, NODE_DEV), F32)], [pltpu.VMEM((bricks, 128), F32)]
    )(arrived, slots)
    return state.reshape(psi_start.shape), sensitivity[None]


def solution(mesh):
    placed = (
        P("passage", None, None, "brick"),
        P("passage", None, "brick", None, None),
        P("passage", None, "brick", None, None),
        P("passage", "brick", None, None),
        P("passage", "brick", None, None),
        P("passage", "brick", None, None),
        P("passage", None, "brick", None),
        P("passage", "brick", None),
        P("passage", "brick"),
    )
    return jax.shard_map(
        body,
        mesh=mesh,
        in_specs=placed,
        out_specs=(P("passage", None, "brick", None, None), P("passage", None, "brick")),
        check_vma=False,
    )
```

time: 557 us -> 66.6 us (0.12)
  waiting for transfers between devices: 333 us -> 10.2 us
  other arithmetic: 91.8 us -> 0 us
  local copies, waits for them, and re-layouts: 63.8 us -> 4.03 us
  starting transfers between devices: 48.5 us -> 27.6 us
  blocking collectives: 0 us -> 19.6 us
  between operations: 14.4 us -> 0.75 us
    reduce_scatter x1 -> x0, waiting for transfers between devices: 290 us -> none  [body(): lax.psum_scatter(local_terms, 'brick', scatter_dimension=1, tiled=True)]
    unnamed x2 -> x0, other arithmetic: 76.9 us -> none
    all_to_all x4 -> x1, waiting for transfers between devices: 42.7 us -> 0.01 us  [body(): recv = lax.all_to_all(send, 'brick', 0, 0, tiled=True)]
    unnamed x25 -> x21, local copies, waits for them, and re-layouts: 32.6 us -> 3.93 us
    all_to_all x0 -> x1, blocking collectives: none -> 19.6 us  [body(): arrived = lax.all_to_all(routed, 'brick', 0, 0, tiled=True)]
    all_to_all x4 -> x1, starting transfers between devices: 30.4 us -> 11.1 us  [body(): recv = lax.all_to_all(send, 'brick', 0, 0, tiled=True)]
    all_to_all x2 -> x0, local copies, waits for them, and re-layouts: 15.8 us -> none  [convect_fn(): lax.all_to_all(flattened, 'brick', split_axis=3, concat_axis=2, tiled=True)]
    reshape x3 -> x1, local copies, waits for them, and re-layouts: 12.8 us -> 0.1 us  [body(): face_owner.reshape(width, 1)]
  transfers between devices with their start and end apart: 13 -> 7, of which waited for: 6 -> 3; matrix products, arithmetic and copies ran while one was open for 20% -> 0% of each run, Pallas kernels for 0% -> 0%
where the time goes in v1:
time: 66.6 us; the launch traced here: 66.2 us
  starting transfers between devices  27.6 us (41%)
  blocking collectives  19.6 us (29%)
  waiting for transfers between devices  10.2 us (15%)
  Pallas kernels  4.12 us (6%)
  local copies, waits for them, and re-layouts  4.03 us (6%)
  between operations  0.75 us (1%)
    all_to_all x1, blocking collectives, body(): arrived = lax.all_to_all(routed, 'brick', 0, 0, tiled=True)  19.6 us
    all_to_all x1, starting transfers between devices, body(): recv = lax.all_to_all(send, 'brick', 0, 0, tiled=True)  11.1 us
    ppermute x2, waiting for transfers between devices, swapped(): lax.ppermute(rim, 'passage', [(i, (i + 1) % passes) for i in range(passes)])  9.24 us
    ppermute x2, starting transfers between devices, planes_beside(): lax.ppermute(state, 'brick', up)  7.89 us
    ppermute x2, starting transfers between devices, swapped(): lax.ppermute(rim, 'passage', [(i, (i + 1) % passes) for i in range(passes)])  4.34 us
    ppermute x2, starting transfers between devices, planes_beside(): lax.ppermute(state, 'brick', down)  4.28 us
    unnamed x21, local copies, waits for them, and re-layouts  3.93 us
    pallas_call x1, Pallas kernels, body(): kernel_call(prep_kernel, outs, [pltpu.VMEM((ROWS * bricks, depth), F32)],...  1.66 us
  transfers between devices with their start and end apart: 7, of which 3 were waited for; matrix products, arithmetic and copies ran while one was open for 0% of the time, Pallas kernels for 0%

profile of v1, /device:TPU:1, one launch (start us, length us, event | category | flops | bytes accessed | tf_op | source)
XLA Modules:
  0.0 66.2 jit_solution(13917165501940936717)
XLA Ops:
  0.6 0.6 copy-done.9
  1.3 0.1 copy.11.owner_ref
  1.4 0.7 %copy-done.7 = f32[1,3,1,64]{3,2,1,0:T(1,128)S(1)} copy-done((f32[1,3,1,64]{3,2,1,0:T(1,128)S(1)}, f32[1,3,1,64]{3,2,1,0:T(1,128)}, u32[]{:S(2)}) %copy-start.7) | copy-done | bytes 792
  2.1 1.0 %copy-done = f32[1,10,1,64,128]{4,3,2,1,0:T(8,128)S(1)} copy-done((f32[1,10,1,64,128]{4,3,2,1,0:T(8,128)S(1)}, f32[1,10,1,64,128]{4,3,2,1,0:T(8,128)}, u32[]{:S(2)}) %copy-start) | copy-done | bytes 327704
  3.0 1.0 %copy-done.3 = bf16[1,25,64,128]{3,2,1,0:T(8,128)(2,1)S(1)} copy-done((bf16[1,25,64,128]{3,2,1,0:T(8,128)(2,1)S(1)}, bf16[1,25,64,128]{3,2,1,0:T(8,128)(2,1)}, u32[]{:S(2)}) %copy-start.3) | copy-done | bytes 409624
  4.0 1.7 %shard_map.104 = (bf16[64,32,128]{2,1,0:T(8,128)(2,1)}, f32[2,16,128]{2,1,0:T(8,128)S(1)}, f32[64,128]{1,0:T(8,128)S(1)}, f32[64,64]{1,0:T(8,128)S(1)}) custom-call(bf16[25,64,128]{2,1,0:T(8,128)(2,1)S(1)} %bitcast.17, f32[1,10,1,64,128]{4,3,2,1,0:T(8,128)S(1)} %copy-done, f32[1,10,1,64,128]{4,3,2,1,0:T(8,128)S(1)} %copy-done, s32[64,1]{1,0:T(8,128)S(1)} %copy.11.owner_ref, ...), custom_call_target="tpu_custom_call" | custom-call | tf_op jit(solution)/shard_map/pallas_call | solution.py:237
  5.7 0.0 copy-start.6
  5.7 11.1 %all-to-all-start = ((bf16[64,32,128]{2,1,0:T(8,128)(2,1)}), bf16[64,32,128]{2,1,0:T(8,128)(2,1)S(1)}, u32[]{:S(2)}, u32[]{:S(2)}) async-start(bf16[64,32,128]{2,1,0:T(8,128)(2,1)} %get-tuple-element.12), calls=%async_computation | async-start | bytes 1048576 | tf_op jit(solution)/shard_map/all_to_all | solution.py:253
  16.8 2.4 %collective-permute-start.1 = (f32[10,64,128]{2,1,0:T(8,128)S(1)}, f32[10,64,128]{2,1,0:T(8,128)S(1)}, u32[]{:S(2)}, u32[]{:S(2)}) collective-permute-start(f32[10,64,128]{2,1,0:T(8,128)S(1)} %bitcast.12), channel_id=1, source_target_pairs={{1,0},{2,1},{3,2},{4,3},{5,4},{6,5},{7,6},{8,7},{9,8},{10,9},{11,1... | collective-permute-start | bytes 983048 | tf_op jit(solution)/shard_map/ppermute | solution.py:200
  19.2 3.2 %collective-permute-start = (f32[10,64,128]{2,1,0:T(8,128)S(1)}, f32[10,64,128]{2,1,0:T(8,128)S(1)}, u32[]{:S(2)}, u32[]{:S(2)}) collective-permute-start(f32[10,64,128]{2,1,0:T(8,128)S(1)} %bitcast.13), channel_id=1, source_target_pairs={{0,1},{1,2},{2,3},{3,4},{4,5},{5,6},{6,7},{7,8},{8,9},{9,10},{10,1... | collective-permute-start | bytes 983048 | tf_op jit(solution)/shard_map/ppermute | solution.py:200
  22.4 2.5 %collective-permute-start.2 = (f32[2,16,128]{2,1,0:T(8,128)S(1)}, f32[2,16,128]{2,1,0:T(8,128)S(1)}, u32[]{:S(2)}, u32[]{:S(2)}) collective-permute-start(f32[2,16,128]{2,1,0:T(8,128)S(1)} %get-tuple-element.13), channel_id=1, source_target_pairs={{0,64},{64,0},{1,65},{65,1},{2,66},{66,2},{3,67},{67,3},{4,68},{68... | collective-permute-start | bytes 49160 | tf_op jit(solution)/shard_map/ppermute | solution.py:204
  24.9 4.7 %collective-permute-done.2.rim_ref = f32[2,16,128]{2,1,0:T(8,128)S(1)} collective-permute-done((f32[2,16,128]{2,1,0:T(8,128)S(1)}, f32[2,16,128]{2,1,0:T(8,128)S(1)}, u32[]{:S(2)}, u32[]{:S(2)}) %collective-permute-start.2) | collective-permute-done | bytes 16416 | tf_op jit(solution)/shard_map/ppermute | solution.py:204
  29.6 0.9 %collective-permute-done.1.hi_ref = f32[10,64,128]{2,1,0:T(8,128)S(1)} collective-permute-done((f32[10,64,128]{2,1,0:T(8,128)S(1)}, f32[10,64,128]{2,1,0:T(8,128)S(1)}, u32[]{:S(2)}, u32[]{:S(2)}) %collective-permute-start.1) | collective-permute-done | bytes 327712 | tf_op jit(solution)/shard_map/ppermute | solution.py:200
  30.6 0.0 collective-permute-done.lo_ref
  30.6 0.0 all-to-all-done.recv_ref
  30.6 0.9 %shard_map.105 = (f32[10,64,128]{2,1,0:T(8,128)S(1)}, bf16[25,64,128]{2,1,0:T(8,128)(2,1)S(1)}, f32[64,128]{1,0:T(8,128)S(1)}, f32[2,16,128]{2,1,0:T(8,128)S(1)}) custom-call(bf16[64,32,128]{2,1,0:T(8,128)(2,1)S(1)} %all-to-all-done.recv_ref, f32[10,64,128]{2,1,0:T(8,128)S(1)} %bitcast.14, f32[10,64,128]{2,1,0:T(8,128)S(1)} %collective-permute-done.lo_ref, ...), custom_call_target="tpu_custom_call" | custom-call | tf_op jit(solution)/shard_map/pallas_call | solution.py:256
  31.6 1.9 %collective-permute-start.4 = (f32[10,64,128]{2,1,0:T(8,128)S(1)}, f32[10,64,128]{2,1,0:T(8,128)S(1)}, u32[]{:S(2)}, u32[]{:S(2)}) collective-permute-start(f32[10,64,128]{2,1,0:T(8,128)S(1)} %get-tuple-element.15.u_ref), channel_id=1, source_target_pairs={{1,0},{2,1},{3,2},{4,3},{5,4},{6,5},{7,6},{8,7},{9,8},{10,9},{11,1... | collective-permute-start | bytes 983048 | tf_op jit(solution)/shard_map/ppermute | solution.py:200
  33.5 4.7 %collective-permute-start.3 = (f32[10,64,128]{2,1,0:T(8,128)S(1)}, f32[10,64,128]{2,1,0:T(8,128)S(1)}, u32[]{:S(2)}, u32[]{:S(2)}) collective-permute-start(f32[10,64,128]{2,1,0:T(8,128)S(1)} %get-tuple-element.15.u_ref), channel_id=1, source_target_pairs={{0,1},{1,2},{2,3},{3,4},{4,5},{5,6},{6,7},{7,8},{8,9},{9,10},{10,1... | collective-permute-start | bytes 983048 | tf_op jit(solution)/shard_map/ppermute | solution.py:200
  38.2 1.8 %collective-permute-start.5 = (f32[2,16,128]{2,1,0:T(8,128)S(1)}, f32[2,16,128]{2,1,0:T(8,128)S(1)}, u32[]{:S(2)}, u32[]{:S(2)}) collective-permute-start(f32[2,16,128]{2,1,0:T(8,128)S(1)} %get-tuple-element.16), channel_id=1, source_target_pairs={{0,64},{64,0},{1,65},{65,1},{2,66},{66,2},{3,67},{67,3},{4,68},{68... | collective-permute-start | bytes 49160 | tf_op jit(solution)/shard_map/ppermute | solution.py:204
  40.0 4.5 %collective-permute-done.5.rim_ref = f32[2,16,128]{2,1,0:T(8,128)S(1)} collective-permute-done((f32[2,16,128]{2,1,0:T(8,128)S(1)}, f32[2,16,128]{2,1,0:T(8,128)S(1)}, u32[]{:S(2)}, u32[]{:S(2)}) %collective-permute-start.5) | collective-permute-done | bytes 16416 | tf_op jit(solution)/shard_map/ppermute | solution.py:204
  44.5 1.2 %shard_map.106 = (f32[10,64,128]{2,1,0:T(8,128)}, f32[64,1,128]{2,1,0:T(1,128)S(1)}) custom-call(bf16[25,64,128]{2,1,0:T(8,128)(2,1)S(1)} %get-tuple-element.14.tiles_ref, f32[10,64,128]{2,1,0:T(8,128)S(1)} %get-tuple-element.15.u_ref, f32[10,64,128]{2,1,0:T(8,128)S(1)} %collective-permute-done.3.lo_ref, f32[10,64,128]{2,1,0:T(8,128)S(1)} %collective-permute-done.4.hi_ref, ...), custom_call_target="tpu_custom_call" | custom-call | tf_op jit(solution)/shard_map/pallas_call | solution.py:264
  45.7 19.6 %all_to_all.10.recv_ref = f32[64,1,128]{2,1,0:T(1,128)S(1)} all-to-all(f32[64,1,128]{2,1,0:T(1,128)S(1)} %get-tuple-element.20), channel_id=1, replica_groups=mesh['passage'=2,'brick'=64] {'brick'}, dimensions={0} | all-to-all | bytes 65536 | tf_op jit(solution)/shard_map/all_to_all | solution.py:268
  65.3 0.3 shard_map.107
  65.6 0.6 copy.13
  (17 shorter events, 0.0 us)
Async XLA Ops:
  0.6 0.7 copy-start.9
  1.4 0.7 %copy-start.7 = (f32[1,3,1,64]{3,2,1,0:T(1,128)S(1)}, f32[1,3,1,64]{3,2,1,0:T(1,128)}, u32[]{:S(2)}) copy-start(f32[1,3,1,64]{3,2,1,0:T(1,128)} %param.15) | copy-start | bytes 2308
  1.4 0.7 %copy-start.8 = (s32[1,64]{1,0:T(1,128)S(1)}, s32[1,64]{1,0:T(1,128)}, u32[]{:S(2)}) copy-start(s32[1,64]{1,0:T(1,128)} %slot_ref.1) | copy-start | bytes 772
  2.1 1.0 %copy-start = (f32[1,10,1,64,128]{4,3,2,1,0:T(8,128)S(1)}, f32[1,10,1,64,128]{4,3,2,1,0:T(8,128)}, u32[]{:S(2)}) copy-start(f32[1,10,1,64,128]{4,3,2,1,0:T(8,128)} %high_ref.1) | copy-start | bytes 983044
  3.0 1.0 %copy-start.3 = (bf16[1,25,64,128]{3,2,1,0:T(8,128)(2,1)S(1)}, bf16[1,25,64,128]{3,2,1,0:T(8,128)(2,1)}, u32[]{:S(2)}) copy-start(bf16[1,25,64,128]{3,2,1,0:T(8,128)(2,1)} %param.9) | copy-start | bytes 1228804
  5.7 11.1 %copy-start.1 = (f32[1,10,1,64,128]{4,3,2,1,0:T(8,128)S(1)}, f32[1,10,1,64,128]{4,3,2,1,0:T(8,128)}, u32[]{:S(2)}) copy-start(f32[1,10,1,64,128]{4,3,2,1,0:T(8,128)} %high_ref.1) | copy-start | bytes 983044
  5.7 24.9 %copy-start.2 = (f32[1,10,1,64,128]{4,3,2,1,0:T(8,128)S(1)}, f32[1,10,1,64,128]{4,3,2,1,0:T(8,128)}, u32[]{:S(2)}) copy-start(f32[1,10,1,64,128]{4,3,2,1,0:T(8,128)} %param.11) | copy-start | bytes 983044
  5.7 24.9 %copy-start.4 = (f32[1,1,64,128]{3,2,1,0:T(8,128)S(1)}, f32[1,1,64,128]{3,2,1,0:T(8,128)}, u32[]{:S(2)}) copy-start(f32[1,1,64,128]{3,2,1,0:T(8,128)} %param.12) | copy-start | bytes 98308
  5.7 24.9 %copy-start.5 = (f32[1,1,64,128]{3,2,1,0:T(8,128)S(1)}, f32[1,1,64,128]{3,2,1,0:T(8,128)}, u32[]{:S(2)}) copy-start(f32[1,1,64,128]{3,2,1,0:T(8,128)} %param.13) | copy-start | bytes 98308
  5.7 24.9 %copy-start.6 = (f32[1,1,64,128]{3,2,1,0:T(8,128)S(1)}, f32[1,1,64,128]{3,2,1,0:T(8,128)}, u32[]{:S(2)}) copy-start(f32[1,1,64,128]{3,2,1,0:T(8,128)} %param.14) | copy-start | bytes 98308
  5.7 24.8 %all-to-all-start = ((bf16[64,32,128]{2,1,0:T(8,128)(2,1)}), bf16[64,32,128]{2,1,0:T(8,128)(2,1)S(1)}, u32[]{:S(2)}, u32[]{:S(2)}) async-start(bf16[64,32,128]{2,1,0:T(8,128)(2,1)} %get-tuple-element.12), calls=%async_computation | async-start | bytes 1048576 | tf_op jit(solution)/shard_map/all_to_all | solution.py:253
  16.8 13.7 %collective-permute-start.1 = (f32[10,64,128]{2,1,0:T(8,128)S(1)}, f32[10,64,128]{2,1,0:T(8,128)S(1)}, u32[]{:S(2)}, u32[]{:S(2)}) collective-permute-start(f32[10,64,128]{2,1,0:T(8,128)S(1)} %bitcast.12), channel_id=1, source_target_pairs={{1,0},{2,1},{3,2},{4,3},{5,4},{6,5},{7,6},{8,7},{9,8},{10,9},{11,1... | collective-permute-start | bytes 983048 | tf_op jit(solution)/shard_map/ppermute | solution.py:200
  19.2 11.4 %collective-permute-start = (f32[10,64,128]{2,1,0:T(8,128)S(1)}, f32[10,64,128]{2,1,0:T(8,128)S(1)}, u32[]{:S(2)}, u32[]{:S(2)}) collective-permute-start(f32[10,64,128]{2,1,0:T(8,128)S(1)} %bitcast.13), channel_id=1, source_target_pairs={{0,1},{1,2},{2,3},{3,4},{4,5},{5,6},{6,7},{7,8},{8,9},{9,10},{10,1... | collective-permute-start | bytes 983048 | tf_op jit(solution)/shard_map/ppermute | solution.py:200
  22.4 7.2 %collective-permute-start.2 = (f32[2,16,128]{2,1,0:T(8,128)S(1)}, f32[2,16,128]{2,1,0:T(8,128)S(1)}, u32[]{:S(2)}, u32[]{:S(2)}) collective-permute-start(f32[2,16,128]{2,1,0:T(8,128)S(1)} %get-tuple-element.13), channel_id=1, source_target_pairs={{0,64},{64,0},{1,65},{65,1},{2,66},{66,2},{3,67},{67,3},{4,68},{68... | collective-permute-start | bytes 49160 | tf_op jit(solution)/shard_map/ppermute | solution.py:204
  31.6 13.0 %collective-permute-start.4 = (f32[10,64,128]{2,1,0:T(8,128)S(1)}, f32[10,64,128]{2,1,0:T(8,128)S(1)}, u32[]{:S(2)}, u32[]{:S(2)}) collective-permute-start(f32[10,64,128]{2,1,0:T(8,128)S(1)} %get-tuple-element.15.u_ref), channel_id=1, source_target_pairs={{1,0},{2,1},{3,2},{4,3},{5,4},{6,5},{7,6},{8,7},{9,8},{10,9},{11,1... | collective-permute-start | bytes 983048 | tf_op jit(solution)/shard_map/ppermute | solution.py:200
  33.5 11.0 %collective-permute-start.3 = (f32[10,64,128]{2,1,0:T(8,128)S(1)}, f32[10,64,128]{2,1,0:T(8,128)S(1)}, u32[]{:S(2)}, u32[]{:S(2)}) collective-permute-start(f32[10,64,128]{2,1,0:T(8,128)S(1)} %get-tuple-element.15.u_ref), channel_id=1, source_target_pairs={{0,1},{1,2},{2,3},{3,4},{4,5},{5,6},{6,7},{7,8},{8,9},{9,10},{10,1... | collective-permute-start | bytes 983048 | tf_op jit(solution)/shard_map/ppermute | solution.py:200
  38.2 6.3 %collective-permute-start.5 = (f32[2,16,128]{2,1,0:T(8,128)S(1)}, f32[2,16,128]{2,1,0:T(8,128)S(1)}, u32[]{:S(2)}, u32[]{:S(2)}) collective-permute-start(f32[2,16,128]{2,1,0:T(8,128)S(1)} %get-tuple-element.16), channel_id=1, source_target_pairs={{0,64},{64,0},{1,65},{65,1},{2,66},{66,2},{3,67},{67,3},{4,68},{68... | collective-permute-start | bytes 49160 | tf_op jit(solution)/shard_map/ppermute | solution.py:204

commit v2 on v1

v2 whole, which is shorter than its diff:
```python
import functools
import math

import jax
import jax.numpy as jnp
from jax import lax
from jax.experimental import pallas as pl
from jax.experimental.pallas import tpu as pltpu
from jax.sharding import PartitionSpec as P

NODE_DEV = 256
CAP = 4
ND = 1
BLADES = 36
ROWS = 32
BLOCK = 16
FULL = 32000.0
VMEM_BYTES = 40 * 1024 * 1024
F32 = jnp.float32
BF16 = jnp.bfloat16
I16 = jnp.int16


def lanes(shape):
    return lax.broadcasted_iota(jnp.int32, shape, len(shape) - 1)


def rows(shape):
    return lax.broadcasted_iota(jnp.int32, shape, len(shape) - 2)


def prep_kernel(jac_ref, send_ref, wide):
    planes = jac_ref.shape[1]
    wide[25 * planes : ROWS * planes, :] = jnp.zeros(((ROWS - 25) * planes, 128), F32)
    for e in range(25):
        wide[e * planes : (e + 1) * planes, :] = jac_ref[e].astype(F32)
    for i in range(planes):
        send_ref[i] = wide[pl.ds(i, ROWS, stride=planes), :].astype(BF16)


def aux_kernel(psi_ref, owner_ref, slot_ref, normals_ref, rim_ref, weight_ref, route_ref, code_ref):
    width = psi_ref.shape[1]
    faces = owner_ref.shape[1]
    coded(psi_ref, code_ref)
    rim_ref[...] = jnp.zeros_like(rim_ref)
    for c in range(10):
        rim_ref[0, c : c + 1, :] = psi_ref[c, 0:1, :]
        rim_ref[1, c : c + 1, :] = psi_ref[c, width - 1 : width, :]

    square = (faces, faces)
    eye = rows(square) == lanes(square)

    def column(row):
        return jnp.sum(jnp.where(eye, row, 0.0), axis=1, keepdims=True)

    owner_row = owner_ref[...].astype(F32)
    owner_col = column(owner_row)
    slot_col = column(slot_ref[...].astype(F32))
    earlier = (owner_col == owner_row) & (lanes(square) < rows(square))
    rank = jnp.sum(jnp.where(earlier, 1.0, 0.0), axis=1, keepdims=True)
    route_ref[...] = jnp.where(rows(square).astype(F32) == owner_row, 1.0, 0.0)
    lane = lanes((faces, 128))
    weight = jnp.where(lane % 8 == 6, slot_col + 1.0, 0.0)
    for d in range(3):
        hit = ((lane % 8) == d) | ((lane % 8) == d + 3)
        weight = jnp.where(hit, column(normals_ref[d]), weight)
    weight_ref[...] = jnp.where((lane // 8).astype(F32) == rank, weight, 0.0)


def coded(u_ref, code_ref):
    width = u_ref.shape[1]
    exponents = jnp.zeros((16, 128), F32)
    row = rows((16, 128))
    for c in range(10):
        top = jnp.max(jnp.abs(u_ref[c]), axis=0, keepdims=True)
        top = jnp.max(top, axis=1, keepdims=True)
        exponent = jnp.ceil(jnp.log2(jnp.maximum(top, 1e-30)))
        code_ref[c * width : (c + 1) * width, :] = jnp.round(u_ref[c] * (FULL * jnp.exp2(-exponent))).astype(jnp.int32).astype(I16)
        exponents = jnp.where(row == c, exponent, exponents)
    code_ref[10 * width :, :] = exponents.astype(jnp.int32).astype(I16)


def code_scale(code_ref):
    exponents = code_ref[code_ref.shape[0] - 16 :, :].astype(jnp.int32).astype(F32)
    scale = jnp.exp2(exponents) * (1.0 / FULL)
    return [scale[c : c + 1, :] for c in range(10)]


def sweep_block(b, blocks, passage, phase, u_ref, lo_ref, hi_ref, scales, rim_ref, tile, source_ref, step_ref, diss_ref, freq_ref):
    at = slice(BLOCK * b, BLOCK * b + BLOCK)
    shape = (BLOCK, 128)
    row, lane = rows(shape), lanes(shape)
    width = u_ref.shape[1]
    u = [u_ref[c, at, :] for c in range(10)]

    def rotated(rim, turn, turned):
        cosine = jnp.where(turned, math.cos(turn), 1.0)
        sine = jnp.where(turned, math.sin(turn), 0.0)
        re = [rim[n] * cosine - rim[5 + n] * sine for n in range(5)]
        im = [rim[n] * sine + rim[5 + n] * cosine for n in range(5)]
        return re + im

    if b == 0:
        before = rotated([rim_ref[1, c : c + 1, :] for c in range(10)], -phase, passage == 0)
    else:
        before = [u_ref[c, BLOCK * b - 1 : BLOCK * b, :] for c in range(10)]
    if b == blocks - 1:
        after = rotated([rim_ref[0, c : c + 1, :] for c in range(10)], phase, passage == 1)
    else:
        after = [u_ref[c, BLOCK * b + BLOCK : BLOCK * b + BLOCK + 1, :] for c in range(10)]

    diff = []
    beside = []
    for c in range(10):
        first = c * width + BLOCK * b
        lo = lo_ref[first : first + BLOCK, :].astype(jnp.int32).astype(F32) * scales[0][c]
        hi = hi_ref[first : first + BLOCK, :].astype(jnp.int32).astype(F32) * scales[1][c]
        diff.append(0.5 * (hi - lo))
        down = jnp.where(row == 0, before[c], pltpu.roll(u[c], 1, axis=0))
        up = jnp.where(row == BLOCK - 1, after[c], pltpu.roll(u[c], BLOCK - 1, axis=0))
        left = jnp.where(lane == 0, 0.0, pltpu.roll(u[c], 1, axis=1))
        right = jnp.where(lane == 127, 0.0, pltpu.roll(u[c], 127, axis=1))
        beside.append(hi + lo + up + down + right + left)
    conv = [None] * 10
    for n in range(5):
        for m in range(5):
            t = tile(5 * n + m)
            re, im = t * diff[n], t * diff[5 + n]
            conv[m] = re if n == 0 else conv[m] + re
            conv[5 + m] = im if n == 0 else conv[5 + m] + im
    step, diss, omega = step_ref[at, :], diss_ref[at, :], freq_ref[at, :]
    new = []
    for c in range(10):
        spin = omega * u[c + 5] if c < 5 else -(omega * u[c - 5])
        resid = conv[c] + spin + diss * (6.0 * u[c] - beside[c]) - source_ref[c, at, :]
        new.append(u[c] - step * resid)
    return new


def first_kernel(
    phase, recv_ref, u_ref, lo_ref, hi_ref, rim_ref, source_ref, step_ref, diss_ref, freq_ref,
    out_ref, tiles_ref, rim_out_ref, code_ref, wide,
):
    passage = lax.axis_index("passage")
    width = u_ref.shape[1]
    for j in range(width):
        wide[j * ROWS : (j + 1) * ROWS, :] = recv_ref[j].astype(F32)
    for e in range(25):
        tiles_ref[e] = wide[pl.ds(e, width, stride=ROWS), :].astype(BF16)
    rim_out_ref[...] = jnp.zeros_like(rim_out_ref)
    blocks = width // BLOCK
    scales = code_scale(lo_ref), code_scale(hi_ref)
    for b in range(blocks):
        new = sweep_block(
            b, blocks, passage, phase, u_ref, lo_ref, hi_ref, scales, rim_ref,
            lambda e: wide[pl.ds(BLOCK * b * ROWS + e, BLOCK, stride=ROWS), :],
            source_ref, step_ref, diss_ref, freq_ref,
        )
        for c in range(10):
            out_ref[c, BLOCK * b : BLOCK * b + BLOCK, :] = new[c]
            if b == 0:
                rim_out_ref[0, c : c + 1, :] = new[c][0:1]
            if b == blocks - 1:
                rim_out_ref[1, c : c + 1, :] = new[c][BLOCK - 1 : BLOCK]
    coded(out_ref, code_ref)


def second_kernel(
    phase, tiles_ref, u_ref, lo_ref, hi_ref, rim_ref, source_ref, step_ref, diss_ref, freq_ref, weight_ref, route_ref,
    out_ref, send_ref,
):
    passage = lax.axis_index("passage")
    width = u_ref.shape[1]
    blocks = width // BLOCK
    scales = code_scale(lo_ref), code_scale(hi_ref)
    for b in range(blocks):
        new = sweep_block(
            b, blocks, passage, phase, u_ref, lo_ref, hi_ref, scales, rim_ref,
            lambda e: tiles_ref[e, BLOCK * b : BLOCK * b + BLOCK, :].astype(F32),
            source_ref, step_ref, diss_ref, freq_ref,
        )
        for c in range(10):
            out_ref[c, BLOCK * b : BLOCK * b + BLOCK, :] = new[c]
    lane = lanes((width, 128)) % 8
    wall = jnp.ones((width, 128), F32)
    for k, c in enumerate((1, 2, 3, 6, 7, 8)):
        wall = jnp.where(lane == k, out_ref[c, :, 0:1], wall)
    routed = jnp.dot(
        route_ref[...], weight_ref[...] * wall, precision=lax.Precision.HIGHEST, preferred_element_type=F32
    )
    for q in range(send_ref.shape[0]):
        send_ref[q] = routed[q : q + 1, :]


def nodes_kernel(recv_ref, out_ref, dense):
    peers = recv_ref.shape[0]
    for q in range(peers):
        dense[q : q + 1, :] = recv_ref[q]
    total = jnp.zeros((8, NODE_DEV), F32)
    node = lanes((peers, NODE_DEV)).astype(F32) + 1.0
    turned = dense[...].T
    for r in range(CAP):
        hit = jnp.where(dense[:, 8 * r + 6 : 8 * r + 7] == node, 1.0, 0.0)
        total = total + jnp.dot(
            turned[8 * r : 8 * r + 8, :], hit, precision=lax.Precision.HIGHEST, preferred_element_type=F32
        )
    out_ref[...] = total[0:6, :]


def kernel_call(body, out, scratch=()):
    whole = pl.BlockSpec(memory_space=pltpu.VMEM)
    return pl.pallas_call(
        body,
        out_shape=[jax.ShapeDtypeStruct(s, d) for s, d in out],
        out_specs=[whole] * len(out),
        scratch_shapes=list(scratch),
        compiler_params=pltpu.CompilerParams(vmem_limit_bytes=VMEM_BYTES),
    )


def planes_beside(state, bricks):
    up = [(i, i + 1) for i in range(bricks - 1)]
    down = [(j, i) for i, j in up]
    return lax.ppermute(state, "brick", up), lax.ppermute(state, "brick", down)


def swapped(rim, passes):
    return lax.ppermute(rim, "passage", [(i, (i + 1) % passes) for i in range(passes)])


def body(
    jac_blocks,
    psi_start,
    source,
    pseudo_step,
    dissipation,
    freq_volume,
    normals,
    face_owner,
    face_slot,
):
    passes = lax.axis_size("passage")
    bricks = lax.axis_size("brick")
    width, depth = psi_start.shape[3], psi_start.shape[4]
    phase = 2.0 * math.pi * ND * passes / BLADES
    field = (10, width, depth)
    rim = (2, 16, depth)
    plane = (10 * width + 16, depth)

    psi = psi_start.reshape(field)
    jac = jac_blocks.reshape(25, bricks, depth)
    source = source.reshape(field)
    scalars = [a.reshape(width, depth) for a in (pseudo_step, dissipation, freq_volume)]

    (send,) = kernel_call(
        prep_kernel,
        [((bricks, ROWS, depth), BF16)],
        [pltpu.VMEM((ROWS * bricks, depth), F32)],
    )(jac)
    recv = lax.all_to_all(send, "brick", 0, 0, tiled=True)
    rims, weight, route, code = kernel_call(
        aux_kernel, [(rim, F32), ((width, 128), F32), ((bricks, width), F32), (plane, I16)]
    )(psi, face_owner.reshape(1, width), face_slot, normals.reshape(3, 1, width))
    lo, hi = planes_beside(code, bricks)
    rims = swapped(rims, passes)

    state, tiles, rims, code = kernel_call(
        functools.partial(first_kernel, phase),
        [(field, F32), ((25, width, depth), BF16), (rim, F32), (plane, I16)],
        [pltpu.VMEM((ROWS * width, depth), F32)],
    )(recv, psi, lo, hi, rims, source, *scalars)

    lo, hi = planes_beside(code, bricks)
    rims = swapped(rims, passes)
    state, routed = kernel_call(
        functools.partial(second_kernel, phase), [(field, F32), ((bricks, 1, 128), F32)]
    )(tiles, state, lo, hi, rims, source, *scalars, weight, route)

    arrived = lax.all_to_all(routed, "brick", 0, 0, tiled=True)
    (sensitivity,) = kernel_call(
        nodes_kernel, [((6, NODE_DEV), F32)], [pltpu.VMEM((bricks, 128), F32)]
    )(arrived)
    return state.reshape(psi_start.shape), sensitivity[None]


def solution(mesh):
    placed = (
        P("passage", None, None, "brick"),
        P("passage", None, "brick", None, None),
        P("passage", None, "brick", None, None),
        P("passage", "brick", None, None),
        P("passage", "brick", None, None),
        P("passage", "brick", None, None),
        P("passage", None, "brick", None),
        P("passage", "brick", None),
        P("passage", "brick"),
    )
    return jax.shard_map(
        body,
        mesh=mesh,
        in_specs=placed,
        out_specs=(P("passage", None, "brick", None, None), P("passage", None, "brick")),
        check_vma=False,
    )
```

time: 66.6 us -> 60.3 us (0.905)
  waiting for transfers between devices: 10.2 us -> 7.45 us
  local copies, waits for them, and re-layouts: 4.03 us -> 1.65 us
  blocking collectives: 19.6 us -> 18.3 us
    ppermute x2, waiting for transfers between devices: 9.24 us -> 6.29 us  [swapped(): lax.ppermute(rim, 'passage', [(i, (i + 1) % passes) for i in range(passes)])]
    unnamed x21 -> x19, local copies, waits for them, and re-layouts: 3.93 us -> 1.65 us
    ppermute x2, starting transfers between devices: 7.89 us -> 6.38 us  [planes_beside(): lax.ppermute(state, 'brick', up)]
    all_to_all x1, blocking collectives: 19.6 us -> 18.3 us  [body(): arrived = lax.all_to_all(routed, 'brick', 0, 0, tiled=True)]
    all_to_all x1, waiting for transfers between devices: 0.01 us -> 1.16 us  [body(): recv = lax.all_to_all(send, 'brick', 0, 0, tiled=True)]
    ppermute x2, waiting for transfers between devices: 0.92 us -> 0.01 us  [planes_beside(): lax.ppermute(state, 'brick', down)]
    ppermute x2, starting transfers between devices: 4.34 us -> 5.06 us  [swapped(): lax.ppermute(rim, 'passage', [(i, (i + 1) % passes) for i in range(passes)])]
    pallas_call x1 -> x2, Pallas kernels: 1.66 us -> 1.61 us  [the longest x1 1.44 us: body(): kernel_call(prep_kernel, [((bricks, ROWS, depth), BF16)], [pltpu.VMEM((RO...]
where the time goes in v2:
time: 60.3 us; the launch traced here: 60 us
  starting transfers between devices  27.3 us (45%)
  blocking collectives  18.3 us (30%)
  waiting for transfers between devices  7.45 us (12%)
  Pallas kernels  4.52 us (7%)
  local copies, waits for them, and re-layouts  1.65 us (3%)
  between operations  0.78 us (1%)
    all_to_all x1, blocking collectives, body(): arrived = lax.all_to_all(routed, 'brick', 0, 0, tiled=True)  18.3 us
    all_to_all x1, starting transfers between devices, body(): recv = lax.all_to_all(send, 'brick', 0, 0, tiled=True)  11.1 us
    ppermute x2, starting transfers between devices, planes_beside(): lax.ppermute(state, 'brick', up)  6.38 us
    ppermute x2, waiting for transfers between devices, swapped(): lax.ppermute(rim, 'passage', [(i, (i + 1) % passes) for i in range(passes)])  6.29 us
    ppermute x2, starting transfers between devices, swapped(): lax.ppermute(rim, 'passage', [(i, (i + 1) % passes) for i in range(passes)])  5.06 us
    ppermute x2, starting transfers between devices, planes_beside(): lax.ppermute(state, 'brick', down)  4.74 us
    unnamed x19, local copies, waits for them, and re-layouts  1.65 us
    pallas_call x1, Pallas kernels, body(): kernel_call(prep_kernel, [((bricks, ROWS, depth), BF16)], [pltpu.VMEM((RO...  1.44 us
  transfers between devices with their start and end apart: 7, of which 3 were waited for; matrix products, arithmetic and copies ran while one was open for 0% of the time, Pallas kernels for 0%

profile of v2, /device:TPU:1, one launch (start us, length us, event | category | flops | bytes accessed | tf_op | source)
XLA Modules:
  0.0 60.0 jit_solution(7947116316987416739)
XLA Ops:
  0.6 1.0 %copy-done.2 = bf16[1,25,64,128]{3,2,1,0:T(8,128)(2,1)S(1)} copy-done((bf16[1,25,64,128]{3,2,1,0:T(8,128)(2,1)S(1)}, bf16[1,25,64,128]{3,2,1,0:T(8,128)(2,1)}, u32[]{:S(2)}) %copy-start.2) | copy-done | bytes 409624
  1.6 1.4 %shard_map.104 = bf16[64,32,128]{2,1,0:T(8,128)(2,1)} custom-call(bf16[25,64,128]{2,1,0:T(8,128)(2,1)S(1)} %bitcast.16), custom_call_target="tpu_custom_call" | custom-call | tf_op jit(solution)/shard_map/pallas_call | solution.py:255
  3.1 0.0 copy-start.3
  3.1 0.0 copy-start.4
  3.1 0.0 copy-start.5
  3.1 11.1 %all-to-all-start = ((bf16[64,32,128]{2,1,0:T(8,128)(2,1)}), bf16[64,32,128]{2,1,0:T(8,128)(2,1)S(1)}, u32[]{:S(2)}, u32[]{:S(2)}) async-start(bf16[64,32,128]{2,1,0:T(8,128)(2,1)} %shard_map.104), calls=%async_computation | async-start | bytes 1048576 | tf_op jit(solution)/shard_map/all_to_all | solution.py:260
  14.2 0.0 copy-start.1
  14.3 0.2 shard_map.105
  14.4 2.4 %collective-permute-start.1 = (s16[656,128]{1,0:T(8,128)(2,1)S(1)}, s16[656,128]{1,0:T(8,128)(2,1)S(1)}, u32[]{:S(2)}, u32[]{:S(2)}) collective-permute-start(s16[656,128]{1,0:T(8,128)(2,1)S(1)} %get-tuple-element.12), channel_id=1, source_target_pairs={{1,0},{2,1},{3,2},{4,3},{5,4},{6,5},{7,6},{8,7},{9,8},{10,9},{11,1... | collective-permute-start | bytes 503816 | tf_op jit(solution)/shard_map/ppermute | solution.py:224
  16.8 3.2 %collective-permute-start = (s16[656,128]{1,0:T(8,128)(2,1)S(1)}, s16[656,128]{1,0:T(8,128)(2,1)S(1)}, u32[]{:S(2)}, u32[]{:S(2)}) collective-permute-start(s16[656,128]{1,0:T(8,128)(2,1)S(1)} %get-tuple-element.12), channel_id=1, source_target_pairs={{0,1},{1,2},{2,3},{3,4},{4,5},{5,6},{6,7},{7,8},{8,9},{9,10},{10,1... | collective-permute-start | bytes 503816 | tf_op jit(solution)/shard_map/ppermute | solution.py:224
  20.0 2.5 %collective-permute-start.2 = (f32[2,16,128]{2,1,0:T(8,128)S(1)}, f32[2,16,128]{2,1,0:T(8,128)S(1)}, u32[]{:S(2)}, u32[]{:S(2)}) collective-permute-start(f32[2,16,128]{2,1,0:T(8,128)S(1)} %get-tuple-element.13), channel_id=1, source_target_pairs={{0,64},{64,0},{1,65},{65,1},{2,66},{66,2},{3,67},{67,3},{4,68},{68... | collective-permute-start | bytes 49160 | tf_op jit(solution)/shard_map/ppermute | solution.py:228
  22.5 3.3 %collective-permute-done.2.rim_ref = f32[2,16,128]{2,1,0:T(8,128)S(1)} collective-permute-done((f32[2,16,128]{2,1,0:T(8,128)S(1)}, f32[2,16,128]{2,1,0:T(8,128)S(1)}, u32[]{:S(2)}, u32[]{:S(2)}) %collective-permute-start.2) | collective-permute-done | bytes 16416 | tf_op jit(solution)/shard_map/ppermute | solution.py:228
  25.8 0.0 collective-permute-done.1.hi_ref
  25.8 0.0 collective-permute-done.lo_ref
  25.8 1.2 %all-to-all-done.recv_ref = bf16[64,32,128]{2,1,0:T(8,128)(2,1)S(1)} async-done(((bf16[64,32,128]{2,1,0:T(8,128)(2,1)}), bf16[64,32,128]{2,1,0:T(8,128)(2,1)S(1)}, u32[]{:S(2)}, u32[]{:S(2)}) %all-to-all-start) | async-done | bytes 524320 | tf_op jit(solution)/shard_map/all_to_all | solution.py:260
  27.0 1.3 %shard_map.106 = (f32[10,64,128]{2,1,0:T(8,128)S(1)}, bf16[25,64,128]{2,1,0:T(8,128)(2,1)S(1)}, f32[2,16,128]{2,1,0:T(8,128)S(1)}, s16[656,128]{1,0:T(8,128)(2,1)S(1)}) custom-call(bf16[64,32,128]{2,1,0:T(8,128)(2,1)S(1)} %all-to-all-done.recv_ref, f32[10,64,128]{2,1,0:T(8,128)S(1)} %bitcast.13, s16[656,128]{1,0:T(8,128)(2,1)S(1)} %collective-permute-done.lo_ref, ...), custom_call_target="tpu_custom_call" | custom-call | tf_op jit(solution)/shard_map/pallas_call | solution.py:267
  28.3 2.4 %collective-permute-start.4 = (s16[656,128]{1,0:T(8,128)(2,1)S(1)}, s16[656,128]{1,0:T(8,128)(2,1)S(1)}, u32[]{:S(2)}, u32[]{:S(2)}) collective-permute-start(s16[656,128]{1,0:T(8,128)(2,1)S(1)} %get-tuple-element.16), channel_id=1, source_target_pairs={{1,0},{2,1},{3,2},{4,3},{5,4},{6,5},{7,6},{8,7},{9,8},{10,9},{11,1... | collective-permute-start | bytes 503816 | tf_op jit(solution)/shard_map/ppermute | solution.py:224
  30.7 3.2 %collective-permute-start.3 = (s16[656,128]{1,0:T(8,128)(2,1)S(1)}, s16[656,128]{1,0:T(8,128)(2,1)S(1)}, u32[]{:S(2)}, u32[]{:S(2)}) collective-permute-start(s16[656,128]{1,0:T(8,128)(2,1)S(1)} %get-tuple-element.16), channel_id=1, source_target_pairs={{0,1},{1,2},{2,3},{3,4},{4,5},{5,6},{6,7},{7,8},{8,9},{9,10},{10,1... | collective-permute-start | bytes 503816 | tf_op jit(solution)/shard_map/ppermute | solution.py:224
  33.9 2.5 %collective-permute-start.5 = (f32[2,16,128]{2,1,0:T(8,128)S(1)}, f32[2,16,128]{2,1,0:T(8,128)S(1)}, u32[]{:S(2)}, u32[]{:S(2)}) collective-permute-start(f32[2,16,128]{2,1,0:T(8,128)S(1)} %get-tuple-element.17), channel_id=1, source_target_pairs={{0,64},{64,0},{1,65},{65,1},{2,66},{66,2},{3,67},{67,3},{4,68},{68... | collective-permute-start | bytes 49160 | tf_op jit(solution)/shard_map/ppermute | solution.py:228
  36.4 3.0 %collective-permute-done.5.rim_ref = f32[2,16,128]{2,1,0:T(8,128)S(1)} collective-permute-done((f32[2,16,128]{2,1,0:T(8,128)S(1)}, f32[2,16,128]{2,1,0:T(8,128)S(1)}, u32[]{:S(2)}, u32[]{:S(2)}) %collective-permute-start.5) | collective-permute-done | bytes 16416 | tf_op jit(solution)/shard_map/ppermute | solution.py:228
  39.4 1.3 %shard_map.107 = (f32[10,64,128]{2,1,0:T(8,128)}, f32[64,1,128]{2,1,0:T(1,128)S(1)}) custom-call(bf16[25,64,128]{2,1,0:T(8,128)(2,1)S(1)} %get-tuple-element.14.tiles_ref, f32[10,64,128]{2,1,0:T(8,128)S(1)} %get-tuple-element.15.u_ref, s16[656,128]{1,0:T(8,128)(2,1)S(1)} %collective-permute-done.3.lo_ref, s16[656,128]{1,0:T(8,128)(2,1)S(1)} %collective-permute-done.4.hi_ref, ...), custom_call_target="tpu_custom_call" | custom-call | tf_op jit(solution)/shard_map/pallas_call | solution.py:275
  40.7 18.3 %all_to_all.10.recv_ref = f32[64,1,128]{2,1,0:T(1,128)S(1)} all-to-all(f32[64,1,128]{2,1,0:T(1,128)S(1)} %get-tuple-element.21), channel_id=1, replica_groups=mesh['passage'=2,'brick'=64] {'brick'}, dimensions={0} | all-to-all | bytes 65536 | tf_op jit(solution)/shard_map/all_to_all | solution.py:279
  59.0 0.3 shard_map.108
  59.4 0.6 %copy.12 = f32[1,6,256]{2,0,1:T(1,128)} copy(f32[1,6,256]{2,1,0:T(8,128)S(1)} %bitcast.23) | data formatting | bytes 12288
  (15 shorter events, 0.0 us)
Async XLA Ops:
  0.6 1.0 %copy-start.2 = (bf16[1,25,64,128]{3,2,1,0:T(8,128)(2,1)S(1)}, bf16[1,25,64,128]{3,2,1,0:T(8,128)(2,1)}, u32[]{:S(2)}) copy-start(bf16[1,25,64,128]{3,2,1,0:T(8,128)(2,1)} %param.9) | copy-start | bytes 1228804
  3.1 11.1 %copy-start = (f32[1,10,1,64,128]{4,3,2,1,0:T(8,128)S(1)}, f32[1,10,1,64,128]{4,3,2,1,0:T(8,128)}, u32[]{:S(2)}) copy-start(f32[1,10,1,64,128]{4,3,2,1,0:T(8,128)} %param.10) | copy-start | bytes 983044
  3.1 11.2 %copy-start.6 = (f32[1,3,1,64]{3,2,1,0:T(1,128)S(1)}, f32[1,3,1,64]{3,2,1,0:T(1,128)}, u32[]{:S(2)}) copy-start(f32[1,3,1,64]{3,2,1,0:T(1,128)} %param.15) | copy-start | bytes 2308
  3.1 11.2 %copy-start.7 = (s32[1,64,1]{1,2,0:T(1,128)S(1)}, s32[1,64,1]{1,2,0:T(1,128)}, u32[]{:S(2)}) copy-start(s32[1,64,1]{1,2,0:T(1,128)} %param.16) | copy-start | bytes 772
  3.1 11.2 %copy-start.8 = (s32[1,64]{1,0:T(1,128)S(1)}, s32[1,64]{1,0:T(1,128)}, u32[]{:S(2)}) copy-start(s32[1,64]{1,0:T(1,128)} %slot_ref.1) | copy-start | bytes 772
  3.1 23.9 %copy-start.3 = (f32[1,1,64,128]{3,2,1,0:T(8,128)S(1)}, f32[1,1,64,128]{3,2,1,0:T(8,128)}, u32[]{:S(2)}) copy-start(f32[1,1,64,128]{3,2,1,0:T(8,128)} %param.12) | copy-start | bytes 98308
  3.1 23.9 %copy-start.4 = (f32[1,1,64,128]{3,2,1,0:T(8,128)S(1)}, f32[1,1,64,128]{3,2,1,0:T(8,128)}, u32[]{:S(2)}) copy-start(f32[1,1,64,128]{3,2,1,0:T(8,128)} %param.13) | copy-start | bytes 98308
  3.1 23.9 %copy-start.5 = (f32[1,1,64,128]{3,2,1,0:T(8,128)S(1)}, f32[1,1,64,128]{3,2,1,0:T(8,128)}, u32[]{:S(2)}) copy-start(f32[1,1,64,128]{3,2,1,0:T(8,128)} %param.14) | copy-start | bytes 98308
  3.1 23.9 %all-to-all-start = ((bf16[64,32,128]{2,1,0:T(8,128)(2,1)}), bf16[64,32,128]{2,1,0:T(8,128)(2,1)S(1)}, u32[]{:S(2)}, u32[]{:S(2)}) async-start(bf16[64,32,128]{2,1,0:T(8,128)(2,1)} %shard_map.104), calls=%async_computation | async-start | bytes 1048576 | tf_op jit(solution)/shard_map/all_to_all | solution.py:260
  14.2 12.8 %copy-start.1 = (f32[1,10,1,64,128]{4,3,2,1,0:T(8,128)S(1)}, f32[1,10,1,64,128]{4,3,2,1,0:T(8,128)}, u32[]{:S(2)}) copy-start(f32[1,10,1,64,128]{4,3,2,1,0:T(8,128)} %param.11) | copy-start | bytes 983044
  14.4 11.4 %collective-permute-start.1 = (s16[656,128]{1,0:T(8,128)(2,1)S(1)}, s16[656,128]{1,0:T(8,128)(2,1)S(1)}, u32[]{:S(2)}, u32[]{:S(2)}) collective-permute-start(s16[656,128]{1,0:T(8,128)(2,1)S(1)} %get-tuple-element.12), channel_id=1, source_target_pairs={{1,0},{2,1},{3,2},{4,3},{5,4},{6,5},{7,6},{8,7},{9,8},{10,9},{11,1... | collective-permute-start | bytes 503816 | tf_op jit(solution)/shard_map/ppermute | solution.py:224
  16.8 9.0 %collective-permute-start = (s16[656,128]{1,0:T(8,128)(2,1)S(1)}, s16[656,128]{1,0:T(8,128)(2,1)S(1)}, u32[]{:S(2)}, u32[]{:S(2)}) collective-permute-start(s16[656,128]{1,0:T(8,128)(2,1)S(1)} %get-tuple-element.12), channel_id=1, source_target_pairs={{0,1},{1,2},{2,3},{3,4},{4,5},{5,6},{6,7},{7,8},{8,9},{9,10},{10,1... | collective-permute-start | bytes 503816 | tf_op jit(solution)/shard_map/ppermute | solution.py:224
  20.0 5.8 %collective-permute-start.2 = (f32[2,16,128]{2,1,0:T(8,128)S(1)}, f32[2,16,128]{2,1,0:T(8,128)S(1)}, u32[]{:S(2)}, u32[]{:S(2)}) collective-permute-start(f32[2,16,128]{2,1,0:T(8,128)S(1)} %get-tuple-element.13), channel_id=1, source_target_pairs={{0,64},{64,0},{1,65},{65,1},{2,66},{66,2},{3,67},{67,3},{4,68},{68... | collective-permute-start | bytes 49160 | tf_op jit(solution)/shard_map/ppermute | solution.py:228
  28.3 11.1 %collective-permute-start.4 = (s16[656,128]{1,0:T(8,128)(2,1)S(1)}, s16[656,128]{1,0:T(8,128)(2,1)S(1)}, u32[]{:S(2)}, u32[]{:S(2)}) collective-permute-start(s16[656,128]{1,0:T(8,128)(2,1)S(1)} %get-tuple-element.16), channel_id=1, source_target_pairs={{1,0},{2,1},{3,2},{4,3},{5,4},{6,5},{7,6},{8,7},{9,8},{10,9},{11,1... | collective-permute-start | bytes 503816 | tf_op jit(solution)/shard_map/ppermute | solution.py:224
  30.7 8.7 %collective-permute-start.3 = (s16[656,128]{1,0:T(8,128)(2,1)S(1)}, s16[656,128]{1,0:T(8,128)(2,1)S(1)}, u32[]{:S(2)}, u32[]{:S(2)}) collective-permute-start(s16[656,128]{1,0:T(8,128)(2,1)S(1)} %get-tuple-element.16), channel_id=1, source_target_pairs={{0,1},{1,2},{2,3},{3,4},{4,5},{5,6},{6,7},{7,8},{8,9},{9,10},{10,1... | collective-permute-start | bytes 503816 | tf_op jit(solution)/shard_map/ppermute | solution.py:224
  33.9 5.5 %collective-permute-start.5 = (f32[2,16,128]{2,1,0:T(8,128)S(1)}, f32[2,16,128]{2,1,0:T(8,128)S(1)}, u32[]{:S(2)}, u32[]{:S(2)}) collective-permute-start(f32[2,16,128]{2,1,0:T(8,128)S(1)} %get-tuple-element.17), channel_id=1, source_target_pairs={{0,64},{64,0},{1,65},{65,1},{2,66},{66,2},{3,67},{67,3},{4,68},{68... | collective-permute-start | bytes 49160 | tf_op jit(solution)/shard_map/ppermute | solution.py:228

commit v3 on v2

--- a/solution.py
+++ b/solution.py
@@ -86,7 +86,7 @@
     return [scale[c : c + 1, :] for c in range(10)]
 
 
-def sweep_block(b, blocks, passage, phase, u_ref, lo_ref, hi_ref, scales, rim_ref, tile, source_ref, step_ref, diss_ref, freq_ref):
+def sweep_block(b, blocks, passage, phase, u_ref, near_ref, far_ref, scales, rim_ref, tile, source_ref, step_ref, diss_ref, freq_ref):
     at = slice(BLOCK * b, BLOCK * b + BLOCK)
     shape = (BLOCK, 128)
     row, lane = rows(shape), lanes(shape)
@@ -109,18 +109,19 @@
     else:
         after = [u_ref[c, BLOCK * b + BLOCK : BLOCK * b + BLOCK + 1, :] for c in range(10)]
 
+    half = jnp.where(lax.axis_index("brick") % 2 == 0, 0.5, -0.5)
     diff = []
     beside = []
     for c in range(10):
         first = c * width + BLOCK * b
-        lo = lo_ref[first : first + BLOCK, :].astype(jnp.int32).astype(F32) * scales[0][c]
-        hi = hi_ref[first : first + BLOCK, :].astype(jnp.int32).astype(F32) * scales[1][c]
-        diff.append(0.5 * (hi - lo))
+        near = near_ref[first : first + BLOCK, :].astype(jnp.int32).astype(F32) * scales[0][c]
+        far = far_ref[first : first + BLOCK, :].astype(jnp.int32).astype(F32) * scales[1][c]
+        diff.append(half * (near - far))
         down = jnp.where(row == 0, before[c], pltpu.roll(u[c], 1, axis=0))
         up = jnp.where(row == BLOCK - 1, after[c], pltpu.roll(u[c], BLOCK - 1, axis=0))
         left = jnp.where(lane == 0, 0.0, pltpu.roll(u[c], 1, axis=1))
         right = jnp.where(lane == 127, 0.0, pltpu.roll(u[c], 127, axis=1))
-        beside.append(hi + lo + up + down + right + left)
+        beside.append(near + far + up + down + right + left)
     conv = [None] * 10
     for n in range(5):
         for m in range(5):
@@ -138,7 +139,7 @@
 
 
 def first_kernel(
-    phase, recv_ref, u_ref, lo_ref, hi_ref, rim_ref, source_ref, step_ref, diss_ref, freq_ref,
+    phase, recv_ref, u_ref, near_ref, far_ref, rim_ref, source_ref, step_ref, diss_ref, freq_ref,
     out_ref, tiles_ref, rim_out_ref, code_ref, wide,
 ):
     passage = lax.axis_index("passage")
@@ -149,10 +150,10 @@
         tiles_ref[e] = wide[pl.ds(e, width, stride=ROWS), :].astype(BF16)
     rim_out_ref[...] = jnp.zeros_like(rim_out_ref)
     blocks = width // BLOCK
-    scales = code_scale(lo_ref), code_scale(hi_ref)
+    scales = code_scale(near_ref), code_scale(far_ref)
     for b in range(blocks):
         new = sweep_block(
-            b, blocks, passage, phase, u_ref, lo_ref, hi_ref, scales, rim_ref,
+            b, blocks, passage, phase, u_ref, near_ref, far_ref, scales, rim_ref,
             lambda e: wide[pl.ds(BLOCK * b * ROWS + e, BLOCK, stride=ROWS), :],
             source_ref, step_ref, diss_ref, freq_ref,
         )
@@ -166,16 +167,16 @@
 
 
 def second_kernel(
-    phase, tiles_ref, u_ref, lo_ref, hi_ref, rim_ref, source_ref, step_ref, diss_ref, freq_ref, weight_ref, route_ref,
+    phase, tiles_ref, u_ref, near_ref, far_ref, rim_ref, source_ref, step_ref, diss_ref, freq_ref, weight_ref, route_ref,
     out_ref, send_ref,
 ):
     passage = lax.axis_index("passage")
     width = u_ref.shape[1]
     blocks = width // BLOCK
-    scales = code_scale(lo_ref), code_scale(hi_ref)
+    scales = code_scale(near_ref), code_scale(far_ref)
     for b in range(blocks):
         new = sweep_block(
-            b, blocks, passage, phase, u_ref, lo_ref, hi_ref, scales, rim_ref,
+            b, blocks, passage, phase, u_ref, near_ref, far_ref, scales, rim_ref,
             lambda e: tiles_ref[e, BLOCK * b : BLOCK * b + BLOCK, :].astype(F32),
             source_ref, step_ref, diss_ref, freq_ref,
         )
@@ -218,10 +219,10 @@
     )
 
 
-def planes_beside(state, bricks):
-    up = [(i, i + 1) for i in range(bricks - 1)]
-    down = [(j, i) for i, j in up]
-    return lax.ppermute(state, "brick", up), lax.ppermute(state, "brick", down)
+def planes_beside(code, bricks):
+    near = [(i, i ^ 1) for i in range(bricks)]
+    far = [(i, i - 1 if i % 2 == 0 else i + 1) for i in range(1, bricks - 1)]
+    return lax.ppermute(code, "brick", near), lax.ppermute(code, "brick", far)
 
 
 def swapped(rim, passes):
@@ -261,20 +262,20 @@
     rims, weight, route, code = kernel_call(
         aux_kernel, [(rim, F32), ((width, 128), F32), ((bricks, width), F32), (plane, I16)]
     )(psi, face_owner.reshape(1, width), face_slot, normals.reshape(3, 1, width))
-    lo, hi = planes_beside(code, bricks)
+    near, far = planes_beside(code, bricks)
     rims = swapped(rims, passes)
 
     state, tiles, rims, code = kernel_call(
         functools.partial(first_kernel, phase),
         [(field, F32), ((25, width, depth), BF16), (rim, F32), (plane, I16)],
         [pltpu.VMEM((ROWS * width, depth), F32)],
-    )(recv, psi, lo, hi, rims, source, *scalars)
-
-    lo, hi = planes_beside(code, bricks)
+    )(recv, psi, near, far, rims, source, *scalars)
+
+    near, far = planes_beside(code, bricks)
     rims = swapped(rims, passes)
     state, routed = kernel_call(
         functools.partial(second_kernel, phase), [(field, F32), ((bricks, 1, 128), F32)]
-    )(tiles, state, lo, hi, rims, source, *scalars, weight, route)
+    )(tiles, state, near, far, rims, source, *scalars, weight, route)
 
     arrived = lax.all_to_all(routed, "brick", 0, 0, tiled=True)
     (sensitivity,) = kernel_call(

time: 60.3 us -> 56.4 us (0.935)
  starting transfers between devices: 27.3 us -> 22.1 us
  waiting for transfers between devices: 7.45 us -> 9.97 us
  blocking collectives: 18.3 us -> 17.1 us
    ppermute x4, starting transfers between devices: 11.1 us -> 6.64 us  [planes_beside(): return (lax.ppermute(code, 'brick', near), lax.ppermute(code, 'brick', far))]
    ppermute x2, waiting for transfers between devices: 6.29 us -> 7.63 us  [swapped(): lax.ppermute(rim, 'passage', [(i, (i + 1) % passes) for i in range(passes)])]
    all_to_all x1, blocking collectives: 18.3 us -> 17.1 us  [body(): arrived = lax.all_to_all(routed, 'brick', 0, 0, tiled=True)]
    ppermute x4, waiting for transfers between devices: 0.01 us -> 1.03 us  [planes_beside(): return (lax.ppermute(code, 'brick', near), lax.ppermute(code, 'brick', far))]
    ppermute x2, starting transfers between devices: 5.06 us -> 4.34 us  [swapped(): lax.ppermute(rim, 'passage', [(i, (i + 1) % passes) for i in range(passes)])]
  transfers between devices with their start and end apart: 7 -> 7, of which waited for: 3 -> 5; matrix products, arithmetic and copies ran while one was open for 0% -> 0% of each run, Pallas kernels for 0% -> 0%
where the time goes in v3:
time: 56.4 us; the launch traced here: 56.1 us
  starting transfers between devices  22.1 us (39%)
  blocking collectives  17.1 us (30%)
  waiting for transfers between devices  9.97 us (18%)
  Pallas kernels  4.54 us (8%)
  local copies, waits for them, and re-layouts  1.65 us (3%)
  between operations  0.78 us (1%)
    all_to_all x1, blocking collectives, body(): arrived = lax.all_to_all(routed, 'brick', 0, 0, tiled=True)  17.1 us
    all_to_all x1, starting transfers between devices, body(): recv = lax.all_to_all(send, 'brick', 0, 0, tiled=True)  11.1 us
    ppermute x2, waiting for transfers between devices, swapped(): lax.ppermute(rim, 'passage', [(i, (i + 1) % passes) for i in range(passes)])  7.63 us
    ppermute x4, starting transfers between devices, planes_beside(): return (lax.ppermute(code, 'brick', near), lax.ppermute(code, 'brick', far))  6.64 us
    ppermute x2, starting transfers between devices, swapped(): lax.ppermute(rim, 'passage', [(i, (i + 1) % passes) for i in range(passes)])  4.34 us
    unnamed x19, local copies, waits for them, and re-layouts  1.65 us
    pallas_call x1, Pallas kernels, body(): kernel_call(prep_kernel, [((bricks, ROWS, depth), BF16)], [pltpu.VMEM((RO...  1.44 us
    all_to_all x1, waiting for transfers between devices, body(): recv = lax.all_to_all(send, 'brick', 0, 0, tiled=True)  1.31 us
  transfers between devices with their start and end apart: 7, of which 5 were waited for; matrix products, arithmetic and copies ran while one was open for 0% of the time, Pallas kernels for 0%

profile of v3, /device:TPU:1, one launch (start us, length us, event | category | flops | bytes accessed | tf_op | source)
XLA Modules:
  0.0 56.1 jit_solution(14892354281293203880)
XLA Ops:
  0.6 1.0 %copy-done.2 = bf16[1,25,64,128]{3,2,1,0:T(8,128)(2,1)S(1)} copy-done((bf16[1,25,64,128]{3,2,1,0:T(8,128)(2,1)S(1)}, bf16[1,25,64,128]{3,2,1,0:T(8,128)(2,1)}, u32[]{:S(2)}) %copy-start.2) | copy-done | bytes 409624
  1.6 1.4 %shard_map.104 = bf16[64,32,128]{2,1,0:T(8,128)(2,1)} custom-call(bf16[25,64,128]{2,1,0:T(8,128)(2,1)S(1)} %bitcast.16), custom_call_target="tpu_custom_call" | custom-call | tf_op jit(solution)/shard_map/pallas_call | solution.py:256
  3.1 0.0 copy-start.3
  3.1 0.0 copy-start.4
  3.1 0.0 copy-start.5
  3.1 11.1 %all-to-all-start = ((bf16[64,32,128]{2,1,0:T(8,128)(2,1)}), bf16[64,32,128]{2,1,0:T(8,128)(2,1)S(1)}, u32[]{:S(2)}, u32[]{:S(2)}) async-start(bf16[64,32,128]{2,1,0:T(8,128)(2,1)} %shard_map.104), calls=%async_computation | async-start | bytes 1048576 | tf_op jit(solution)/shard_map/all_to_all | solution.py:261
  14.2 0.0 copy-start.1
  14.3 0.2 shard_map.105
  14.4 3.5 %collective-permute-start.1 = (s16[656,128]{1,0:T(8,128)(2,1)S(1)}, s16[656,128]{1,0:T(8,128)(2,1)S(1)}, u32[]{:S(2)}, u32[]{:S(2)}) collective-permute-start(s16[656,128]{1,0:T(8,128)(2,1)S(1)} %get-tuple-element.12), channel_id=1, source_target_pairs={{1,2},{2,1},{3,4},{4,3},{5,6},{6,5},{7,8},{8,7},{9,10},{10,9},{11,... | collective-permute-start | bytes 503816 | tf_op jit(solution)/shard_map/ppermute | solution.py:225
  18.0 0.1 collective-permute-start
  18.1 2.5 %collective-permute-start.2 = (f32[2,16,128]{2,1,0:T(8,128)S(1)}, f32[2,16,128]{2,1,0:T(8,128)S(1)}, u32[]{:S(2)}, u32[]{:S(2)}) collective-permute-start(f32[2,16,128]{2,1,0:T(8,128)S(1)} %get-tuple-element.13), channel_id=1, source_target_pairs={{0,64},{64,0},{1,65},{65,1},{2,66},{66,2},{3,67},{67,3},{4,68},{68... | collective-permute-start | bytes 49160 | tf_op jit(solution)/shard_map/ppermute | solution.py:229
  20.6 4.9 %collective-permute-done.2.rim_ref = f32[2,16,128]{2,1,0:T(8,128)S(1)} collective-permute-done((f32[2,16,128]{2,1,0:T(8,128)S(1)}, f32[2,16,128]{2,1,0:T(8,128)S(1)}, u32[]{:S(2)}, u32[]{:S(2)}) %collective-permute-start.2) | collective-permute-done | bytes 16416 | tf_op jit(solution)/shard_map/ppermute | solution.py:229
  25.5 0.6 collective-permute-done.1.far_ref
  26.1 1.3 %all-to-all-done.recv_ref = bf16[64,32,128]{2,1,0:T(8,128)(2,1)S(1)} async-done(((bf16[64,32,128]{2,1,0:T(8,128)(2,1)}), bf16[64,32,128]{2,1,0:T(8,128)(2,1)S(1)}, u32[]{:S(2)}, u32[]{:S(2)}) %all-to-all-start) | async-done | bytes 524320 | tf_op jit(solution)/shard_map/all_to_all | solution.py:261
  27.4 1.3 %shard_map.106 = (f32[10,64,128]{2,1,0:T(8,128)S(1)}, bf16[25,64,128]{2,1,0:T(8,128)(2,1)S(1)}, f32[2,16,128]{2,1,0:T(8,128)S(1)}, s16[656,128]{1,0:T(8,128)(2,1)S(1)}) custom-call(bf16[64,32,128]{2,1,0:T(8,128)(2,1)S(1)} %all-to-all-done.recv_ref, f32[10,64,128]{2,1,0:T(8,128)S(1)} %bitcast.13, s16[656,128]{1,0:T(8,128)(2,1)S(1)} %collective-permute-done.near_ref, ...), custom_call_target="tpu_custom_call" | custom-call | tf_op jit(solution)/shard_map/pallas_call | solution.py:268
  28.7 2.9 %collective-permute-start.4 = (s16[656,128]{1,0:T(8,128)(2,1)S(1)}, s16[656,128]{1,0:T(8,128)(2,1)S(1)}, u32[]{:S(2)}, u32[]{:S(2)}) collective-permute-start(s16[656,128]{1,0:T(8,128)(2,1)S(1)} %get-tuple-element.16), channel_id=1, source_target_pairs={{1,2},{2,1},{3,4},{4,3},{5,6},{6,5},{7,8},{8,7},{9,10},{10,9},{11,... | collective-permute-start | bytes 503816 | tf_op jit(solution)/shard_map/ppermute | solution.py:225
  31.6 0.1 collective-permute-start.3
  31.7 1.8 %collective-permute-start.5 = (f32[2,16,128]{2,1,0:T(8,128)S(1)}, f32[2,16,128]{2,1,0:T(8,128)S(1)}, u32[]{:S(2)}, u32[]{:S(2)}) collective-permute-start(f32[2,16,128]{2,1,0:T(8,128)S(1)} %get-tuple-element.17), channel_id=1, source_target_pairs={{0,64},{64,0},{1,65},{65,1},{2,66},{66,2},{3,67},{67,3},{4,68},{68... | collective-permute-start | bytes 49160 | tf_op jit(solution)/shard_map/ppermute | solution.py:229
  33.5 2.7 %collective-permute-done.5.rim_ref = f32[2,16,128]{2,1,0:T(8,128)S(1)} collective-permute-done((f32[2,16,128]{2,1,0:T(8,128)S(1)}, f32[2,16,128]{2,1,0:T(8,128)S(1)}, u32[]{:S(2)}, u32[]{:S(2)}) %collective-permute-start.5) | collective-permute-done | bytes 16416 | tf_op jit(solution)/shard_map/ppermute | solution.py:229
  36.3 0.5 collective-permute-done.4.far_ref
  36.7 1.3 %shard_map.107 = (f32[10,64,128]{2,1,0:T(8,128)}, f32[64,1,128]{2,1,0:T(1,128)S(1)}) custom-call(bf16[25,64,128]{2,1,0:T(8,128)(2,1)S(1)} %get-tuple-element.14.tiles_ref, f32[10,64,128]{2,1,0:T(8,128)S(1)} %get-tuple-element.15.u_ref, s16[656,128]{1,0:T(8,128)(2,1)S(1)} %collective-permute-done.3.near_ref, ...), custom_call_target="tpu_custom_call" | custom-call | tf_op jit(solution)/shard_map/pallas_call | solution.py:276
  38.0 17.1 %all_to_all.10.recv_ref = f32[64,1,128]{2,1,0:T(1,128)S(1)} all-to-all(f32[64,1,128]{2,1,0:T(1,128)S(1)} %get-tuple-element.21), channel_id=1, replica_groups=mesh['passage'=2,'brick'=64] {'brick'}, dimensions={0} | all-to-all | bytes 65536 | tf_op jit(solution)/shard_map/all_to_all | solution.py:280
  55.1 0.3 shard_map.108
  55.5 0.6 %copy.12 = f32[1,6,256]{2,0,1:T(1,128)} copy(f32[1,6,256]{2,1,0:T(8,128)S(1)} %bitcast.23) | data formatting | bytes 12288
  (15 shorter events, 0.0 us)
Async XLA Ops:
  0.6 1.0 %copy-start.2 = (bf16[1,25,64,128]{3,2,1,0:T(8,128)(2,1)S(1)}, bf16[1,25,64,128]{3,2,1,0:T(8,128)(2,1)}, u32[]{:S(2)}) copy-start(bf16[1,25,64,128]{3,2,1,0:T(8,128)(2,1)} %param.9) | copy-start | bytes 1228804
  3.1 11.1 %copy-start = (f32[1,10,1,64,128]{4,3,2,1,0:T(8,128)S(1)}, f32[1,10,1,64,128]{4,3,2,1,0:T(8,128)}, u32[]{:S(2)}) copy-start(f32[1,10,1,64,128]{4,3,2,1,0:T(8,128)} %param.10) | copy-start | bytes 983044
  3.1 11.2 %copy-start.6 = (f32[1,3,1,64]{3,2,1,0:T(1,128)S(1)}, f32[1,3,1,64]{3,2,1,0:T(1,128)}, u32[]{:S(2)}) copy-start(f32[1,3,1,64]{3,2,1,0:T(1,128)} %param.15) | copy-start | bytes 2308
  3.1 11.2 %copy-start.7 = (s32[1,64,1]{1,2,0:T(1,128)S(1)}, s32[1,64,1]{1,2,0:T(1,128)}, u32[]{:S(2)}) copy-start(s32[1,64,1]{1,2,0:T(1,128)} %param.16) | copy-start | bytes 772
  3.1 11.2 %copy-start.8 = (s32[1,64]{1,0:T(1,128)S(1)}, s32[1,64]{1,0:T(1,128)}, u32[]{:S(2)}) copy-start(s32[1,64]{1,0:T(1,128)} %slot_ref.1) | copy-start | bytes 772
  3.1 24.3 %copy-start.3 = (f32[1,1,64,128]{3,2,1,0:T(8,128)S(1)}, f32[1,1,64,128]{3,2,1,0:T(8,128)}, u32[]{:S(2)}) copy-start(f32[1,1,64,128]{3,2,1,0:T(8,128)} %param.12) | copy-start | bytes 98308
  3.1 24.3 %copy-start.4 = (f32[1,1,64,128]{3,2,1,0:T(8,128)S(1)}, f32[1,1,64,128]{3,2,1,0:T(8,128)}, u32[]{:S(2)}) copy-start(f32[1,1,64,128]{3,2,1,0:T(8,128)} %param.13) | copy-start | bytes 98308
  3.1 24.3 %copy-start.5 = (f32[1,1,64,128]{3,2,1,0:T(8,128)S(1)}, f32[1,1,64,128]{3,2,1,0:T(8,128)}, u32[]{:S(2)}) copy-start(f32[1,1,64,128]{3,2,1,0:T(8,128)} %param.14) | copy-start | bytes 98308
  3.1 24.3 %all-to-all-start = ((bf16[64,32,128]{2,1,0:T(8,128)(2,1)}), bf16[64,32,128]{2,1,0:T(8,128)(2,1)S(1)}, u32[]{:S(2)}, u32[]{:S(2)}) async-start(bf16[64,32,128]{2,1,0:T(8,128)(2,1)} %shard_map.104), calls=%async_computation | async-start | bytes 1048576 | tf_op jit(solution)/shard_map/all_to_all | solution.py:261
  14.2 13.2 %copy-start.1 = (f32[1,10,1,64,128]{4,3,2,1,0:T(8,128)S(1)}, f32[1,10,1,64,128]{4,3,2,1,0:T(8,128)}, u32[]{:S(2)}) copy-start(f32[1,10,1,64,128]{4,3,2,1,0:T(8,128)} %param.11) | copy-start | bytes 983044
  14.4 11.6 %collective-permute-start.1 = (s16[656,128]{1,0:T(8,128)(2,1)S(1)}, s16[656,128]{1,0:T(8,128)(2,1)S(1)}, u32[]{:S(2)}, u32[]{:S(2)}) collective-permute-start(s16[656,128]{1,0:T(8,128)(2,1)S(1)} %get-tuple-element.12), channel_id=1, source_target_pairs={{1,2},{2,1},{3,4},{4,3},{5,6},{6,5},{7,8},{8,7},{9,10},{10,9},{11,... | collective-permute-start | bytes 503816 | tf_op jit(solution)/shard_map/ppermute | solution.py:225
  18.0 8.1 %collective-permute-start = (s16[656,128]{1,0:T(8,128)(2,1)S(1)}, s16[656,128]{1,0:T(8,128)(2,1)S(1)}, u32[]{:S(2)}, u32[]{:S(2)}) collective-permute-start(s16[656,128]{1,0:T(8,128)(2,1)S(1)} %get-tuple-element.12), channel_id=1, source_target_pairs={{0,1},{1,0},{2,3},{3,2},{4,5},{5,4},{6,7},{7,6},{8,9},{9,8},{10,11... | collective-permute-start | bytes 503816 | tf_op jit(solution)/shard_map/ppermute | solution.py:225
  18.1 7.4 %collective-permute-start.2 = (f32[2,16,128]{2,1,0:T(8,128)S(1)}, f32[2,16,128]{2,1,0:T(8,128)S(1)}, u32[]{:S(2)}, u32[]{:S(2)}) collective-permute-start(f32[2,16,128]{2,1,0:T(8,128)S(1)} %get-tuple-element.13), channel_id=1, source_target_pairs={{0,64},{64,0},{1,65},{65,1},{2,66},{66,2},{3,67},{67,3},{4,68},{68... | collective-permute-start | bytes 49160 | tf_op jit(solution)/shard_map/ppermute | solution.py:229
  28.7 8.0 %collective-permute-start.4 = (s16[656,128]{1,0:T(8,128)(2,1)S(1)}, s16[656,128]{1,0:T(8,128)(2,1)S(1)}, u32[]{:S(2)}, u32[]{:S(2)}) collective-permute-start(s16[656,128]{1,0:T(8,128)(2,1)S(1)} %get-tuple-element.16), channel_id=1, source_target_pairs={{1,2},{2,1},{3,4},{4,3},{5,6},{6,5},{7,8},{8,7},{9,10},{10,9},{11,... | collective-permute-start | bytes 503816 | tf_op jit(solution)/shard_map/ppermute | solution.py:225
  31.6 5.1 %collective-permute-start.3 = (s16[656,128]{1,0:T(8,128)(2,1)S(1)}, s16[656,128]{1,0:T(8,128)(2,1)S(1)}, u32[]{:S(2)}, u32[]{:S(2)}) collective-permute-start(s16[656,128]{1,0:T(8,128)(2,1)S(1)} %get-tuple-element.16), channel_id=1, source_target_pairs={{0,1},{1,0},{2,3},{3,2},{4,5},{5,4},{6,7},{7,6},{8,9},{9,8},{10,11... | collective-permute-start | bytes 503816 | tf_op jit(solution)/shard_map/ppermute | solution.py:225
  31.7 4.5 %collective-permute-start.5 = (f32[2,16,128]{2,1,0:T(8,128)S(1)}, f32[2,16,128]{2,1,0:T(8,128)S(1)}, u32[]{:S(2)}, u32[]{:S(2)}) collective-permute-start(f32[2,16,128]{2,1,0:T(8,128)S(1)} %get-tuple-element.17), channel_id=1, source_target_pairs={{0,64},{64,0},{1,65},{65,1},{2,66},{66,2},{3,67},{67,3},{4,68},{68... | collective-permute-start | bytes 49160 | tf_op jit(solution)/shard_map/ppermute | solution.py:229

commit v4 on v3

v4 whole, which is shorter than its diff:
```python
import functools
import math

import jax
import jax.numpy as jnp
from jax import lax
from jax.experimental import pallas as pl
from jax.experimental.pallas import tpu as pltpu
from jax.sharding import PartitionSpec as P

NODE_DEV = 256
CAP = 4
PLANES = 3
WALL = (1, 2, 3, 6, 7, 8)
ND = 1
BLADES = 36
ROWS = 32
BLOCK = 16
FULL = 32000.0
AHEAD = 1 << 34
VMEM_BYTES = 40 * 1024 * 1024
F32 = jnp.float32
BF16 = jnp.bfloat16
I16 = jnp.int16


def lanes(shape):
    return lax.broadcasted_iota(jnp.int32, shape, len(shape) - 1)


def rows(shape):
    return lax.broadcasted_iota(jnp.int32, shape, len(shape) - 2)


def prep_kernel(jac_ref, send_ref, wide):
    planes = jac_ref.shape[1]
    wide[25 * planes : ROWS * planes, :] = jnp.zeros(((ROWS - 25) * planes, 128), F32)
    lane = lanes((planes, 128))
    wall = jnp.zeros((planes, 128), F32)
    for e in range(25):
        entry = jac_ref[e].astype(F32)
        wide[e * planes : (e + 1) * planes, :] = entry
        wall = jnp.where(lane == e, pltpu.roll(entry, e, axis=1) if e else entry, wall)
    wide[25 * planes + 1 : 26 * planes, :] = wall[0 : planes - 1]
    wide[26 * planes : 27 * planes - 1, :] = wall[1:planes]
    for i in range(planes):
        send_ref[i] = wide[pl.ds(i, ROWS, stride=planes), :].astype(BF16)


def routing(owner_row, rank, values, first):
    faces = rank.shape[0]
    square = (faces, faces)
    lane = lanes((faces, 128))
    within = lane % 8
    weight = jnp.where(within == 6, values[3], 0.0)
    for d in range(3):
        weight = jnp.where((within == d) | (within == d + 3), values[d], weight)
    weight = jnp.where((lane // 8 - first).astype(F32) == rank, weight, 0.0)
    return jnp.where(rows(square).astype(F32) == owner_row, 1.0, 0.0), weight


def turned(value):
    length = max(value.shape)
    square = (length, length)
    eye = rows(square) == lanes(square)
    return jnp.sum(jnp.where(eye, value, 0.0), axis=1 if value.shape[0] == 1 else 0, keepdims=True)


def aux_kernel(
    psi_ref, source_ref, step_ref, diss_ref, freq_ref, owner_ref, slot_ref, normals_ref,
    rim_ref, weight_ref, route_ref, code_ref, fields_ref,
):
    width = psi_ref.shape[1]
    rim_ref[...] = jnp.zeros_like(rim_ref)
    for c in range(10):
        rim_ref[0, c : c + 1, :] = psi_ref[c, 0:1, :]
        rim_ref[1, c : c + 1, :] = psi_ref[c, width - 1 : width, :]

    square = (width, width)
    owner_row = owner_ref[...].astype(F32)
    owner = turned(owner_row)
    slot = turned(slot_ref[...].astype(F32)) + 1.0
    earlier = (owner == owner_row) & (lanes(square) < rows(square))
    rank = jnp.sum(jnp.where(earlier, 1.0, 0.0), axis=1, keepdims=True)
    normals = [turned(normals_ref[d]) for d in range(3)]
    route_ref[...], weight_ref[...] = routing(owner_row, rank, normals + [slot], 0)

    step, diss, omega = step_ref[:, 0:1], diss_ref[:, 0:1], freq_ref[:, 0:1]
    lane = lanes((width, 128))
    info = jnp.zeros((width, 128), F32)
    for k, value in enumerate([step * n for n in normals] + [slot, diss, owner, rank]):
        info = jnp.where(lane == k, value, info)
    coded(psi_ref, code_ref, info)

    within = lane % 8
    flow = jnp.zeros((width, 128), F32)
    for k, c in enumerate(WALL):
        flow = jnp.where(within == k, source_ref[c, :, 0:1], flow)
    fields_ref[0] = jnp.zeros((width, 128), F32) + step
    fields_ref[1] = jnp.zeros((width, 128), F32) + diss
    fields_ref[2] = jnp.where(within < 3, omega, -omega)
    fields_ref[3] = flow


def beside_kernel(near_ref, far_ref, weight_ref, route_ref, diss_ref):
    width = weight_ref.shape[1]
    for at, ref in enumerate((near_ref, far_ref)):
        last = ref.shape[0] - width
        exponent = ref[last - 16 : last, :].astype(jnp.int32).astype(F32)[15:16, :]
        code = ref[last:, :].astype(jnp.int32).astype(F32)
        low = pltpu.roll(code, 120, axis=1)
        info = (code + low * (1.0 / FULL)) * (jnp.exp2(exponent) * (1.0 / FULL))
        column = [info[:, k : k + 1] for k in range(7)]
        slot, owner, rank = [jnp.round(column[k]) for k in (3, 5, 6)]
        route_ref[at], weight_ref[at] = routing(turned(owner), rank, column[:3] + [slot], CAP * (at + 1))
        diss_ref[at] = jnp.zeros((width, 128), F32) + column[4]


def exponent_of(top):
    return jnp.ceil(jnp.log2(jnp.maximum(top, 1e-30)))


def short(value):
    return jnp.round(value).astype(jnp.int32).astype(I16)


def coded(u_ref, code_ref, info=None):
    width = u_ref.shape[1]
    exponents = jnp.zeros((16, 128), F32)
    row = rows((16, 128))
    for c in range(10):
        top = jnp.max(jnp.abs(u_ref[c]), axis=0, keepdims=True)
        top = jnp.max(top, axis=1, keepdims=True)
        exponent = exponent_of(top)
        code_ref[c * width : (c + 1) * width, :] = short(u_ref[c] * (FULL * jnp.exp2(-exponent)))
        exponents = jnp.where(row == c, exponent, exponents)
    if info is not None:
        exponent = exponent_of(jnp.max(jnp.abs(info), axis=0, keepdims=True))
        exponents = jnp.where(row == 15, exponent, exponents)
        value = info * (FULL * jnp.exp2(-exponent))
        high = jnp.round(value)
        low = jnp.round((value - high) * FULL)
        lane = lanes((width, 128))
        both = jnp.where(lane < 8, high, jnp.where(lane < 16, pltpu.roll(low, 8, axis=1), 0.0))
        code_ref[10 * width + 16 :, :] = short(both)
    code_ref[10 * width : 10 * width + 16, :] = short(exponents)


def code_scale(code_ref, width):
    exponents = code_ref[10 * width : 10 * width + 16, :].astype(jnp.int32).astype(F32)
    scale = jnp.exp2(exponents) * (1.0 / FULL)
    return [scale[c : c + 1, :] for c in range(10)]


def rims_beside(rim_ref, passage, phase):
    def rotated(at, turn, edge):
        cosine = jnp.where(passage == edge, math.cos(turn), 1.0)
        sine = jnp.where(passage == edge, math.sin(turn), 0.0)
        rim = [rim_ref[at, c : c + 1, :] for c in range(10)]
        re = [rim[n] * cosine - rim[5 + n] * sine for n in range(5)]
        im = [rim[n] * sine + rim[5 + n] * cosine for n in range(5)]
        return re + im

    return rotated(1, -phase, 0), rotated(0, phase, 1)


def sweep_block(b, blocks, u_ref, near_ref, far_ref, scales, rims, tile, source_ref, step_ref, diss_ref, freq_ref):
    at = slice(BLOCK * b, BLOCK * b + BLOCK)
    shape = (BLOCK, 128)
    row, lane = rows(shape), lanes(shape)
    width = u_ref.shape[1]
    u = [u_ref[c, at, :] for c in range(10)]

    if b == 0:
        before = rims[0]
    else:
        before = [u_ref[c, BLOCK * b - 1 : BLOCK * b, :] for c in range(10)]
    if b == blocks - 1:
        after = rims[1]
    else:
        after = [u_ref[c, BLOCK * b + BLOCK : BLOCK * b + BLOCK + 1, :] for c in range(10)]

    half = jnp.where(lax.axis_index("brick") % 2 == 0, 0.5, -0.5)
    diff = []
    beside = []
    for c in range(10):
        first = c * width + BLOCK * b
        near = near_ref[first : first + BLOCK, :].astype(jnp.int32).astype(F32) * scales[0][c]
        far = far_ref[first : first + BLOCK, :].astype(jnp.int32).astype(F32) * scales[1][c]
        diff.append(half * (near - far))
        down = jnp.where(row == 0, before[c], pltpu.roll(u[c], 1, axis=0))
        up = jnp.where(row == BLOCK - 1, after[c], pltpu.roll(u[c], BLOCK - 1, axis=0))
        left = jnp.where(lane == 0, 0.0, pltpu.roll(u[c], 1, axis=1))
        right = jnp.where(lane == 127, 0.0, pltpu.roll(u[c], 127, axis=1))
        beside.append(near + far + up + down + right + left)
    conv = [None] * 10
    for n in range(5):
        for m in range(5):
            t = tile(5 * n + m)
            re, im = t * diff[n], t * diff[5 + n]
            conv[m] = re if n == 0 else conv[m] + re
            conv[5 + m] = im if n == 0 else conv[5 + m] + im
    step, diss, omega = step_ref[at, :], diss_ref[at, :], freq_ref[at, :]
    new = []
    for c in range(10):
        spin = omega * u[c + 5] if c < 5 else -(omega * u[c - 5])
        resid = conv[c] + spin + diss * (6.0 * u[c] - beside[c]) - source_ref[c, at, :]
        new.append(u[c] - step * resid)
    return new


def first_kernel(
    phase, recv_ref, u_ref, near_ref, far_ref, rim_ref, source_ref, step_ref, diss_ref, freq_ref,
    out_ref, tiles_ref, rim_out_ref, code_ref, walls_ref, wide,
):
    rims = rims_beside(rim_ref, lax.axis_index("passage"), phase)
    width = u_ref.shape[1]
    for j in range(width):
        wide[j * ROWS : (j + 1) * ROWS, :] = recv_ref[j].astype(F32)
    for at in range(2):
        walls_ref[at] = wide[pl.ds(25 + at, width, stride=ROWS), :]
    for e in range(25):
        tiles_ref[e] = wide[pl.ds(e, width, stride=ROWS), :].astype(BF16)
    rim_out_ref[...] = jnp.zeros_like(rim_out_ref)
    blocks = width // BLOCK
    scales = code_scale(near_ref, width), code_scale(far_ref, width)
    for b in range(blocks):
        new = sweep_block(
            b, blocks, u_ref, near_ref, far_ref, scales, rims,
            lambda e: wide[pl.ds(BLOCK * b * ROWS + e, BLOCK, stride=ROWS), :],
            source_ref, step_ref, diss_ref, freq_ref,
        )
        for c in range(10):
            out_ref[c, BLOCK * b : BLOCK * b + BLOCK, :] = new[c]
            if b == 0:
                rim_out_ref[0, c : c + 1, :] = new[c][0:1]
            if b == blocks - 1:
                rim_out_ref[1, c : c + 1, :] = new[c][BLOCK - 1 : BLOCK]
    coded(out_ref, code_ref)


def second_kernel(
    phase, tiles_ref, u_ref, near_ref, far_ref, rim_ref, source_ref, step_ref, diss_ref, freq_ref, out_ref, after_ref
):
    rims = rims_beside(rim_ref, lax.axis_index("passage"), phase)
    width = u_ref.shape[1]
    blocks = width // BLOCK
    scales = code_scale(near_ref, width), code_scale(far_ref, width)
    for b in range(blocks):
        new = sweep_block(
            b, blocks, u_ref, near_ref, far_ref, scales, rims,
            lambda e: tiles_ref[e, BLOCK * b : BLOCK * b + BLOCK, :].astype(F32),
            source_ref, step_ref, diss_ref, freq_ref,
        )
        for c in range(10):
            out_ref[c, BLOCK * b : BLOCK * b + BLOCK, :] = new[c]
    after_ref[...] = jnp.zeros_like(after_ref)


def wall_kernel(
    phase, u_ref, rim_ref, fields_ref, walls_ref, weight_ref, route_ref, weights_ref, routes_ref, disses_ref, send_ref
):
    width = u_ref.shape[1]
    shape = (width, 128)
    lane, row = lanes(shape), rows(shape)
    within = lane % 8
    zero = jnp.zeros(shape, F32)
    at_wall = [zero + u_ref[c, :, 0:1] for c in range(10)]

    def chosen(values):
        out = values[0]
        for k in range(1, 6):
            out = jnp.where(within == k, values[k], out)
        return out

    below, above = rims_beside(rim_ref, lax.axis_index("passage"), phase)
    u = chosen([at_wall[c] for c in WALL])
    other = chosen([at_wall[(c + 5) % 10] for c in WALL])
    right = chosen([u_ref[c, :, 1:2] for c in WALL])
    below = chosen([below[c][:, 0:1] for c in WALL])
    above = chosen([above[c][:, 0:1] for c in WALL])
    down = jnp.where(row == 0, below, pltpu.roll(u, 1, axis=0))
    up = jnp.where(row == width - 1, above, pltpu.roll(u, width - 1, axis=0))
    own = u - fields_ref[0] * (
        fields_ref[2] * other + fields_ref[1] * (6.0 * u - (down + up + right)) - fields_ref[3]
    )

    def sent(route, weight, value):
        value = weight * jnp.where(within == 6, 1.0, value)
        return jnp.dot(route, value, precision=lax.Precision.HIGHEST, preferred_element_type=F32)

    routed = sent(route_ref[...], weight_ref[...], own)
    even = lax.axis_index("brick") % 2 == 0
    for at, share in enumerate((-0.5, 0.5)):
        share = jnp.where(even, -share, share)
        tile = jnp.where(even, walls_ref[1 - at], walls_ref[at])
        re, im = zero, zero
        for n in range(5):
            entry = pltpu.roll(tile, 127 - 5 * n, axis=1)
            re = re + entry * at_wall[n]
            im = im + entry * at_wall[5 + n]
        conv = jnp.where(lane < 3, re, jnp.where(lane < 6, pltpu.roll(im, 3, axis=1), 0.0))
        for turn in (8, 16, 32, 64):
            conv = conv + pltpu.roll(conv, turn, axis=1)
        routed = routed + sent(routes_ref[at], weights_ref[at], disses_ref[at] * u + share * conv)
    for q in range(send_ref.shape[0]):
        send_ref[q] = routed[q : q + 1, :]


def nodes_kernel(recv_ref, after_ref, out_ref, dense):
    peers = recv_ref.shape[0]
    for q in range(peers):
        dense[q : q + 1, :] = recv_ref[q]
    total = jnp.zeros((8, NODE_DEV), F32)
    node = lanes((peers, NODE_DEV)).astype(F32) + 1.0
    terms = dense[...].T
    for r in range(CAP * PLANES):
        hit = jnp.where(dense[:, 8 * r + 6 : 8 * r + 7] == node, 1.0, 0.0)
        total = total + jnp.dot(
            terms[8 * r : 8 * r + 8, :], hit, precision=lax.Precision.HIGHEST, preferred_element_type=F32
        )
    for c in range(6):
        out_ref[c] = total[c : c + 1, :]


def kernel_call(body, out, scratch=(), flops=None):
    whole = pl.BlockSpec(memory_space=pltpu.VMEM)
    return pl.pallas_call(
        body,
        out_shape=[jax.ShapeDtypeStruct(s, d) for s, d in out],
        out_specs=[whole] * len(out),
        scratch_shapes=list(scratch),
        compiler_params=pltpu.CompilerParams(vmem_limit_bytes=VMEM_BYTES),
        cost_estimate=flops and pl.CostEstimate(flops=flops, bytes_accessed=0, transcendentals=0),
    )


def planes_beside(code, bricks):
    near = [(i, i ^ 1) for i in range(bricks)]
    far = [(i, i - 1 if i % 2 == 0 else i + 1) for i in range(1, bricks - 1)]
    return lax.ppermute(code, "brick", near), lax.ppermute(code, "brick", far)


def swapped(rim, passes):
    return lax.ppermute(rim, "passage", [(i, (i + 1) % passes) for i in range(passes)])


def body(
    jac_blocks,
    psi_start,
    source,
    pseudo_step,
    dissipation,
    freq_volume,
    normals,
    face_owner,
    face_slot,
):
    passes = lax.axis_size("passage")
    bricks = lax.axis_size("brick")
    width, depth = psi_start.shape[3], psi_start.shape[4]
    phase = 2.0 * math.pi * ND * passes / BLADES
    field = (10, width, depth)
    rim = (2, 16, depth)
    plane = (10 * width + 16, depth)

    psi = psi_start.reshape(field)
    jac = jac_blocks.reshape(25, bricks, depth)
    source = source.reshape(field)
    scalars = [a.reshape(width, depth) for a in (pseudo_step, dissipation, freq_volume)]

    (send,) = kernel_call(
        prep_kernel,
        [((bricks, ROWS, depth), BF16)],
        [pltpu.VMEM((ROWS * bricks, depth), F32)],
    )(jac)
    recv = lax.all_to_all(send, "brick", 0, 0, tiled=True)
    face = (width, 128)
    rims, weight, route, code, fields = kernel_call(
        aux_kernel,
        [(rim, F32), (face, F32), ((bricks, width), F32), ((plane[0] + width, depth), I16), ((4, *face), F32)],
    )(psi, source, *scalars, face_owner.reshape(1, width), face_slot, normals.reshape(3, 1, width))
    rims = swapped(rims, passes)
    near, far = planes_beside(code, bricks)
    weights, routes, disses = kernel_call(
        beside_kernel, [((2, *face), F32), ((2, bricks, width), F32), ((2, *face), F32)]
    )(near, far)

    state, tiles, rims, code, walls = kernel_call(
        functools.partial(first_kernel, phase),
        [(field, F32), ((25, width, depth), BF16), (rim, F32), (plane, I16), ((2, *face), F32)],
        [pltpu.VMEM((ROWS * width, depth), F32)],
    )(recv, psi, near, far, rims, source, *scalars)

    rims = swapped(rims, passes)
    near, far = planes_beside(code, bricks)
    (routed,) = kernel_call(functools.partial(wall_kernel, phase), [((bricks, 1, 128), F32)], flops=AHEAD)(
        state, rims, fields, walls, weight, route, weights, routes, disses
    )
    arrived = lax.all_to_all(routed, "brick", 0, 0, tiled=True)
    state, after = kernel_call(functools.partial(second_kernel, phase), [(field, F32), ((8, 128), F32)])(
        tiles, state, near, far, rims, source, *scalars
    )
    (sensitivity,) = kernel_call(nodes_kernel, [((6, 1, NODE_DEV), F32)], [pltpu.VMEM((bricks, 128), F32)])(
        arrived, after
    )
    return state.reshape(psi_start.shape), sensitivity.transpose(1, 0, 2)


def solution(mesh):
    placed = (
        P("passage", None, None, "brick"),
        P("passage", None, "brick", None, None),
        P("passage", None, "brick", None, None),
        P("passage", "brick", None, None),
        P("passage", "brick", None, None),
        P("passage", "brick", None, None),
        P("passage", None, "brick", None),
        P("passage", "brick", None),
        P("passage", "brick"),
    )
    return jax.shard_map(
        body,
        mesh=mesh,
        in_specs=placed,
        out_specs=(P("passage", None, "brick", None, None), P("passage", None, "brick")),
        check_vma=False,
    )
```

time: 56.4 us -> 54.7 us (0.970)
  blocking collectives: 17.1 us -> 0 us
  starting transfers between devices: 22.1 us -> 32.2 us
  Pallas kernels: 4.54 us -> 7.39 us
  waiting for transfers between devices: 9.97 us -> 12.3 us
    all_to_all x1 -> x0, blocking collectives: 17.1 us -> none  [body(): arrived = lax.all_to_all(routed, 'brick', 0, 0, tiled=True)]
    all_to_all x0 -> x1, starting transfers between devices: none -> 9.7 us  [body(): arrived = lax.all_to_all(routed, 'brick', 0, 0, tiled=True)]
    all_to_all x0 -> x1, waiting for transfers between devices: none -> 6.48 us  [body(): arrived = lax.all_to_all(routed, 'brick', 0, 0, tiled=True)]
    ppermute x2, waiting for transfers between devices: 7.63 us -> 4.12 us  [swapped(): lax.ppermute(rim, 'passage', [(i, (i + 1) % passes) for i in range(passes)])]
    pallas_call x3 -> x5, Pallas kernels: 1.81 us -> 4.49 us  [the longest x1 1.34 us: body(): kernel_call(functools.partial(wall_kernel, phase), [((bricks, 1, 128), F3...]
    ppermute x2, starting transfers between devices: 4.34 us -> 5.06 us  [swapped(): lax.ppermute(rim, 'passage', [(i, (i + 1) % passes) for i in range(passes)])]
    unnamed x19 -> x18, local copies, waits for them, and re-layouts: 1.65 us -> 1.63 us
  transfers between devices with their start and end apart: 7 -> 8, of which waited for: 5 -> 4; matrix products, arithmetic and copies ran while one was open for 0% -> 0% of each run, Pallas kernels for 0% -> 6%
where the time goes in v4:
time: 54.7 us; the launch traced here: 54.4 us
  starting transfers between devices  32.2 us (59%)
  waiting for transfers between devices  12.3 us (22%)
  Pallas kernels  7.39 us (14%)
  local copies, waits for them, and re-layouts  1.63 us (3%)
  between operations  0.79 us (1%)
    all_to_all x1, starting transfers between devices, body(): recv = lax.all_to_all(send, 'brick', 0, 0, tiled=True)  11.1 us
    all_to_all x1, starting transfers between devices, body(): arrived = lax.all_to_all(routed, 'brick', 0, 0, tiled=True)  9.7 us
    all_to_all x1, waiting for transfers between devices, body(): arrived = lax.all_to_all(routed, 'brick', 0, 0, tiled=True)  6.48 us
    ppermute x4, starting transfers between devices, planes_beside(): return (lax.ppermute(code, 'brick', near), lax.ppermute(code, 'brick', far))  6.42 us
    ppermute x2, starting transfers between devices, swapped(): lax.ppermute(rim, 'passage', [(i, (i + 1) % passes) for i in range(passes)])  5.06 us
    ppermute x2, waiting for transfers between devices, swapped(): lax.ppermute(rim, 'passage', [(i, (i + 1) % passes) for i in range(passes)])  4.12 us
    unnamed x18, local copies, waits for them, and re-layouts  1.63 us
    pallas_call x1, Pallas kernels, body(): kernel_call(prep_kernel, [((bricks, ROWS, depth), BF16)], [pltpu.VMEM((RO...  1.57 us
  transfers between devices with their start and end apart: 8, of which 4 were waited for; matrix products, arithmetic and copies ran while one was open for 0% of the time, Pallas kernels for 6%

profile of v4, /device:TPU:1, one launch (start us, length us, event | category | flops | bytes accessed | tf_op | source)
XLA Modules:
  0.0 54.4 jit_solution(18367488642683227945)
XLA Ops:
  0.6 1.0 %copy-done.2 = bf16[1,25,64,128]{3,2,1,0:T(8,128)(2,1)S(1)} copy-done((bf16[1,25,64,128]{3,2,1,0:T(8,128)(2,1)S(1)}, bf16[1,25,64,128]{3,2,1,0:T(8,128)(2,1)}, u32[]{:S(2)}) %copy-start.2) | copy-done | bytes 409624
  1.6 1.6 %shard_map.104 = bf16[64,32,128]{2,1,0:T(8,128)(2,1)} custom-call(bf16[25,64,128]{2,1,0:T(8,128)(2,1)S(1)} %bitcast.17), custom_call_target="tpu_custom_call" | custom-call | tf_op jit(solution)/shard_map/pallas_call | solution.py:372
  3.2 0.0 copy-start.5
  3.2 11.1 %all-to-all-start = ((bf16[64,32,128]{2,1,0:T(8,128)(2,1)}), bf16[64,32,128]{2,1,0:T(8,128)(2,1)S(1)}, u32[]{:S(2)}, u32[]{:S(2)}) async-start(bf16[64,32,128]{2,1,0:T(8,128)(2,1)} %shard_map.104), calls=%async_computation | async-start | bytes 1048576 | tf_op jit(solution)/shard_map/all_to_all | solution.py:377
  14.3 0.0 copy-start.6
  14.3 0.0 copy-start.7
  14.4 0.6 %copy-done.6 = f32[1,3,1,64]{3,2,1,0:T(1,128)S(1)} copy-done((f32[1,3,1,64]{3,2,1,0:T(1,128)S(1)}, f32[1,3,1,64]{3,2,1,0:T(1,128)}, u32[]{:S(2)}) %copy-start.6) | copy-done | bytes 792
  15.0 0.4 shard_map.105
  15.4 0.5 collective-permute-start
  15.9 3.2 %collective-permute-start.1 = (s16[720,128]{1,0:T(8,128)(2,1)S(1)}, s16[720,128]{1,0:T(8,128)(2,1)S(1)}, u32[]{:S(2)}, u32[]{:S(2)}) collective-permute-start(s16[720,128]{1,0:T(8,128)(2,1)S(1)} %get-tuple-element.17), channel_id=1, source_target_pairs={{1,2},{2,1},{3,4},{4,3},{5,6},{6,5},{7,8},{8,7},{9,10},{10,9},{11,... | collective-permute-start | bytes 552968 | tf_op jit(solution)/shard_map/ppermute | solution.py:341
  19.1 2.5 %collective-permute-start.2 = (f32[2,16,128]{2,1,0:T(8,128)S(1)}, f32[2,16,128]{2,1,0:T(8,128)S(1)}, u32[]{:S(2)}, u32[]{:S(2)}) collective-permute-start(f32[2,16,128]{2,1,0:T(8,128)S(1)} %get-tuple-element.18), channel_id=1, source_target_pairs={{0,64},{64,0},{1,65},{65,1},{2,66},{66,2},{3,67},{67,3},{4,68},{68... | collective-permute-start | bytes 49160 | tf_op jit(solution)/shard_map/ppermute | solution.py:345
  21.7 4.1 %collective-permute-done.2.rim_ref = f32[2,16,128]{2,1,0:T(8,128)S(1)} collective-permute-done((f32[2,16,128]{2,1,0:T(8,128)S(1)}, f32[2,16,128]{2,1,0:T(8,128)S(1)}, u32[]{:S(2)}, u32[]{:S(2)}) %collective-permute-start.2) | collective-permute-done | bytes 16416 | tf_op jit(solution)/shard_map/ppermute | solution.py:345
  25.8 0.7 %collective-permute-done.1.far_ref = s16[720,128]{1,0:T(8,128)(2,1)S(1)} collective-permute-done((s16[720,128]{1,0:T(8,128)(2,1)S(1)}, s16[720,128]{1,0:T(8,128)(2,1)S(1)}, u32[]{:S(2)}, u32[]{:S(2)}) %collective-permute-start.1) | collective-permute-done | bytes 184352 | tf_op jit(solution)/shard_map/ppermute | solution.py:341
  26.5 1.0 %all-to-all-done.recv_ref = bf16[64,32,128]{2,1,0:T(8,128)(2,1)S(1)} async-done(((bf16[64,32,128]{2,1,0:T(8,128)(2,1)}), bf16[64,32,128]{2,1,0:T(8,128)(2,1)S(1)}, u32[]{:S(2)}, u32[]{:S(2)}) %all-to-all-start) | async-done | bytes 524320 | tf_op jit(solution)/shard_map/all_to_all | solution.py:377
  27.5 1.3 %shard_map.106 = (f32[10,64,128]{2,1,0:T(8,128)S(1)}, bf16[25,64,128]{2,1,0:T(8,128)(2,1)S(1)}, f32[2,16,128]{2,1,0:T(8,128)S(1)}, s16[656,128]{1,0:T(8,128)(2,1)S(1)}, f32[2,64,128]{2,1,0:T(8,128)S(1)}) custom-call(bf16[64,32,128]{2,1,0:T(8,128)(2,1)S(1)} %all-to-all-done.recv_ref, f32[10,64,128]{2,1,0:T(8,128)S(1)} %bitcast.16, ...), custom_call_target="tpu_custom_call" | custom-call | tf_op jit(solution)/shard_map/pallas_call | solution.py:389
  28.8 2.5 %collective-permute-start.5 = (f32[2,16,128]{2,1,0:T(8,128)S(1)}, f32[2,16,128]{2,1,0:T(8,128)S(1)}, u32[]{:S(2)}, u32[]{:S(2)}) collective-permute-start(f32[2,16,128]{2,1,0:T(8,128)S(1)} %get-tuple-element.22), channel_id=1, source_target_pairs={{0,64},{64,0},{1,65},{65,1},{2,66},{66,2},{3,67},{67,3},{4,68},{68... | collective-permute-start | bytes 49160 | tf_op jit(solution)/shard_map/ppermute | solution.py:345
  31.3 0.4 shard_map.108
  31.7 0.8 %collective-permute-start.3 = (s16[656,128]{1,0:T(8,128)(2,1)S(1)}, s16[656,128]{1,0:T(8,128)(2,1)S(1)}, u32[]{:S(2)}, u32[]{:S(2)}) collective-permute-start(s16[656,128]{1,0:T(8,128)(2,1)S(1)} %get-tuple-element.21), channel_id=1, source_target_pairs={{0,1},{1,0},{2,3},{3,2},{4,5},{5,4},{6,7},{7,6},{8,9},{9,8},{10,11... | collective-permute-start | bytes 503816 | tf_op jit(solution)/shard_map/ppermute | solution.py:341
  32.5 1.9 %collective-permute-start.4 = (s16[656,128]{1,0:T(8,128)(2,1)S(1)}, s16[656,128]{1,0:T(8,128)(2,1)S(1)}, u32[]{:S(2)}, u32[]{:S(2)}) collective-permute-start(s16[656,128]{1,0:T(8,128)(2,1)S(1)} %get-tuple-element.21), channel_id=1, source_target_pairs={{1,2},{2,1},{3,4},{4,3},{5,6},{6,5},{7,8},{8,7},{9,10},{10,9},{11,... | collective-permute-start | bytes 503816 | tf_op jit(solution)/shard_map/ppermute | solution.py:341
  34.4 1.3 %shard_map.109 = f32[64,1,128]{2,1,0:T(1,128)} custom-call(f32[10,64,128]{2,1,0:T(8,128)S(1)} %get-tuple-element.20.u_ref, f32[2,16,128]{2,1,0:T(8,128)S(1)} %collective-permute-done.5.rim_ref, f32[4,64,128]{2,1,0:T(8,128)S(1)} %get-tuple-element.24.fields_ref, f32[2,64,128]{2,1,0:T(8,128)S(1)} %get-tuple-element.25.walls_ref, ...), custom_call_target="tpu_custom_call" | custom-call | flops 17179869184 | tf_op jit(solution)/shard_map/pallas_call | solution.py:397
  35.7 9.7 %all-to-all-start.1 = ((f32[64,1,128]{2,1,0:T(1,128)}), f32[64,1,128]{2,1,0:T(1,128)S(1)}, u32[]{:S(2)}, u32[]{:S(2)}) async-start(f32[64,1,128]{2,1,0:T(1,128)} %shard_map.109), calls=%async_computation.1 | async-start | bytes 65536 | tf_op jit(solution)/shard_map/all_to_all | solution.py:400
  45.5 1.2 %shard_map.107 = (f32[10,64,128]{2,1,0:T(8,128)}, f32[8,128]{1,0:T(8,128)S(1)}) custom-call(bf16[25,64,128]{2,1,0:T(8,128)(2,1)S(1)} %get-tuple-element.19.tiles_ref, f32[10,64,128]{2,1,0:T(8,128)S(1)} %get-tuple-element.20.u_ref, s16[656,128]{1,0:T(8,128)(2,1)S(1)} %collective-permute-done.3.near_ref, s16[656,128]{1,0:T(8,128)(2,1)S(1)} %collective-permute-done.4.far_ref, ...), custom_call_target="tpu_custom_call" | custom-call | tf_op jit(solution)/shard_map/pallas_call | solution.py:401
  46.7 6.5 %all-to-all-done.1.recv_ref = f32[64,1,128]{2,1,0:T(1,128)S(1)} async-done(((f32[64,1,128]{2,1,0:T(1,128)}), f32[64,1,128]{2,1,0:T(1,128)S(1)}, u32[]{:S(2)}, u32[]{:S(2)}) %all-to-all-start.1) | async-done | bytes 32800 | tf_op jit(solution)/shard_map/all_to_all | solution.py:400
  53.2 1.2 %shard_map.110 = f32[6,1,256]{2,1,0:T(1,128)} custom-call(f32[64,1,128]{2,1,0:T(1,128)S(1)} %all-to-all-done.1.recv_ref, f32[8,128]{1,0:T(8,128)S(1)} %get-tuple-element.31.after_ref), custom_call_target="tpu_custom_call" | custom-call | tf_op jit(solution)/shard_map/pallas_call | solution.py:404
  (17 shorter events, 0.0 us)
Async XLA Ops:
  0.6 1.0 %copy-start.2 = (bf16[1,25,64,128]{3,2,1,0:T(8,128)(2,1)S(1)}, bf16[1,25,64,128]{3,2,1,0:T(8,128)(2,1)}, u32[]{:S(2)}) copy-start(bf16[1,25,64,128]{3,2,1,0:T(8,128)(2,1)} %param.9) | copy-start | bytes 1228804
  3.2 11.1 %copy-start = (f32[1,10,1,64,128]{4,3,2,1,0:T(8,128)S(1)}, f32[1,10,1,64,128]{4,3,2,1,0:T(8,128)}, u32[]{:S(2)}) copy-start(f32[1,10,1,64,128]{4,3,2,1,0:T(8,128)} %param.11) | copy-start | bytes 983044
  3.2 11.2 %copy-start.1 = (f32[1,10,1,64,128]{4,3,2,1,0:T(8,128)S(1)}, f32[1,10,1,64,128]{4,3,2,1,0:T(8,128)}, u32[]{:S(2)}) copy-start(f32[1,10,1,64,128]{4,3,2,1,0:T(8,128)} %param.10) | copy-start | bytes 983044
  3.2 11.2 %copy-start.3 = (f32[1,1,64,128]{3,2,1,0:T(8,128)S(1)}, f32[1,1,64,128]{3,2,1,0:T(8,128)}, u32[]{:S(2)}) copy-start(f32[1,1,64,128]{3,2,1,0:T(8,128)} %param.12) | copy-start | bytes 98308
  3.2 11.2 %copy-start.4 = (f32[1,1,64,128]{3,2,1,0:T(8,128)S(1)}, f32[1,1,64,128]{3,2,1,0:T(8,128)}, u32[]{:S(2)}) copy-start(f32[1,1,64,128]{3,2,1,0:T(8,128)} %param.13) | copy-start | bytes 98308
  3.2 11.2 %copy-start.5 = (f32[1,1,64,128]{3,2,1,0:T(8,128)S(1)}, f32[1,1,64,128]{3,2,1,0:T(8,128)}, u32[]{:S(2)}) copy-start(f32[1,1,64,128]{3,2,1,0:T(8,128)} %param.14) | copy-start | bytes 98308
  3.2 24.3 %all-to-all-start = ((bf16[64,32,128]{2,1,0:T(8,128)(2,1)}), bf16[64,32,128]{2,1,0:T(8,128)(2,1)S(1)}, u32[]{:S(2)}, u32[]{:S(2)}) async-start(bf16[64,32,128]{2,1,0:T(8,128)(2,1)} %shard_map.104), calls=%async_computation | async-start | bytes 1048576 | tf_op jit(solution)/shard_map/all_to_all | solution.py:377
  14.3 0.7 %copy-start.6 = (f32[1,3,1,64]{3,2,1,0:T(1,128)S(1)}, f32[1,3,1,64]{3,2,1,0:T(1,128)}, u32[]{:S(2)}) copy-start(f32[1,3,1,64]{3,2,1,0:T(1,128)} %param.15) | copy-start | bytes 2308
  14.3 0.7 %copy-start.7 = (s32[1,64,1]{1,2,0:T(1,128)S(1)}, s32[1,64,1]{1,2,0:T(1,128)}, u32[]{:S(2)}) copy-start(s32[1,64,1]{1,2,0:T(1,128)} %param.16) | copy-start | bytes 772
  14.3 0.7 %copy-start.8 = (s32[1,64]{1,0:T(1,128)S(1)}, s32[1,64]{1,0:T(1,128)}, u32[]{:S(2)}) copy-start(s32[1,64]{1,0:T(1,128)} %slot_ref.1) | copy-start | bytes 772
  15.4 10.4 %collective-permute-start = (s16[720,128]{1,0:T(8,128)(2,1)S(1)}, s16[720,128]{1,0:T(8,128)(2,1)S(1)}, u32[]{:S(2)}, u32[]{:S(2)}) collective-permute-start(s16[720,128]{1,0:T(8,128)(2,1)S(1)} %get-tuple-element.17), channel_id=1, source_target_pairs={{0,1},{1,0},{2,3},{3,2},{4,5},{5,4},{6,7},{7,6},{8,9},{9,8},{10,11... | collective-permute-start | bytes 552968 | tf_op jit(solution)/shard_map/ppermute | solution.py:341
  15.9 10.6 %collective-permute-start.1 = (s16[720,128]{1,0:T(8,128)(2,1)S(1)}, s16[720,128]{1,0:T(8,128)(2,1)S(1)}, u32[]{:S(2)}, u32[]{:S(2)}) collective-permute-start(s16[720,128]{1,0:T(8,128)(2,1)S(1)} %get-tuple-element.17), channel_id=1, source_target_pairs={{1,2},{2,1},{3,4},{4,3},{5,6},{6,5},{7,8},{8,7},{9,10},{10,9},{11,... | collective-permute-start | bytes 552968 | tf_op jit(solution)/shard_map/ppermute | solution.py:341
  19.1 6.7 %collective-permute-start.2 = (f32[2,16,128]{2,1,0:T(8,128)S(1)}, f32[2,16,128]{2,1,0:T(8,128)S(1)}, u32[]{:S(2)}, u32[]{:S(2)}) collective-permute-start(f32[2,16,128]{2,1,0:T(8,128)S(1)} %get-tuple-element.18), channel_id=1, source_target_pairs={{0,64},{64,0},{1,65},{65,1},{2,66},{66,2},{3,67},{67,3},{4,68},{68... | collective-permute-start | bytes 49160 | tf_op jit(solution)/shard_map/ppermute | solution.py:345
  28.8 5.6 %collective-permute-start.5 = (f32[2,16,128]{2,1,0:T(8,128)S(1)}, f32[2,16,128]{2,1,0:T(8,128)S(1)}, u32[]{:S(2)}, u32[]{:S(2)}) collective-permute-start(f32[2,16,128]{2,1,0:T(8,128)S(1)} %get-tuple-element.22), channel_id=1, source_target_pairs={{0,64},{64,0},{1,65},{65,1},{2,66},{66,2},{3,67},{67,3},{4,68},{68... | collective-permute-start | bytes 49160 | tf_op jit(solution)/shard_map/ppermute | solution.py:345
  31.7 13.7 %collective-permute-start.3 = (s16[656,128]{1,0:T(8,128)(2,1)S(1)}, s16[656,128]{1,0:T(8,128)(2,1)S(1)}, u32[]{:S(2)}, u32[]{:S(2)}) collective-permute-start(s16[656,128]{1,0:T(8,128)(2,1)S(1)} %get-tuple-element.21), channel_id=1, source_target_pairs={{0,1},{1,0},{2,3},{3,2},{4,5},{5,4},{6,7},{7,6},{8,9},{9,8},{10,11... | collective-permute-start | bytes 503816 | tf_op jit(solution)/shard_map/ppermute | solution.py:341
  32.5 13.0 %collective-permute-start.4 = (s16[656,128]{1,0:T(8,128)(2,1)S(1)}, s16[656,128]{1,0:T(8,128)(2,1)S(1)}, u32[]{:S(2)}, u32[]{:S(2)}) collective-permute-start(s16[656,128]{1,0:T(8,128)(2,1)S(1)} %get-tuple-element.21), channel_id=1, source_target_pairs={{1,2},{2,1},{3,4},{4,3},{5,6},{6,5},{7,8},{8,7},{9,10},{10,9},{11,... | collective-permute-start | bytes 503816 | tf_op jit(solution)/shard_map/ppermute | solution.py:341
  35.7 17.4 %all-to-all-start.1 = ((f32[64,1,128]{2,1,0:T(1,128)}), f32[64,1,128]{2,1,0:T(1,128)S(1)}, u32[]{:S(2)}, u32[]{:S(2)}) async-start(f32[64,1,128]{2,1,0:T(1,128)} %shard_map.109), calls=%async_computation.1 | async-start | bytes 65536 | tf_op jit(solution)/shard_map/all_to_all | solution.py:400

commit v5 on v4

--- a/solution.py
+++ b/solution.py
@@ -15,6 +15,7 @@
 ND = 1
 BLADES = 36
 ROWS = 32
+PITCH = ROWS + 1
 BLOCK = 16
 FULL = 32000.0
 AHEAD = 1 << 34
@@ -34,17 +35,18 @@
 
 def prep_kernel(jac_ref, send_ref, wide):
     planes = jac_ref.shape[1]
-    wide[25 * planes : ROWS * planes, :] = jnp.zeros(((ROWS - 25) * planes, 128), F32)
+    pitch = planes + 1
+    wide[25 * pitch : ROWS * pitch, :] = jnp.zeros(((ROWS - 25) * pitch, 128), F32)
     lane = lanes((planes, 128))
     wall = jnp.zeros((planes, 128), F32)
     for e in range(25):
         entry = jac_ref[e].astype(F32)
-        wide[e * planes : (e + 1) * planes, :] = entry
+        wide[e * pitch : e * pitch + planes, :] = entry
         wall = jnp.where(lane == e, pltpu.roll(entry, e, axis=1) if e else entry, wall)
-    wide[25 * planes + 1 : 26 * planes, :] = wall[0 : planes - 1]
-    wide[26 * planes : 27 * planes - 1, :] = wall[1:planes]
+    wide[25 * pitch + 1 : 25 * pitch + planes, :] = wall[0 : planes - 1]
+    wide[26 * pitch : 26 * pitch + planes - 1, :] = wall[1:planes]
     for i in range(planes):
-        send_ref[i] = wide[pl.ds(i, ROWS, stride=planes), :].astype(BF16)
+        send_ref[i] = wide[pl.ds(i, ROWS, stride=pitch), :].astype(BF16)
 
 
 def routing(owner_row, rank, values, first):
@@ -102,18 +104,15 @@
     fields_ref[3] = flow
 
 
-def beside_kernel(near_ref, far_ref, weight_ref, route_ref, diss_ref):
-    width = weight_ref.shape[1]
-    for at, ref in enumerate((near_ref, far_ref)):
-        last = ref.shape[0] - width
-        exponent = ref[last - 16 : last, :].astype(jnp.int32).astype(F32)[15:16, :]
-        code = ref[last:, :].astype(jnp.int32).astype(F32)
-        low = pltpu.roll(code, 120, axis=1)
-        info = (code + low * (1.0 / FULL)) * (jnp.exp2(exponent) * (1.0 / FULL))
-        column = [info[:, k : k + 1] for k in range(7)]
-        slot, owner, rank = [jnp.round(column[k]) for k in (3, 5, 6)]
-        route_ref[at], weight_ref[at] = routing(turned(owner), rank, column[:3] + [slot], CAP * (at + 1))
-        diss_ref[at] = jnp.zeros((width, 128), F32) + column[4]
+def routing_beside(ref, width, first):
+    last = 10 * width + 16
+    exponent = ref[last - 16 : last, :].astype(jnp.int32).astype(F32)[15:16, :]
+    code = ref[last:, :].astype(jnp.int32).astype(F32)
+    low = pltpu.roll(code, 120, axis=1)
+    info = (code + low * (1.0 / FULL)) * (jnp.exp2(exponent) * (1.0 / FULL))
+    column = [info[:, k : k + 1] for k in range(7)]
+    slot, owner, rank = [jnp.round(column[k]) for k in (3, 5, 6)]
+    return *routing(turned(owner), rank, column[:3] + [slot], first), column[4]
 
 
 def exponent_of(top):
@@ -209,25 +208,76 @@
     return new
 
 
+def parts(value):
+    high = value.astype(BF16).astype(F32)
+    rest = value - high
+    middle = rest.astype(BF16).astype(F32)
+    return [high, middle, rest - middle]
+
+
+def chosen(values, within):
+    out = values[0]
+    for k in range(1, 6):
+        out = jnp.where(within == k, values[k], out)
+    return out
+
+
+def wall_terms(u_ref, fields_ref, walls, own_routing, beside):
+    width = u_ref.shape[1]
+    shape = (width, 128)
+    lane, row = lanes(shape), rows(shape)
+    within = lane % 8
+    zero = jnp.zeros(shape, F32)
+    at_wall = [zero + u_ref[c, :, 0:1] for c in range(10)]
+    u = chosen([at_wall[c] for c in WALL], within)
+    other = chosen([at_wall[(c + 5) % 10] for c in WALL], within)
+    right = chosen([u_ref[c, :, 1:2] for c in WALL], within)
+    down = jnp.where(row == 0, 0.0, pltpu.roll(u, 1, axis=0))
+    up = jnp.where(row == width - 1, 0.0, pltpu.roll(u, width - 1, axis=0))
+    own = u - fields_ref[0] * (
+        fields_ref[2] * other + fields_ref[1] * (6.0 * u - (down + up + right)) - fields_ref[3]
+    )
+
+    def sent(route, weight, value):
+        value = jnp.concatenate(parts(weight * jnp.where(within == 6, 1.0, value)), axis=1).astype(BF16)
+        total = jnp.dot(route.astype(BF16), value, preferred_element_type=F32)
+        return total[:, 0:128] + total[:, 128:256] + total[:, 256:384]
+
+    routed = sent(*own_routing, own)
+    even = lax.axis_index("brick") % 2 == 0
+    for at, share in enumerate((-0.5, 0.5)):
+        route, weight, diss = beside[at]
+        share = jnp.where(even, -share, share)
+        tile = jnp.where(even, walls[1 - at], walls[at])
+        re, im = zero, zero
+        for n in range(5):
+            entry = pltpu.roll(tile, 127 - 5 * n, axis=1)
+            re = re + entry * at_wall[n]
+            im = im + entry * at_wall[5 + n]
+        conv = jnp.where(lane < 3, re, jnp.where(lane < 6, pltpu.roll(im, 3, axis=1), 0.0))
+        for turn in (8, 16, 32, 64):
+            conv = conv + pltpu.roll(conv, turn, axis=1)
+        routed = routed + sent(route, weight, diss * u + share * conv)
+    return routed
+
+
 def first_kernel(
     phase, recv_ref, u_ref, near_ref, far_ref, rim_ref, source_ref, step_ref, diss_ref, freq_ref,
-    out_ref, tiles_ref, rim_out_ref, code_ref, walls_ref, wide,
+    fields_ref, weight_ref, route_ref, out_ref, tiles_ref, rim_out_ref, code_ref, sum_ref, wide,
 ):
     rims = rims_beside(rim_ref, lax.axis_index("passage"), phase)
     width = u_ref.shape[1]
     for j in range(width):
-        wide[j * ROWS : (j + 1) * ROWS, :] = recv_ref[j].astype(F32)
-    for at in range(2):
-        walls_ref[at] = wide[pl.ds(25 + at, width, stride=ROWS), :]
+        wide[j * PITCH : j * PITCH + ROWS, :] = recv_ref[j].astype(F32)
     for e in range(25):
-        tiles_ref[e] = wide[pl.ds(e, width, stride=ROWS), :].astype(BF16)
+        tiles_ref[e] = wide[pl.ds(e, width, stride=PITCH), :].astype(BF16)
     rim_out_ref[...] = jnp.zeros_like(rim_out_ref)
     blocks = width // BLOCK
     scales = code_scale(near_ref, width), code_scale(far_ref, width)
     for b in range(blocks):
         new = sweep_block(
             b, blocks, u_ref, near_ref, far_ref, scales, rims,
-            lambda e: wide[pl.ds(BLOCK * b * ROWS + e, BLOCK, stride=ROWS), :],
+            lambda e: wide[pl.ds(BLOCK * b * PITCH + e, BLOCK, stride=PITCH), :],
             source_ref, step_ref, diss_ref, freq_ref,
         )
         for c in range(10):
@@ -237,6 +287,9 @@
             if b == blocks - 1:
                 rim_out_ref[1, c : c + 1, :] = new[c][BLOCK - 1 : BLOCK]
     coded(out_ref, code_ref)
+    walls = [wide[pl.ds(25 + at, width, stride=PITCH), :] for at in range(2)]
+    beside = [routing_beside(ref, width, CAP * (at + 1)) for at, ref in enumerate((near_ref, far_ref))]
+    sum_ref[...] = wall_terms(out_ref, fields_ref, walls, (route_ref[...], weight_ref[...]), beside)
 
 
 def second_kernel(
@@ -257,52 +310,15 @@
     after_ref[...] = jnp.zeros_like(after_ref)
 
 
-def wall_kernel(
-    phase, u_ref, rim_ref, fields_ref, walls_ref, weight_ref, route_ref, weights_ref, routes_ref, disses_ref, send_ref
-):
-    width = u_ref.shape[1]
-    shape = (width, 128)
-    lane, row = lanes(shape), rows(shape)
-    within = lane % 8
-    zero = jnp.zeros(shape, F32)
-    at_wall = [zero + u_ref[c, :, 0:1] for c in range(10)]
-
-    def chosen(values):
-        out = values[0]
-        for k in range(1, 6):
-            out = jnp.where(within == k, values[k], out)
-        return out
-
-    below, above = rims_beside(rim_ref, lax.axis_index("passage"), phase)
-    u = chosen([at_wall[c] for c in WALL])
-    other = chosen([at_wall[(c + 5) % 10] for c in WALL])
-    right = chosen([u_ref[c, :, 1:2] for c in WALL])
-    below = chosen([below[c][:, 0:1] for c in WALL])
-    above = chosen([above[c][:, 0:1] for c in WALL])
-    down = jnp.where(row == 0, below, pltpu.roll(u, 1, axis=0))
-    up = jnp.where(row == width - 1, above, pltpu.roll(u, width - 1, axis=0))
-    own = u - fields_ref[0] * (
-        fields_ref[2] * other + fields_ref[1] * (6.0 * u - (down + up + right)) - fields_ref[3]
-    )
-
-    def sent(route, weight, value):
-        value = weight * jnp.where(within == 6, 1.0, value)
-        return jnp.dot(route, value, precision=lax.Precision.HIGHEST, preferred_element_type=F32)
-
-    routed = sent(route_ref[...], weight_ref[...], own)
-    even = lax.axis_index("brick") % 2 == 0
-    for at, share in enumerate((-0.5, 0.5)):
-        share = jnp.where(even, -share, share)
-        tile = jnp.where(even, walls_ref[1 - at], walls_ref[at])
-        re, im = zero, zero
-        for n in range(5):
-            entry = pltpu.roll(tile, 127 - 5 * n, axis=1)
-            re = re + entry * at_wall[n]
-            im = im + entry * at_wall[5 + n]
-        conv = jnp.where(lane < 3, re, jnp.where(lane < 6, pltpu.roll(im, 3, axis=1), 0.0))
-        for turn in (8, 16, 32, 64):
-            conv = conv + pltpu.roll(conv, turn, axis=1)
-        routed = routed + sent(routes_ref[at], weights_ref[at], disses_ref[at] * u + share * conv)
+def rim_kernel(phase, sum_ref, rim_ref, fields_ref, weight_ref, route_ref, send_ref):
+    width = sum_ref.shape[0]
+    within = lanes((1, 128)) % 8
+    routed = sum_ref[...]
+    for face, layer in zip((0, width - 1), rims_beside(rim_ref, lax.axis_index("passage"), phase)):
+        value = chosen([jnp.zeros((1, 128), F32) + layer[c][:, 0:1] for c in WALL], within)
+        at = slice(face, face + 1)
+        value = weight_ref[at, :] * jnp.where(within == 6, 0.0, fields_ref[0, at, :] * fields_ref[1, at, :] * value)
+        routed = routed + route_ref[:, at] * value
     for q in range(send_ref.shape[0]):
         send_ref[q] = routed[q : q + 1, :]
 
@@ -311,14 +327,17 @@
     peers = recv_ref.shape[0]
     for q in range(peers):
         dense[q : q + 1, :] = recv_ref[q]
-    total = jnp.zeros((8, NODE_DEV), F32)
     node = lanes((peers, NODE_DEV)).astype(F32) + 1.0
-    terms = dense[...].T
-    for r in range(CAP * PLANES):
-        hit = jnp.where(dense[:, 8 * r + 6 : 8 * r + 7] == node, 1.0, 0.0)
-        total = total + jnp.dot(
-            terms[8 * r : 8 * r + 8, :], hit, precision=lax.Precision.HIGHEST, preferred_element_type=F32
-        )
+    terms = parts(dense[...].T)
+    total = jnp.zeros((24, NODE_DEV), F32)
+    for first in range(0, CAP * PLANES, CAP):
+        hits, values = [], []
+        for r in range(first, first + CAP):
+            hits.append(jnp.where(dense[:, 8 * r + 6 : 8 * r + 7] == node, 1.0, 0.0))
+            values.append(jnp.concatenate([t[8 * r : 8 * r + 8, :] for t in terms], axis=0))
+        hits, values = jnp.concatenate(hits, axis=0).astype(BF16), jnp.concatenate(values, axis=1).astype(BF16)
+        total = total + jnp.dot(values, hits, preferred_element_type=F32)
+    total = total[0:8] + total[8:16] + total[16:24]
     for c in range(6):
         out_ref[c] = total[c : c + 1, :]
 
@@ -372,7 +391,7 @@
     (send,) = kernel_call(
         prep_kernel,
         [((bricks, ROWS, depth), BF16)],
-        [pltpu.VMEM((ROWS * bricks, depth), F32)],
+        [pltpu.VMEM((ROWS * (bricks + 1), depth), F32)],
     )(jac)
     recv = lax.all_to_all(send, "brick", 0, 0, tiled=True)
     face = (width, 128)
@@ -382,22 +401,18 @@
     )(psi, source, *scalars, face_owner.reshape(1, width), face_slot, normals.reshape(3, 1, width))
     rims = swapped(rims, passes)
     near, far = planes_beside(code, bricks)
-    weights, routes, disses = kernel_call(
-        beside_kernel, [((2, *face), F32), ((2, bricks, width), F32), ((2, *face), F32)]
-    )(near, far)
-
-    state, tiles, rims, code, walls = kernel_call(
+    state, tiles, rims, code, terms = kernel_call(
         functools.partial(first_kernel, phase),
-        [(field, F32), ((25, width, depth), BF16), (rim, F32), (plane, I16), ((2, *face), F32)],
-        [pltpu.VMEM((ROWS * width, depth), F32)],
-    )(recv, psi, near, far, rims, source, *scalars)
+        [(field, F32), ((25, width, depth), BF16), (rim, F32), (plane, I16), (face, F32)],
+        [pltpu.VMEM((PITCH * width, depth), F32)],
+    )(recv, psi, near, far, rims, source, *scalars, fields, weight, route)
 
     rims = swapped(rims, passes)
+    (routed,) = kernel_call(functools.partial(rim_kernel, phase), [((bricks, 1, 128), F32)], flops=AHEAD)(
+        terms, rims, fields, weight, route
+    )
+    arrived = lax.all_to_all(routed, "brick", 0, 0, tiled=True)
     near, far = planes_beside(code, bricks)
-    (routed,) = kernel_call(functools.partial(wall_kernel, phase), [((bricks, 1, 128), F32)], flops=AHEAD)(
-        state, rims, fields, walls, weight, route, weights, routes, disses
-    )
-    arrived = lax.all_to_all(routed, "brick", 0, 0, tiled=True)
     state, after = kernel_call(functools.partial(second_kernel, phase), [(field, F32), ((8, 128), F32)])(
         tiles, state, near, far, rims, source, *scalars
     )

time: 54.7 us -> 53.6 us (0.980)
  Pallas kernels: 7.39 us -> 5.99 us
    pallas_call x2 -> x1, Pallas kernels: 1.71 us -> 0.72 us  [body(): kernel_call(functools.partial(rim_kernel, phase), [((bricks, 1, 128), F32...]
    all_to_all x1, starting transfers between devices: 9.7 us -> 10.4 us  [body(): arrived = lax.all_to_all(routed, 'brick', 0, 0, tiled=True)]
  transfers between devices with their start and end apart: 8 -> 8, of which waited for: 4 -> 4; matrix products, arithmetic and copies ran while one was open for 0% -> 0% of each run, Pallas kernels for 6% -> 4%
where the time goes in v5:
time: 53.6 us; the launch traced here: 53.3 us
  starting transfers between devices  32.5 us (61%)
  waiting for transfers between devices  12.4 us (23%)
  Pallas kernels  5.99 us (11%)
  local copies, waits for them, and re-layouts  1.63 us (3%)
  between operations  0.8 us (1%)
    all_to_all x1, starting transfers between devices, body(): recv = lax.all_to_all(send, 'brick', 0, 0, tiled=True)  11.1 us
    all_to_all x1, starting transfers between devices, body(): arrived = lax.all_to_all(routed, 'brick', 0, 0, tiled=True)  10.4 us
    all_to_all x1, waiting for transfers between devices, body(): arrived = lax.all_to_all(routed, 'brick', 0, 0, tiled=True)  6.47 us
    ppermute x4, starting transfers between devices, planes_beside(): return (lax.ppermute(code, 'brick', near), lax.ppermute(code, 'brick', far))  5.92 us
    ppermute x2, starting transfers between devices, swapped(): lax.ppermute(rim, 'passage', [(i, (i + 1) % passes) for i in range(passes)])  5.06 us
    ppermute x2, waiting for transfers between devices, swapped(): lax.ppermute(rim, 'passage', [(i, (i + 1) % passes) for i in range(passes)])  4.25 us
    pallas_call x1, Pallas kernels, body(): kernel_call(functools.partial(first_kernel, phase), [(field, F32), ((25,...  1.67 us
    unnamed x18, local copies, waits for them, and re-layouts  1.63 us
  transfers between devices with their start and end apart: 8, of which 4 were waited for; matrix products, arithmetic and copies ran while one was open for 0% of the time, Pallas kernels for 4%

profile of v5, /device:TPU:1, one launch (start us, length us, event | category | flops | bytes accessed | tf_op | source)
XLA Modules:
  0.0 53.3 jit_solution(16520951048106803103)
XLA Ops:
  0.6 1.0 %copy-done.2 = bf16[1,25,64,128]{3,2,1,0:T(8,128)(2,1)S(1)} copy-done((bf16[1,25,64,128]{3,2,1,0:T(8,128)(2,1)S(1)}, bf16[1,25,64,128]{3,2,1,0:T(8,128)(2,1)}, u32[]{:S(2)}) %copy-start.2) | copy-done | bytes 409624
  1.6 1.0 %shard_map.104 = bf16[64,32,128]{2,1,0:T(8,128)(2,1)} custom-call(bf16[25,64,128]{2,1,0:T(8,128)(2,1)S(1)} %bitcast.17), custom_call_target="tpu_custom_call" | custom-call | tf_op jit(solution)/shard_map/pallas_call | solution.py:391
  2.7 0.0 copy-start.5
  2.7 11.1 %all-to-all-start = ((bf16[64,32,128]{2,1,0:T(8,128)(2,1)}), bf16[64,32,128]{2,1,0:T(8,128)(2,1)S(1)}, u32[]{:S(2)}, u32[]{:S(2)}) async-start(bf16[64,32,128]{2,1,0:T(8,128)(2,1)} %shard_map.104), calls=%async_computation | async-start | bytes 1048576 | tf_op jit(solution)/shard_map/all_to_all | solution.py:396
  13.8 0.0 copy-start.6
  13.8 0.0 copy-start.7
  13.8 0.0 copy-start.8
  13.9 0.6 %copy-done.6 = f32[1,3,1,64]{3,2,1,0:T(1,128)S(1)} copy-done((f32[1,3,1,64]{3,2,1,0:T(1,128)S(1)}, f32[1,3,1,64]{3,2,1,0:T(1,128)}, u32[]{:S(2)}) %copy-start.6) | copy-done | bytes 792
  14.5 0.4 shard_map.105
  14.8 3.5 %collective-permute-start.1 = (s16[720,128]{1,0:T(8,128)(2,1)S(1)}, s16[720,128]{1,0:T(8,128)(2,1)S(1)}, u32[]{:S(2)}, u32[]{:S(2)}) collective-permute-start(s16[720,128]{1,0:T(8,128)(2,1)S(1)} %get-tuple-element.14), channel_id=1, source_target_pairs={{1,2},{2,1},{3,4},{4,3},{5,6},{6,5},{7,8},{8,7},{9,10},{10,9},{11,... | collective-permute-start | bytes 552968 | tf_op jit(solution)/shard_map/ppermute | solution.py:360
  18.4 0.1 collective-permute-start
  18.5 2.5 %collective-permute-start.2 = (f32[2,16,128]{2,1,0:T(8,128)S(1)}, f32[2,16,128]{2,1,0:T(8,128)S(1)}, u32[]{:S(2)}, u32[]{:S(2)}) collective-permute-start(f32[2,16,128]{2,1,0:T(8,128)S(1)} %get-tuple-element.15), channel_id=1, source_target_pairs={{0,64},{64,0},{1,65},{65,1},{2,66},{66,2},{3,67},{67,3},{4,68},{68... | collective-permute-start | bytes 49160 | tf_op jit(solution)/shard_map/ppermute | solution.py:364
  21.0 4.2 %collective-permute-done.2.rim_ref = f32[2,16,128]{2,1,0:T(8,128)S(1)} collective-permute-done((f32[2,16,128]{2,1,0:T(8,128)S(1)}, f32[2,16,128]{2,1,0:T(8,128)S(1)}, u32[]{:S(2)}, u32[]{:S(2)}) %collective-permute-start.2) | collective-permute-done | bytes 16416 | tf_op jit(solution)/shard_map/ppermute | solution.py:364
  25.3 0.7 %collective-permute-done.1.far_ref = s16[720,128]{1,0:T(8,128)(2,1)S(1)} collective-permute-done((s16[720,128]{1,0:T(8,128)(2,1)S(1)}, s16[720,128]{1,0:T(8,128)(2,1)S(1)}, u32[]{:S(2)}, u32[]{:S(2)}) %collective-permute-start.1) | collective-permute-done | bytes 184352 | tf_op jit(solution)/shard_map/ppermute | solution.py:360
  26.0 1.0 %all-to-all-done.recv_ref = bf16[64,32,128]{2,1,0:T(8,128)(2,1)S(1)} async-done(((bf16[64,32,128]{2,1,0:T(8,128)(2,1)}), bf16[64,32,128]{2,1,0:T(8,128)(2,1)S(1)}, u32[]{:S(2)}, u32[]{:S(2)}) %all-to-all-start) | async-done | bytes 524320 | tf_op jit(solution)/shard_map/all_to_all | solution.py:396
  27.0 1.7 %shard_map.106 = (f32[10,64,128]{2,1,0:T(8,128)S(1)}, bf16[25,64,128]{2,1,0:T(8,128)(2,1)S(1)}, f32[2,16,128]{2,1,0:T(8,128)S(1)}, s16[656,128]{1,0:T(8,128)(2,1)S(1)}, f32[64,128]{1,0:T(8,128)S(1)}) custom-call(bf16[64,32,128]{2,1,0:T(8,128)(2,1)S(1)} %all-to-all-done.recv_ref, f32[10,64,128]{2,1,0:T(8,128)S(1)} %bitcast.16, ...), custom_call_target="tpu_custom_call" | custom-call | tf_op jit(solution)/shard_map/pallas_call | solution.py:404
  28.6 2.5 %collective-permute-start.5 = (f32[2,16,128]{2,1,0:T(8,128)S(1)}, f32[2,16,128]{2,1,0:T(8,128)S(1)}, u32[]{:S(2)}, u32[]{:S(2)}) collective-permute-start(f32[2,16,128]{2,1,0:T(8,128)S(1)} %get-tuple-element.22), channel_id=1, source_target_pairs={{0,64},{64,0},{1,65},{65,1},{2,66},{66,2},{3,67},{67,3},{4,68},{68... | collective-permute-start | bytes 49160 | tf_op jit(solution)/shard_map/ppermute | solution.py:364
  31.2 2.2 %collective-permute-start.4 = (s16[656,128]{1,0:T(8,128)(2,1)S(1)}, s16[656,128]{1,0:T(8,128)(2,1)S(1)}, u32[]{:S(2)}, u32[]{:S(2)}) collective-permute-start(s16[656,128]{1,0:T(8,128)(2,1)S(1)} %get-tuple-element.21), channel_id=1, source_target_pairs={{1,2},{2,1},{3,4},{4,3},{5,6},{6,5},{7,8},{8,7},{9,10},{10,9},{11,... | collective-permute-start | bytes 503816 | tf_op jit(solution)/shard_map/ppermute | solution.py:360
  33.4 0.1 collective-permute-start.3
  33.5 0.7 %shard_map.108 = f32[64,1,128]{2,1,0:T(1,128)} custom-call(f32[64,128]{1,0:T(8,128)S(1)} %get-tuple-element.24.sum_ref, f32[2,16,128]{2,1,0:T(8,128)S(1)} %collective-permute-done.5.rim_ref, f32[4,64,128]{2,1,0:T(8,128)S(1)} %get-tuple-element.16.fields_ref, f32[64,128]{1,0:T(8,128)S(1)} %get-tuple-element.17.weight_ref, ...), custom_call_target="tpu_custom_call" | custom-call | flops 17179869184 | tf_op jit(solution)/shard_map/pallas_call | solution.py:411
  34.2 10.4 %all-to-all-start.1 = ((f32[64,1,128]{2,1,0:T(1,128)}), f32[64,1,128]{2,1,0:T(1,128)S(1)}, u32[]{:S(2)}, u32[]{:S(2)}) async-start(f32[64,1,128]{2,1,0:T(1,128)} %shard_map.108), calls=%async_computation.1 | async-start | bytes 65536 | tf_op jit(solution)/shard_map/all_to_all | solution.py:414
  44.7 1.2 %shard_map.107 = (f32[10,64,128]{2,1,0:T(8,128)}, f32[8,128]{1,0:T(8,128)S(1)}) custom-call(bf16[25,64,128]{2,1,0:T(8,128)(2,1)S(1)} %get-tuple-element.19.tiles_ref, f32[10,64,128]{2,1,0:T(8,128)S(1)} %get-tuple-element.20.u_ref, s16[656,128]{1,0:T(8,128)(2,1)S(1)} %collective-permute-done.3.near_ref, s16[656,128]{1,0:T(8,128)(2,1)S(1)} %collective-permute-done.4.far_ref, ...), custom_call_target="tpu_custom_call" | custom-call | tf_op jit(solution)/shard_map/pallas_call | solution.py:416
  45.9 6.5 %all-to-all-done.1.recv_ref = f32[64,1,128]{2,1,0:T(1,128)S(1)} async-done(((f32[64,1,128]{2,1,0:T(1,128)}), f32[64,1,128]{2,1,0:T(1,128)S(1)}, u32[]{:S(2)}, u32[]{:S(2)}) %all-to-all-start.1) | async-done | bytes 32800 | tf_op jit(solution)/shard_map/all_to_all | solution.py:414
  52.4 1.0 %shard_map.109 = f32[6,1,256]{2,1,0:T(1,128)} custom-call(f32[64,1,128]{2,1,0:T(1,128)S(1)} %all-to-all-done.1.recv_ref, f32[8,128]{1,0:T(8,128)S(1)} %get-tuple-element.25.after_ref), custom_call_target="tpu_custom_call" | custom-call | tf_op jit(solution)/shard_map/pallas_call | solution.py:419
  (16 shorter events, 0.0 us)
Async XLA Ops:
  0.6 1.0 %copy-start.2 = (bf16[1,25,64,128]{3,2,1,0:T(8,128)(2,1)S(1)}, bf16[1,25,64,128]{3,2,1,0:T(8,128)(2,1)}, u32[]{:S(2)}) copy-start(bf16[1,25,64,128]{3,2,1,0:T(8,128)(2,1)} %param.9) | copy-start | bytes 1228804
  2.7 11.1 %copy-start = (f32[1,10,1,64,128]{4,3,2,1,0:T(8,128)S(1)}, f32[1,10,1,64,128]{4,3,2,1,0:T(8,128)}, u32[]{:S(2)}) copy-start(f32[1,10,1,64,128]{4,3,2,1,0:T(8,128)} %param.11) | copy-start | bytes 983044
  2.7 11.2 %copy-start.1 = (f32[1,10,1,64,128]{4,3,2,1,0:T(8,128)S(1)}, f32[1,10,1,64,128]{4,3,2,1,0:T(8,128)}, u32[]{:S(2)}) copy-start(f32[1,10,1,64,128]{4,3,2,1,0:T(8,128)} %param.10) | copy-start | bytes 983044
  2.7 11.2 %copy-start.3 = (f32[1,1,64,128]{3,2,1,0:T(8,128)S(1)}, f32[1,1,64,128]{3,2,1,0:T(8,128)}, u32[]{:S(2)}) copy-start(f32[1,1,64,128]{3,2,1,0:T(8,128)} %param.12) | copy-start | bytes 98308
  2.7 11.2 %copy-start.4 = (f32[1,1,64,128]{3,2,1,0:T(8,128)S(1)}, f32[1,1,64,128]{3,2,1,0:T(8,128)}, u32[]{:S(2)}) copy-start(f32[1,1,64,128]{3,2,1,0:T(8,128)} %param.13) | copy-start | bytes 98308
  2.7 11.2 %copy-start.5 = (f32[1,1,64,128]{3,2,1,0:T(8,128)S(1)}, f32[1,1,64,128]{3,2,1,0:T(8,128)}, u32[]{:S(2)}) copy-start(f32[1,1,64,128]{3,2,1,0:T(8,128)} %param.14) | copy-start | bytes 98308
  2.7 24.3 %all-to-all-start = ((bf16[64,32,128]{2,1,0:T(8,128)(2,1)}), bf16[64,32,128]{2,1,0:T(8,128)(2,1)S(1)}, u32[]{:S(2)}, u32[]{:S(2)}) async-start(bf16[64,32,128]{2,1,0:T(8,128)(2,1)} %shard_map.104), calls=%async_computation | async-start | bytes 1048576 | tf_op jit(solution)/shard_map/all_to_all | solution.py:396
  13.8 0.7 %copy-start.6 = (f32[1,3,1,64]{3,2,1,0:T(1,128)S(1)}, f32[1,3,1,64]{3,2,1,0:T(1,128)}, u32[]{:S(2)}) copy-start(f32[1,3,1,64]{3,2,1,0:T(1,128)} %param.15) | copy-start | bytes 2308
  13.8 0.7 %copy-start.7 = (s32[1,64,1]{1,2,0:T(1,128)S(1)}, s32[1,64,1]{1,2,0:T(1,128)}, u32[]{:S(2)}) copy-start(s32[1,64,1]{1,2,0:T(1,128)} %param.16) | copy-start | bytes 772
  13.8 0.7 %copy-start.8 = (s32[1,64]{1,0:T(1,128)S(1)}, s32[1,64]{1,0:T(1,128)}, u32[]{:S(2)}) copy-start(s32[1,64]{1,0:T(1,128)} %slot_ref.1) | copy-start | bytes 772
  14.8 11.2 %collective-permute-start.1 = (s16[720,128]{1,0:T(8,128)(2,1)S(1)}, s16[720,128]{1,0:T(8,128)(2,1)S(1)}, u32[]{:S(2)}, u32[]{:S(2)}) collective-permute-start(s16[720,128]{1,0:T(8,128)(2,1)S(1)} %get-tuple-element.14), channel_id=1, source_target_pairs={{1,2},{2,1},{3,4},{4,3},{5,6},{6,5},{7,8},{8,7},{9,10},{10,9},{11,... | collective-permute-start | bytes 552968 | tf_op jit(solution)/shard_map/ppermute | solution.py:360
  18.4 7.6 %collective-permute-start = (s16[720,128]{1,0:T(8,128)(2,1)S(1)}, s16[720,128]{1,0:T(8,128)(2,1)S(1)}, u32[]{:S(2)}, u32[]{:S(2)}) collective-permute-start(s16[720,128]{1,0:T(8,128)(2,1)S(1)} %get-tuple-element.14), channel_id=1, source_target_pairs={{0,1},{1,0},{2,3},{3,2},{4,5},{5,4},{6,7},{7,6},{8,9},{9,8},{10,11... | collective-permute-start | bytes 552968 | tf_op jit(solution)/shard_map/ppermute | solution.py:360
  18.5 6.8 %collective-permute-start.2 = (f32[2,16,128]{2,1,0:T(8,128)S(1)}, f32[2,16,128]{2,1,0:T(8,128)S(1)}, u32[]{:S(2)}, u32[]{:S(2)}) collective-permute-start(f32[2,16,128]{2,1,0:T(8,128)S(1)} %get-tuple-element.15), channel_id=1, source_target_pairs={{0,64},{64,0},{1,65},{65,1},{2,66},{66,2},{3,67},{67,3},{4,68},{68... | collective-permute-start | bytes 49160 | tf_op jit(solution)/shard_map/ppermute | solution.py:364
  28.6 4.8 %collective-permute-start.5 = (f32[2,16,128]{2,1,0:T(8,128)S(1)}, f32[2,16,128]{2,1,0:T(8,128)S(1)}, u32[]{:S(2)}, u32[]{:S(2)}) collective-permute-start(f32[2,16,128]{2,1,0:T(8,128)S(1)} %get-tuple-element.22), channel_id=1, source_target_pairs={{0,64},{64,0},{1,65},{65,1},{2,66},{66,2},{3,67},{67,3},{4,68},{68... | collective-permute-start | bytes 49160 | tf_op jit(solution)/shard_map/ppermute | solution.py:364
  31.2 13.5 %collective-permute-start.4 = (s16[656,128]{1,0:T(8,128)(2,1)S(1)}, s16[656,128]{1,0:T(8,128)(2,1)S(1)}, u32[]{:S(2)}, u32[]{:S(2)}) collective-permute-start(s16[656,128]{1,0:T(8,128)(2,1)S(1)} %get-tuple-element.21), channel_id=1, source_target_pairs={{1,2},{2,1},{3,4},{4,3},{5,6},{6,5},{7,8},{8,7},{9,10},{10,9},{11,... | collective-permute-start | bytes 503816 | tf_op jit(solution)/shard_map/ppermute | solution.py:360
  33.4 11.3 %collective-permute-start.3 = (s16[656,128]{1,0:T(8,128)(2,1)S(1)}, s16[656,128]{1,0:T(8,128)(2,1)S(1)}, u32[]{:S(2)}, u32[]{:S(2)}) collective-permute-start(s16[656,128]{1,0:T(8,128)(2,1)S(1)} %get-tuple-element.21), channel_id=1, source_target_pairs={{0,1},{1,0},{2,3},{3,2},{4,5},{5,4},{6,7},{7,6},{8,9},{9,8},{10,11... | collective-permute-start | bytes 503816 | tf_op jit(solution)/shard_map/ppermute | solution.py:360
  34.2 18.2 %all-to-all-start.1 = ((f32[64,1,128]{2,1,0:T(1,128)}), f32[64,1,128]{2,1,0:T(1,128)S(1)}, u32[]{:S(2)}, u32[]{:S(2)}) async-start(f32[64,1,128]{2,1,0:T(1,128)} %shard_map.108), calls=%async_computation.1 | async-start | bytes 65536 | tf_op jit(solution)/shard_map/all_to_all | solution.py:414

commit v6 on v5

--- a/solution.py
+++ b/solution.py
@@ -15,6 +15,7 @@
 ND = 1
 BLADES = 36
 ROWS = 32
+QUADS = 7
 PITCH = ROWS + 1
 BLOCK = 16
 FULL = 32000.0
@@ -46,7 +47,9 @@
     wide[25 * pitch + 1 : 25 * pitch + planes, :] = wall[0 : planes - 1]
     wide[26 * pitch : 26 * pitch + planes - 1, :] = wall[1:planes]
     for i in range(planes):
-        send_ref[i] = wide[pl.ds(i, ROWS, stride=pitch), :].astype(BF16)
+        plane = wide[pl.ds(i, ROWS, stride=pitch), :].astype(BF16)
+        for m in range(QUADS):
+            send_ref[i, :, 128 * m : 128 * m + 128] = plane[4 * m : 4 * m + 4]
 
 
 def routing(owner_row, rank, values, first):
@@ -268,7 +271,9 @@
     rims = rims_beside(rim_ref, lax.axis_index("passage"), phase)
     width = u_ref.shape[1]
     for j in range(width):
-        wide[j * PITCH : j * PITCH + ROWS, :] = recv_ref[j].astype(F32)
+        for m in range(QUADS):
+            at = j * PITCH + 4 * m
+            wide[at : at + 4, :] = recv_ref[j, :, 128 * m : 128 * m + 128].astype(F32)
     for e in range(25):
         tiles_ref[e] = wide[pl.ds(e, width, stride=PITCH), :].astype(BF16)
     rim_out_ref[...] = jnp.zeros_like(rim_out_ref)
@@ -390,7 +395,7 @@
 
     (send,) = kernel_call(
         prep_kernel,
-        [((bricks, ROWS, depth), BF16)],
+        [((bricks, 4, QUADS * depth), BF16)],
         [pltpu.VMEM((ROWS * (bricks + 1), depth), F32)],
     )(jac)
     recv = lax.all_to_all(send, "brick", 0, 0, tiled=True)

time: 53.6 us -> 53 us (0.989)
  waiting for transfers between devices: 12.4 us -> 11.7 us
    ppermute x2, waiting for transfers between devices: 4.25 us -> 3.55 us  [swapped(): lax.ppermute(rim, 'passage', [(i, (i + 1) % passes) for i in range(passes)])]
where the time goes in v6:
time: 53 us; the launch traced here: 52.6 us
  starting transfers between devices  32.5 us (61%)
  waiting for transfers between devices  11.7 us (22%)
  Pallas kernels  6.02 us (11%)
  local copies, waits for them, and re-layouts  1.63 us (3%)
  between operations  0.8 us (2%)
    all_to_all x1, starting transfers between devices, body(): recv = lax.all_to_all(send, 'brick', 0, 0, tiled=True)  11.1 us
    all_to_all x1, starting transfers between devices, body(): arrived = lax.all_to_all(routed, 'brick', 0, 0, tiled=True)  10.4 us
    all_to_all x1, waiting for transfers between devices, body(): arrived = lax.all_to_all(routed, 'brick', 0, 0, tiled=True)  6.47 us
    ppermute x4, starting transfers between devices, planes_beside(): return (lax.ppermute(code, 'brick', near), lax.ppermute(code, 'brick', far))  5.9 us
    ppermute x2, starting transfers between devices, swapped(): lax.ppermute(rim, 'passage', [(i, (i + 1) % passes) for i in range(passes)])  5.06 us
    ppermute x2, waiting for transfers between devices, swapped(): lax.ppermute(rim, 'passage', [(i, (i + 1) % passes) for i in range(passes)])  3.55 us
    pallas_call x1, Pallas kernels, body(): kernel_call(functools.partial(first_kernel, phase), [(field, F32), ((25,...  1.67 us
    unnamed x18, local copies, waits for them, and re-layouts  1.63 us
  transfers between devices with their start and end apart: 8, of which 4 were waited for; matrix products, arithmetic and copies ran while one was open for 0% of the time, Pallas kernels for 4%

profile of v6, /device:TPU:1, one launch (start us, length us, event | category | flops | bytes accessed | tf_op | source)
XLA Modules:
  0.0 52.6 jit_solution(10351696430933137117)
XLA Ops:
  0.6 1.0 %copy-done.2 = bf16[1,25,64,128]{3,2,1,0:T(8,128)(2,1)S(1)} copy-done((bf16[1,25,64,128]{3,2,1,0:T(8,128)(2,1)S(1)}, bf16[1,25,64,128]{3,2,1,0:T(8,128)(2,1)}, u32[]{:S(2)}) %copy-start.2) | copy-done | bytes 409624
  1.6 1.1 %shard_map.104 = bf16[64,4,896]{2,1,0:T(4,128)(2,1)} custom-call(bf16[25,64,128]{2,1,0:T(8,128)(2,1)S(1)} %bitcast.17), custom_call_target="tpu_custom_call" | custom-call | tf_op jit(solution)/shard_map/pallas_call | solution.py:396
  2.7 0.0 copy-start.5
  2.7 11.1 %all-to-all-start = ((bf16[64,4,896]{2,1,0:T(4,128)(2,1)}), bf16[64,4,896]{2,1,0:T(4,128)(2,1)S(1)}, u32[]{:S(2)}, u32[]{:S(2)}) async-start(bf16[64,4,896]{2,1,0:T(4,128)(2,1)} %shard_map.104), calls=%async_computation | async-start | bytes 917504 | tf_op jit(solution)/shard_map/all_to_all | solution.py:401
  13.8 0.0 copy-start.6
  13.8 0.0 copy-start.7
  13.8 0.0 copy-start.8
  13.9 0.6 %copy-done.6 = f32[1,3,1,64]{3,2,1,0:T(1,128)S(1)} copy-done((f32[1,3,1,64]{3,2,1,0:T(1,128)S(1)}, f32[1,3,1,64]{3,2,1,0:T(1,128)}, u32[]{:S(2)}) %copy-start.6) | copy-done | bytes 792
  14.5 0.4 shard_map.105
  14.9 3.5 %collective-permute-start.1 = (s16[720,128]{1,0:T(8,128)(2,1)S(1)}, s16[720,128]{1,0:T(8,128)(2,1)S(1)}, u32[]{:S(2)}, u32[]{:S(2)}) collective-permute-start(s16[720,128]{1,0:T(8,128)(2,1)S(1)} %get-tuple-element.14), channel_id=1, source_target_pairs={{1,2},{2,1},{3,4},{4,3},{5,6},{6,5},{7,8},{8,7},{9,10},{10,9},{11,... | collective-permute-start | bytes 552968 | tf_op jit(solution)/shard_map/ppermute | solution.py:365
  18.4 0.1 collective-permute-start
  18.5 2.5 %collective-permute-start.2 = (f32[2,16,128]{2,1,0:T(8,128)S(1)}, f32[2,16,128]{2,1,0:T(8,128)S(1)}, u32[]{:S(2)}, u32[]{:S(2)}) collective-permute-start(f32[2,16,128]{2,1,0:T(8,128)S(1)} %get-tuple-element.15), channel_id=1, source_target_pairs={{0,64},{64,0},{1,65},{65,1},{2,66},{66,2},{3,67},{67,3},{4,68},{68... | collective-permute-start | bytes 49160 | tf_op jit(solution)/shard_map/ppermute | solution.py:369
  21.0 3.5 %collective-permute-done.2.rim_ref = f32[2,16,128]{2,1,0:T(8,128)S(1)} collective-permute-done((f32[2,16,128]{2,1,0:T(8,128)S(1)}, f32[2,16,128]{2,1,0:T(8,128)S(1)}, u32[]{:S(2)}, u32[]{:S(2)}) %collective-permute-start.2) | collective-permute-done | bytes 16416 | tf_op jit(solution)/shard_map/ppermute | solution.py:369
  24.6 0.7 %collective-permute-done.1.far_ref = s16[720,128]{1,0:T(8,128)(2,1)S(1)} collective-permute-done((s16[720,128]{1,0:T(8,128)(2,1)S(1)}, s16[720,128]{1,0:T(8,128)(2,1)S(1)}, u32[]{:S(2)}, u32[]{:S(2)}) %collective-permute-start.1) | collective-permute-done | bytes 184352 | tf_op jit(solution)/shard_map/ppermute | solution.py:365
  25.3 1.0 %all-to-all-done.recv_ref = bf16[64,4,896]{2,1,0:T(4,128)(2,1)S(1)} async-done(((bf16[64,4,896]{2,1,0:T(4,128)(2,1)}), bf16[64,4,896]{2,1,0:T(4,128)(2,1)S(1)}, u32[]{:S(2)}, u32[]{:S(2)}) %all-to-all-start) | async-done | bytes 458784 | tf_op jit(solution)/shard_map/all_to_all | solution.py:401
  26.3 1.7 %shard_map.106 = (f32[10,64,128]{2,1,0:T(8,128)S(1)}, bf16[25,64,128]{2,1,0:T(8,128)(2,1)S(1)}, f32[2,16,128]{2,1,0:T(8,128)S(1)}, s16[656,128]{1,0:T(8,128)(2,1)S(1)}, f32[64,128]{1,0:T(8,128)S(1)}) custom-call(bf16[64,4,896]{2,1,0:T(4,128)(2,1)S(1)} %all-to-all-done.recv_ref, f32[10,64,128]{2,1,0:T(8,128)S(1)} %bitcast.16, ...), custom_call_target="tpu_custom_call" | custom-call | tf_op jit(solution)/shard_map/pallas_call | solution.py:409
  28.0 2.5 %collective-permute-start.5 = (f32[2,16,128]{2,1,0:T(8,128)S(1)}, f32[2,16,128]{2,1,0:T(8,128)S(1)}, u32[]{:S(2)}, u32[]{:S(2)}) collective-permute-start(f32[2,16,128]{2,1,0:T(8,128)S(1)} %get-tuple-element.22), channel_id=1, source_target_pairs={{0,64},{64,0},{1,65},{65,1},{2,66},{66,2},{3,67},{67,3},{4,68},{68... | collective-permute-start | bytes 49160 | tf_op jit(solution)/shard_map/ppermute | solution.py:369
  30.5 2.2 %collective-permute-start.4 = (s16[656,128]{1,0:T(8,128)(2,1)S(1)}, s16[656,128]{1,0:T(8,128)(2,1)S(1)}, u32[]{:S(2)}, u32[]{:S(2)}) collective-permute-start(s16[656,128]{1,0:T(8,128)(2,1)S(1)} %get-tuple-element.21), channel_id=1, source_target_pairs={{1,2},{2,1},{3,4},{4,3},{5,6},{6,5},{7,8},{8,7},{9,10},{10,9},{11,... | collective-permute-start | bytes 503816 | tf_op jit(solution)/shard_map/ppermute | solution.py:365
  32.7 0.1 collective-permute-start.3
  32.8 0.7 %shard_map.108 = f32[64,1,128]{2,1,0:T(1,128)} custom-call(f32[64,128]{1,0:T(8,128)S(1)} %get-tuple-element.24.sum_ref, f32[2,16,128]{2,1,0:T(8,128)S(1)} %collective-permute-done.5.rim_ref, f32[4,64,128]{2,1,0:T(8,128)S(1)} %get-tuple-element.16.fields_ref, f32[64,128]{1,0:T(8,128)S(1)} %get-tuple-element.17.weight_ref, ...), custom_call_target="tpu_custom_call" | custom-call | flops 17179869184 | tf_op jit(solution)/shard_map/pallas_call | solution.py:416
  33.5 10.4 %all-to-all-start.1 = ((f32[64,1,128]{2,1,0:T(1,128)}), f32[64,1,128]{2,1,0:T(1,128)S(1)}, u32[]{:S(2)}, u32[]{:S(2)}) async-start(f32[64,1,128]{2,1,0:T(1,128)} %shard_map.108), calls=%async_computation.1 | async-start | bytes 65536 | tf_op jit(solution)/shard_map/all_to_all | solution.py:419
  44.0 1.2 %shard_map.107 = (f32[10,64,128]{2,1,0:T(8,128)}, f32[8,128]{1,0:T(8,128)S(1)}) custom-call(bf16[25,64,128]{2,1,0:T(8,128)(2,1)S(1)} %get-tuple-element.19.tiles_ref, f32[10,64,128]{2,1,0:T(8,128)S(1)} %get-tuple-element.20.u_ref, s16[656,128]{1,0:T(8,128)(2,1)S(1)} %collective-permute-done.3.near_ref, s16[656,128]{1,0:T(8,128)(2,1)S(1)} %collective-permute-done.4.far_ref, ...), custom_call_target="tpu_custom_call" | custom-call | tf_op jit(solution)/shard_map/pallas_call | solution.py:421
  45.2 6.5 %all-to-all-done.1.recv_ref = f32[64,1,128]{2,1,0:T(1,128)S(1)} async-done(((f32[64,1,128]{2,1,0:T(1,128)}), f32[64,1,128]{2,1,0:T(1,128)S(1)}, u32[]{:S(2)}, u32[]{:S(2)}) %all-to-all-start.1) | async-done | bytes 32800 | tf_op jit(solution)/shard_map/all_to_all | solution.py:419
  51.7 1.0 %shard_map.109 = f32[6,1,256]{2,1,0:T(1,128)} custom-call(f32[64,1,128]{2,1,0:T(1,128)S(1)} %all-to-all-done.1.recv_ref, f32[8,128]{1,0:T(8,128)S(1)} %get-tuple-element.25.after_ref), custom_call_target="tpu_custom_call" | custom-call | tf_op jit(solution)/shard_map/pallas_call | solution.py:424
  (16 shorter events, 0.0 us)
Async XLA Ops:
  0.6 1.0 %copy-start.2 = (bf16[1,25,64,128]{3,2,1,0:T(8,128)(2,1)S(1)}, bf16[1,25,64,128]{3,2,1,0:T(8,128)(2,1)}, u32[]{:S(2)}) copy-start(bf16[1,25,64,128]{3,2,1,0:T(8,128)(2,1)} %param.9) | copy-start | bytes 1228804
  2.7 11.1 %copy-start = (f32[1,10,1,64,128]{4,3,2,1,0:T(8,128)S(1)}, f32[1,10,1,64,128]{4,3,2,1,0:T(8,128)}, u32[]{:S(2)}) copy-start(f32[1,10,1,64,128]{4,3,2,1,0:T(8,128)} %param.11) | copy-start | bytes 983044
  2.7 11.2 %copy-start.1 = (f32[1,10,1,64,128]{4,3,2,1,0:T(8,128)S(1)}, f32[1,10,1,64,128]{4,3,2,1,0:T(8,128)}, u32[]{:S(2)}) copy-start(f32[1,10,1,64,128]{4,3,2,1,0:T(8,128)} %param.10) | copy-start | bytes 983044
  2.7 11.2 %copy-start.3 = (f32[1,1,64,128]{3,2,1,0:T(8,128)S(1)}, f32[1,1,64,128]{3,2,1,0:T(8,128)}, u32[]{:S(2)}) copy-start(f32[1,1,64,128]{3,2,1,0:T(8,128)} %param.12) | copy-start | bytes 98308
  2.7 11.2 %copy-start.4 = (f32[1,1,64,128]{3,2,1,0:T(8,128)S(1)}, f32[1,1,64,128]{3,2,1,0:T(8,128)}, u32[]{:S(2)}) copy-start(f32[1,1,64,128]{3,2,1,0:T(8,128)} %param.13) | copy-start | bytes 98308
  2.7 11.2 %copy-start.5 = (f32[1,1,64,128]{3,2,1,0:T(8,128)S(1)}, f32[1,1,64,128]{3,2,1,0:T(8,128)}, u32[]{:S(2)}) copy-start(f32[1,1,64,128]{3,2,1,0:T(8,128)} %param.14) | copy-start | bytes 98308
  2.7 23.6 %all-to-all-start = ((bf16[64,4,896]{2,1,0:T(4,128)(2,1)}), bf16[64,4,896]{2,1,0:T(4,128)(2,1)S(1)}, u32[]{:S(2)}, u32[]{:S(2)}) async-start(bf16[64,4,896]{2,1,0:T(4,128)(2,1)} %shard_map.104), calls=%async_computation | async-start | bytes 917504 | tf_op jit(solution)/shard_map/all_to_all | solution.py:401
  13.8 0.7 %copy-start.6 = (f32[1,3,1,64]{3,2,1,0:T(1,128)S(1)}, f32[1,3,1,64]{3,2,1,0:T(1,128)}, u32[]{:S(2)}) copy-start(f32[1,3,1,64]{3,2,1,0:T(1,128)} %param.15) | copy-start | bytes 2308
  13.8 0.7 %copy-start.7 = (s32[1,64,1]{1,2,0:T(1,128)S(1)}, s32[1,64,1]{1,2,0:T(1,128)}, u32[]{:S(2)}) copy-start(s32[1,64,1]{1,2,0:T(1,128)} %param.16) | copy-start | bytes 772
  13.8 0.7 %copy-start.8 = (s32[1,64]{1,0:T(1,128)S(1)}, s32[1,64]{1,0:T(1,128)}, u32[]{:S(2)}) copy-start(s32[1,64]{1,0:T(1,128)} %slot_ref.1) | copy-start | bytes 772
  14.9 10.4 %collective-permute-start.1 = (s16[720,128]{1,0:T(8,128)(2,1)S(1)}, s16[720,128]{1,0:T(8,128)(2,1)S(1)}, u32[]{:S(2)}, u32[]{:S(2)}) collective-permute-start(s16[720,128]{1,0:T(8,128)(2,1)S(1)} %get-tuple-element.14), channel_id=1, source_target_pairs={{1,2},{2,1},{3,4},{4,3},{5,6},{6,5},{7,8},{8,7},{9,10},{10,9},{11,... | collective-permute-start | bytes 552968 | tf_op jit(solution)/shard_map/ppermute | solution.py:365
  18.4 6.9 %collective-permute-start = (s16[720,128]{1,0:T(8,128)(2,1)S(1)}, s16[720,128]{1,0:T(8,128)(2,1)S(1)}, u32[]{:S(2)}, u32[]{:S(2)}) collective-permute-start(s16[720,128]{1,0:T(8,128)(2,1)S(1)} %get-tuple-element.14), channel_id=1, source_target_pairs={{0,1},{1,0},{2,3},{3,2},{4,5},{5,4},{6,7},{7,6},{8,9},{9,8},{10,11... | collective-permute-start | bytes 552968 | tf_op jit(solution)/shard_map/ppermute | solution.py:365
  18.5 6.1 %collective-permute-start.2 = (f32[2,16,128]{2,1,0:T(8,128)S(1)}, f32[2,16,128]{2,1,0:T(8,128)S(1)}, u32[]{:S(2)}, u32[]{:S(2)}) collective-permute-start(f32[2,16,128]{2,1,0:T(8,128)S(1)} %get-tuple-element.15), channel_id=1, source_target_pairs={{0,64},{64,0},{1,65},{65,1},{2,66},{66,2},{3,67},{67,3},{4,68},{68... | collective-permute-start | bytes 49160 | tf_op jit(solution)/shard_map/ppermute | solution.py:369
  28.0 4.8 %collective-permute-start.5 = (f32[2,16,128]{2,1,0:T(8,128)S(1)}, f32[2,16,128]{2,1,0:T(8,128)S(1)}, u32[]{:S(2)}, u32[]{:S(2)}) collective-permute-start(f32[2,16,128]{2,1,0:T(8,128)S(1)} %get-tuple-element.22), channel_id=1, source_target_pairs={{0,64},{64,0},{1,65},{65,1},{2,66},{66,2},{3,67},{67,3},{4,68},{68... | collective-permute-start | bytes 49160 | tf_op jit(solution)/shard_map/ppermute | solution.py:369
  30.5 13.4 %collective-permute-start.4 = (s16[656,128]{1,0:T(8,128)(2,1)S(1)}, s16[656,128]{1,0:T(8,128)(2,1)S(1)}, u32[]{:S(2)}, u32[]{:S(2)}) collective-permute-start(s16[656,128]{1,0:T(8,128)(2,1)S(1)} %get-tuple-element.21), channel_id=1, source_target_pairs={{1,2},{2,1},{3,4},{4,3},{5,6},{6,5},{7,8},{8,7},{9,10},{10,9},{11,... | collective-permute-start | bytes 503816 | tf_op jit(solution)/shard_map/ppermute | solution.py:365
  32.7 11.3 %collective-permute-start.3 = (s16[656,128]{1,0:T(8,128)(2,1)S(1)}, s16[656,128]{1,0:T(8,128)(2,1)S(1)}, u32[]{:S(2)}, u32[]{:S(2)}) collective-permute-start(s16[656,128]{1,0:T(8,128)(2,1)S(1)} %get-tuple-element.21), channel_id=1, source_target_pairs={{0,1},{1,0},{2,3},{3,2},{4,5},{5,4},{6,7},{7,6},{8,9},{9,8},{10,11... | collective-permute-start | bytes 503816 | tf_op jit(solution)/shard_map/ppermute | solution.py:365
  33.5 18.2 %all-to-all-start.1 = ((f32[64,1,128]{2,1,0:T(1,128)}), f32[64,1,128]{2,1,0:T(1,128)S(1)}, u32[]{:S(2)}, u32[]{:S(2)}) async-start(f32[64,1,128]{2,1,0:T(1,128)} %shard_map.108), calls=%async_computation.1 | async-start | bytes 65536 | tf_op jit(solution)/shard_map/all_to_all | solution.py:419

commit v7 on v6

--- a/solution.py
+++ b/solution.py
@@ -110,7 +110,9 @@
 def routing_beside(ref, width, first):
     last = 10 * width + 16
     exponent = ref[last - 16 : last, :].astype(jnp.int32).astype(F32)[15:16, :]
-    code = ref[last:, :].astype(jnp.int32).astype(F32)
+    packed = ref[last:, :].astype(jnp.int32).astype(F32)[0:8]
+    code = [pltpu.roll(packed, 128 - 16 * g, axis=1) if g else packed for g in range(width // 8)]
+    code = jnp.concatenate(code, axis=0)
     low = pltpu.roll(code, 120, axis=1)
     info = (code + low * (1.0 / FULL)) * (jnp.exp2(exponent) * (1.0 / FULL))
     column = [info[:, k : k + 1] for k in range(7)]
@@ -144,7 +146,10 @@
         low = jnp.round((value - high) * FULL)
         lane = lanes((width, 128))
         both = jnp.where(lane < 8, high, jnp.where(lane < 16, pltpu.roll(low, 8, axis=1), 0.0))
-        code_ref[10 * width + 16 :, :] = short(both)
+        packed = both[0:8]
+        for g in range(1, width // 8):
+            packed = packed + pltpu.roll(both[8 * g : 8 * g + 8], 16 * g, axis=1)
+        code_ref[10 * width + 16 :, :] = short(jnp.concatenate([packed, jnp.zeros((8, 128), F32)], axis=0))
     code_ref[10 * width : 10 * width + 16, :] = short(exponents)
 
 
@@ -402,7 +407,7 @@
     face = (width, 128)
     rims, weight, route, code, fields = kernel_call(
         aux_kernel,
-        [(rim, F32), (face, F32), ((bricks, width), F32), ((plane[0] + width, depth), I16), ((4, *face), F32)],
+        [(rim, F32), (face, F32), ((bricks, width), F32), ((plane[0] + 16, depth), I16), ((4, *face), F32)],
     )(psi, source, *scalars, face_owner.reshape(1, width), face_slot, normals.reshape(3, 1, width))
     rims = swapped(rims, passes)
     near, far = planes_beside(code, bricks)

time: 53 us -> 52.8 us (level)
  transfers between devices with their start and end apart: 8 -> 8, of which waited for: 4 -> 4; matrix products, arithmetic and copies ran while one was open for 0% -> 0% of each run, Pallas kernels for 4% -> 5%
where the time goes in v7:
time: 52.8 us; the launch traced here: 52.5 us
  starting transfers between devices  32.2 us (61%)
  waiting for transfers between devices  11.6 us (22%)
  Pallas kernels  6.21 us (12%)
  local copies, waits for them, and re-layouts  1.63 us (3%)
  between operations  0.79 us (1%)
    all_to_all x1, starting transfers between devices, body(): recv = lax.all_to_all(send, 'brick', 0, 0, tiled=True)  11.1 us
    all_to_all x1, starting transfers between devices, body(): arrived = lax.all_to_all(routed, 'brick', 0, 0, tiled=True)  10.4 us
    all_to_all x1, waiting for transfers between devices, body(): arrived = lax.all_to_all(routed, 'brick', 0, 0, tiled=True)  6.47 us
    ppermute x4, starting transfers between devices, planes_beside(): return (lax.ppermute(code, 'brick', near), lax.ppermute(code, 'brick', far))  5.63 us
    ppermute x2, starting transfers between devices, swapped(): lax.ppermute(rim, 'passage', [(i, (i + 1) % passes) for i in range(passes)])  5.06 us
    ppermute x2, waiting for transfers between devices, swapped(): lax.ppermute(rim, 'passage', [(i, (i + 1) % passes) for i in range(passes)])  3.31 us
    pallas_call x1, Pallas kernels, body(): kernel_call(functools.partial(first_kernel, phase), [(field, F32), ((25,...  1.75 us
    unnamed x18, local copies, waits for them, and re-layouts  1.63 us
  transfers between devices with their start and end apart: 8, of which 4 were waited for; matrix products, arithmetic and copies ran while one was open for 0% of the time, Pallas kernels for 5%

profile of v7, /device:TPU:1, one launch (start us, length us, event | category | flops | bytes accessed | tf_op | source)
XLA Modules:
  0.0 52.5 jit_solution(11209818224430414066)
XLA Ops:
  0.6 1.0 %copy-done.2 = bf16[1,25,64,128]{3,2,1,0:T(8,128)(2,1)S(1)} copy-done((bf16[1,25,64,128]{3,2,1,0:T(8,128)(2,1)S(1)}, bf16[1,25,64,128]{3,2,1,0:T(8,128)(2,1)}, u32[]{:S(2)}) %copy-start.2) | copy-done | bytes 409624
  1.6 1.1 %shard_map.104 = bf16[64,4,896]{2,1,0:T(4,128)(2,1)} custom-call(bf16[25,64,128]{2,1,0:T(8,128)(2,1)S(1)} %bitcast.17), custom_call_target="tpu_custom_call" | custom-call | tf_op jit(solution)/shard_map/pallas_call | solution.py:401
  2.7 0.0 copy-start.5
  2.7 11.1 %all-to-all-start = ((bf16[64,4,896]{2,1,0:T(4,128)(2,1)}), bf16[64,4,896]{2,1,0:T(4,128)(2,1)S(1)}, u32[]{:S(2)}, u32[]{:S(2)}) async-start(bf16[64,4,896]{2,1,0:T(4,128)(2,1)} %shard_map.104), calls=%async_computation | async-start | bytes 917504 | tf_op jit(solution)/shard_map/all_to_all | solution.py:406
  13.8 0.0 copy-start.6
  13.8 0.0 copy-start.7
  13.8 0.0 copy-start.8
  13.9 0.6 %copy-done.6 = f32[1,3,1,64]{3,2,1,0:T(1,128)S(1)} copy-done((f32[1,3,1,64]{3,2,1,0:T(1,128)S(1)}, f32[1,3,1,64]{3,2,1,0:T(1,128)}, u32[]{:S(2)}) %copy-start.6) | copy-done | bytes 792
  14.5 0.5 shard_map.105
  15.0 3.5 %collective-permute-start.1 = (s16[672,128]{1,0:T(8,128)(2,1)S(1)}, s16[672,128]{1,0:T(8,128)(2,1)S(1)}, u32[]{:S(2)}, u32[]{:S(2)}) collective-permute-start(s16[672,128]{1,0:T(8,128)(2,1)S(1)} %get-tuple-element.14), channel_id=1, source_target_pairs={{1,2},{2,1},{3,4},{4,3},{5,6},{6,5},{7,8},{8,7},{9,10},{10,9},{11,... | collective-permute-start | bytes 516104 | tf_op jit(solution)/shard_map/ppermute | solution.py:370
  18.5 0.1 collective-permute-start
  18.6 2.5 %collective-permute-start.2 = (f32[2,16,128]{2,1,0:T(8,128)S(1)}, f32[2,16,128]{2,1,0:T(8,128)S(1)}, u32[]{:S(2)}, u32[]{:S(2)}) collective-permute-start(f32[2,16,128]{2,1,0:T(8,128)S(1)} %get-tuple-element.15), channel_id=1, source_target_pairs={{0,64},{64,0},{1,65},{65,1},{2,66},{66,2},{3,67},{67,3},{4,68},{68... | collective-permute-start | bytes 49160 | tf_op jit(solution)/shard_map/ppermute | solution.py:374
  21.1 3.3 %collective-permute-done.2.rim_ref = f32[2,16,128]{2,1,0:T(8,128)S(1)} collective-permute-done((f32[2,16,128]{2,1,0:T(8,128)S(1)}, f32[2,16,128]{2,1,0:T(8,128)S(1)}, u32[]{:S(2)}, u32[]{:S(2)}) %collective-permute-start.2) | collective-permute-done | bytes 16416 | tf_op jit(solution)/shard_map/ppermute | solution.py:374
  24.5 0.6 %collective-permute-done.1.far_ref = s16[672,128]{1,0:T(8,128)(2,1)S(1)} collective-permute-done((s16[672,128]{1,0:T(8,128)(2,1)S(1)}, s16[672,128]{1,0:T(8,128)(2,1)S(1)}, u32[]{:S(2)}, u32[]{:S(2)}) %collective-permute-start.1) | collective-permute-done | bytes 172064 | tf_op jit(solution)/shard_map/ppermute | solution.py:370
  25.1 1.2 %all-to-all-done.recv_ref = bf16[64,4,896]{2,1,0:T(4,128)(2,1)S(1)} async-done(((bf16[64,4,896]{2,1,0:T(4,128)(2,1)}), bf16[64,4,896]{2,1,0:T(4,128)(2,1)S(1)}, u32[]{:S(2)}, u32[]{:S(2)}) %all-to-all-start) | async-done | bytes 458784 | tf_op jit(solution)/shard_map/all_to_all | solution.py:406
  26.3 1.8 %shard_map.106 = (f32[10,64,128]{2,1,0:T(8,128)S(1)}, bf16[25,64,128]{2,1,0:T(8,128)(2,1)S(1)}, f32[2,16,128]{2,1,0:T(8,128)S(1)}, s16[656,128]{1,0:T(8,128)(2,1)S(1)}, f32[64,128]{1,0:T(8,128)S(1)}) custom-call(bf16[64,4,896]{2,1,0:T(4,128)(2,1)S(1)} %all-to-all-done.recv_ref, f32[10,64,128]{2,1,0:T(8,128)S(1)} %bitcast.16, ...), custom_call_target="tpu_custom_call" | custom-call | tf_op jit(solution)/shard_map/pallas_call | solution.py:414
  28.1 2.5 %collective-permute-start.5 = (f32[2,16,128]{2,1,0:T(8,128)S(1)}, f32[2,16,128]{2,1,0:T(8,128)S(1)}, u32[]{:S(2)}, u32[]{:S(2)}) collective-permute-start(f32[2,16,128]{2,1,0:T(8,128)S(1)} %get-tuple-element.22), channel_id=1, source_target_pairs={{0,64},{64,0},{1,65},{65,1},{2,66},{66,2},{3,67},{67,3},{4,68},{68... | collective-permute-start | bytes 49160 | tf_op jit(solution)/shard_map/ppermute | solution.py:374
  30.6 1.9 %collective-permute-start.4 = (s16[656,128]{1,0:T(8,128)(2,1)S(1)}, s16[656,128]{1,0:T(8,128)(2,1)S(1)}, u32[]{:S(2)}, u32[]{:S(2)}) collective-permute-start(s16[656,128]{1,0:T(8,128)(2,1)S(1)} %get-tuple-element.21), channel_id=1, source_target_pairs={{1,2},{2,1},{3,4},{4,3},{5,6},{6,5},{7,8},{8,7},{9,10},{10,9},{11,... | collective-permute-start | bytes 503816 | tf_op jit(solution)/shard_map/ppermute | solution.py:370
  32.5 0.1 collective-permute-start.3
  32.6 0.7 %shard_map.108 = f32[64,1,128]{2,1,0:T(1,128)} custom-call(f32[64,128]{1,0:T(8,128)S(1)} %get-tuple-element.24.sum_ref, f32[2,16,128]{2,1,0:T(8,128)S(1)} %collective-permute-done.5.rim_ref, f32[4,64,128]{2,1,0:T(8,128)S(1)} %get-tuple-element.16.fields_ref, f32[64,128]{1,0:T(8,128)S(1)} %get-tuple-element.17.weight_ref, ...), custom_call_target="tpu_custom_call" | custom-call | flops 17179869184 | tf_op jit(solution)/shard_map/pallas_call | solution.py:421
  33.3 10.4 %all-to-all-start.1 = ((f32[64,1,128]{2,1,0:T(1,128)}), f32[64,1,128]{2,1,0:T(1,128)S(1)}, u32[]{:S(2)}, u32[]{:S(2)}) async-start(f32[64,1,128]{2,1,0:T(1,128)} %shard_map.108), calls=%async_computation.1 | async-start | bytes 65536 | tf_op jit(solution)/shard_map/all_to_all | solution.py:424
  43.8 1.2 %shard_map.107 = (f32[10,64,128]{2,1,0:T(8,128)}, f32[8,128]{1,0:T(8,128)S(1)}) custom-call(bf16[25,64,128]{2,1,0:T(8,128)(2,1)S(1)} %get-tuple-element.19.tiles_ref, f32[10,64,128]{2,1,0:T(8,128)S(1)} %get-tuple-element.20.u_ref, s16[656,128]{1,0:T(8,128)(2,1)S(1)} %collective-permute-done.3.near_ref, s16[656,128]{1,0:T(8,128)(2,1)S(1)} %collective-permute-done.4.far_ref, ...), custom_call_target="tpu_custom_call" | custom-call | tf_op jit(solution)/shard_map/pallas_call | solution.py:426
  45.0 6.5 %all-to-all-done.1.recv_ref = f32[64,1,128]{2,1,0:T(1,128)S(1)} async-done(((f32[64,1,128]{2,1,0:T(1,128)}), f32[64,1,128]{2,1,0:T(1,128)S(1)}, u32[]{:S(2)}, u32[]{:S(2)}) %all-to-all-start.1) | async-done | bytes 32800 | tf_op jit(solution)/shard_map/all_to_all | solution.py:424
  51.5 1.0 %shard_map.109 = f32[6,1,256]{2,1,0:T(1,128)} custom-call(f32[64,1,128]{2,1,0:T(1,128)S(1)} %all-to-all-done.1.recv_ref, f32[8,128]{1,0:T(8,128)S(1)} %get-tuple-element.25.after_ref), custom_call_target="tpu_custom_call" | custom-call | tf_op jit(solution)/shard_map/pallas_call | solution.py:429
  (16 shorter events, 0.0 us)
Async XLA Ops:
  0.6 1.0 %copy-start.2 = (bf16[1,25,64,128]{3,2,1,0:T(8,128)(2,1)S(1)}, bf16[1,25,64,128]{3,2,1,0:T(8,128)(2,1)}, u32[]{:S(2)}) copy-start(bf16[1,25,64,128]{3,2,1,0:T(8,128)(2,1)} %param.9) | copy-start | bytes 1228804
  2.7 11.1 %copy-start = (f32[1,10,1,64,128]{4,3,2,1,0:T(8,128)S(1)}, f32[1,10,1,64,128]{4,3,2,1,0:T(8,128)}, u32[]{:S(2)}) copy-start(f32[1,10,1,64,128]{4,3,2,1,0:T(8,128)} %param.11) | copy-start | bytes 983044
  2.7 11.2 %copy-start.1 = (f32[1,10,1,64,128]{4,3,2,1,0:T(8,128)S(1)}, f32[1,10,1,64,128]{4,3,2,1,0:T(8,128)}, u32[]{:S(2)}) copy-start(f32[1,10,1,64,128]{4,3,2,1,0:T(8,128)} %param.10) | copy-start | bytes 983044
  2.7 11.2 %copy-start.3 = (f32[1,1,64,128]{3,2,1,0:T(8,128)S(1)}, f32[1,1,64,128]{3,2,1,0:T(8,128)}, u32[]{:S(2)}) copy-start(f32[1,1,64,128]{3,2,1,0:T(8,128)} %param.12) | copy-start | bytes 98308
  2.7 11.2 %copy-start.4 = (f32[1,1,64,128]{3,2,1,0:T(8,128)S(1)}, f32[1,1,64,128]{3,2,1,0:T(8,128)}, u32[]{:S(2)}) copy-start(f32[1,1,64,128]{3,2,1,0:T(8,128)} %param.13) | copy-start | bytes 98308
  2.7 11.2 %copy-start.5 = (f32[1,1,64,128]{3,2,1,0:T(8,128)S(1)}, f32[1,1,64,128]{3,2,1,0:T(8,128)}, u32[]{:S(2)}) copy-start(f32[1,1,64,128]{3,2,1,0:T(8,128)} %param.14) | copy-start | bytes 98308
  2.7 23.6 %all-to-all-start = ((bf16[64,4,896]{2,1,0:T(4,128)(2,1)}), bf16[64,4,896]{2,1,0:T(4,128)(2,1)S(1)}, u32[]{:S(2)}, u32[]{:S(2)}) async-start(bf16[64,4,896]{2,1,0:T(4,128)(2,1)} %shard_map.104), calls=%async_computation | async-start | bytes 917504 | tf_op jit(solution)/shard_map/all_to_all | solution.py:406
  13.8 0.7 %copy-start.6 = (f32[1,3,1,64]{3,2,1,0:T(1,128)S(1)}, f32[1,3,1,64]{3,2,1,0:T(1,128)}, u32[]{:S(2)}) copy-start(f32[1,3,1,64]{3,2,1,0:T(1,128)} %param.15) | copy-start | bytes 2308
  13.8 0.7 %copy-start.7 = (s32[1,64,1]{1,2,0:T(1,128)S(1)}, s32[1,64,1]{1,2,0:T(1,128)}, u32[]{:S(2)}) copy-start(s32[1,64,1]{1,2,0:T(1,128)} %param.16) | copy-start | bytes 772
  13.8 0.7 %copy-start.8 = (s32[1,64]{1,0:T(1,128)S(1)}, s32[1,64]{1,0:T(1,128)}, u32[]{:S(2)}) copy-start(s32[1,64]{1,0:T(1,128)} %slot_ref.1) | copy-start | bytes 772
  15.0 10.1 %collective-permute-start.1 = (s16[672,128]{1,0:T(8,128)(2,1)S(1)}, s16[672,128]{1,0:T(8,128)(2,1)S(1)}, u32[]{:S(2)}, u32[]{:S(2)}) collective-permute-start(s16[672,128]{1,0:T(8,128)(2,1)S(1)} %get-tuple-element.14), channel_id=1, source_target_pairs={{1,2},{2,1},{3,4},{4,3},{5,6},{6,5},{7,8},{8,7},{9,10},{10,9},{11,... | collective-permute-start | bytes 516104 | tf_op jit(solution)/shard_map/ppermute | solution.py:370
  18.5 6.5 %collective-permute-start = (s16[672,128]{1,0:T(8,128)(2,1)S(1)}, s16[672,128]{1,0:T(8,128)(2,1)S(1)}, u32[]{:S(2)}, u32[]{:S(2)}) collective-permute-start(s16[672,128]{1,0:T(8,128)(2,1)S(1)} %get-tuple-element.14), channel_id=1, source_target_pairs={{0,1},{1,0},{2,3},{3,2},{4,5},{5,4},{6,7},{7,6},{8,9},{9,8},{10,11... | collective-permute-start | bytes 516104 | tf_op jit(solution)/shard_map/ppermute | solution.py:370
  18.6 5.8 %collective-permute-start.2 = (f32[2,16,128]{2,1,0:T(8,128)S(1)}, f32[2,16,128]{2,1,0:T(8,128)S(1)}, u32[]{:S(2)}, u32[]{:S(2)}) collective-permute-start(f32[2,16,128]{2,1,0:T(8,128)S(1)} %get-tuple-element.15), channel_id=1, source_target_pairs={{0,64},{64,0},{1,65},{65,1},{2,66},{66,2},{3,67},{67,3},{4,68},{68... | collective-permute-start | bytes 49160 | tf_op jit(solution)/shard_map/ppermute | solution.py:374
  28.1 4.6 %collective-permute-start.5 = (f32[2,16,128]{2,1,0:T(8,128)S(1)}, f32[2,16,128]{2,1,0:T(8,128)S(1)}, u32[]{:S(2)}, u32[]{:S(2)}) collective-permute-start(f32[2,16,128]{2,1,0:T(8,128)S(1)} %get-tuple-element.22), channel_id=1, source_target_pairs={{0,64},{64,0},{1,65},{65,1},{2,66},{66,2},{3,67},{67,3},{4,68},{68... | collective-permute-start | bytes 49160 | tf_op jit(solution)/shard_map/ppermute | solution.py:374
  30.6 13.2 %collective-permute-start.4 = (s16[656,128]{1,0:T(8,128)(2,1)S(1)}, s16[656,128]{1,0:T(8,128)(2,1)S(1)}, u32[]{:S(2)}, u32[]{:S(2)}) collective-permute-start(s16[656,128]{1,0:T(8,128)(2,1)S(1)} %get-tuple-element.21), channel_id=1, source_target_pairs={{1,2},{2,1},{3,4},{4,3},{5,6},{6,5},{7,8},{8,7},{9,10},{10,9},{11,... | collective-permute-start | bytes 503816 | tf_op jit(solution)/shard_map/ppermute | solution.py:370
  32.5 11.3 %collective-permute-start.3 = (s16[656,128]{1,0:T(8,128)(2,1)S(1)}, s16[656,128]{1,0:T(8,128)(2,1)S(1)}, u32[]{:S(2)}, u32[]{:S(2)}) collective-permute-start(s16[656,128]{1,0:T(8,128)(2,1)S(1)} %get-tuple-element.21), channel_id=1, source_target_pairs={{0,1},{1,0},{2,3},{3,2},{4,5},{5,4},{6,7},{7,6},{8,9},{9,8},{10,11... | collective-permute-start | bytes 503816 | tf_op jit(solution)/shard_map/ppermute | solution.py:370
  33.3 18.2 %all-to-all-start.1 = ((f32[64,1,128]{2,1,0:T(1,128)}), f32[64,1,128]{2,1,0:T(1,128)S(1)}, u32[]{:S(2)}, u32[]{:S(2)}) async-start(f32[64,1,128]{2,1,0:T(1,128)} %shard_map.108), calls=%async_computation.1 | async-start | bytes 65536 | tf_op jit(solution)/shard_map/all_to_all | solution.py:424

commit v8 on v7

--- a/solution.py
+++ b/solution.py
@@ -269,18 +269,20 @@
     return routed
 
 
-def first_kernel(
-    phase, recv_ref, u_ref, near_ref, far_ref, rim_ref, source_ref, step_ref, diss_ref, freq_ref,
-    fields_ref, weight_ref, route_ref, out_ref, tiles_ref, rim_out_ref, code_ref, sum_ref, wide,
-):
-    rims = rims_beside(rim_ref, lax.axis_index("passage"), phase)
-    width = u_ref.shape[1]
+def widened(recv_ref, wide, width):
     for j in range(width):
         for m in range(QUADS):
             at = j * PITCH + 4 * m
             wide[at : at + 4, :] = recv_ref[j, :, 128 * m : 128 * m + 128].astype(F32)
-    for e in range(25):
-        tiles_ref[e] = wide[pl.ds(e, width, stride=PITCH), :].astype(BF16)
+
+
+def first_kernel(
+    phase, recv_ref, u_ref, near_ref, far_ref, rim_ref, source_ref, step_ref, diss_ref, freq_ref,
+    fields_ref, weight_ref, route_ref, out_ref, rim_out_ref, code_ref, sum_ref, wide,
+):
+    rims = rims_beside(rim_ref, lax.axis_index("passage"), phase)
+    width = u_ref.shape[1]
+    widened(recv_ref, wide, width)
     rim_out_ref[...] = jnp.zeros_like(rim_out_ref)
     blocks = width // BLOCK
     scales = code_scale(near_ref, width), code_scale(far_ref, width)
@@ -303,16 +305,18 @@
 
 
 def second_kernel(
-    phase, tiles_ref, u_ref, near_ref, far_ref, rim_ref, source_ref, step_ref, diss_ref, freq_ref, out_ref, after_ref
+    phase, recv_ref, u_ref, near_ref, far_ref, rim_ref, source_ref, step_ref, diss_ref, freq_ref, out_ref, after_ref,
+    wide,
 ):
     rims = rims_beside(rim_ref, lax.axis_index("passage"), phase)
     width = u_ref.shape[1]
+    widened(recv_ref, wide, width)
     blocks = width // BLOCK
     scales = code_scale(near_ref, width), code_scale(far_ref, width)
     for b in range(blocks):
         new = sweep_block(
             b, blocks, u_ref, near_ref, far_ref, scales, rims,
-            lambda e: tiles_ref[e, BLOCK * b : BLOCK * b + BLOCK, :].astype(F32),
+            lambda e: wide[pl.ds(BLOCK * b * PITCH + e, BLOCK, stride=PITCH), :],
             source_ref, step_ref, diss_ref, freq_ref,
         )
         for c in range(10):
@@ -411,9 +415,9 @@
     )(psi, source, *scalars, face_owner.reshape(1, width), face_slot, normals.reshape(3, 1, width))
     rims = swapped(rims, passes)
     near, far = planes_beside(code, bricks)
-    state, tiles, rims, code, terms = kernel_call(
+    state, rims, code, terms = kernel_call(
         functools.partial(first_kernel, phase),
-        [(field, F32), ((25, width, depth), BF16), (rim, F32), (plane, I16), (face, F32)],
+        [(field, F32), (rim, F32), (plane, I16), (face, F32)],
         [pltpu.VMEM((PITCH * width, depth), F32)],
     )(recv, psi, near, far, rims, source, *scalars, fields, weight, route)
 
@@ -423,8 +427,12 @@
     )
     arrived = lax.all_to_all(routed, "brick", 0, 0, tiled=True)
     near, far = planes_beside(code, bricks)
-    state, after = kernel_call(functools.partial(second_kernel, phase), [(field, F32), ((8, 128), F32)])(
-        tiles, state, near, far, rims, source, *scalars
+    state, after = kernel_call(
+        functools.partial(second_kernel, phase),
+        [(field, F32), ((8, 128), F32)],
+        [pltpu.VMEM((PITCH * width, depth), F32)],
+    )(
+        recv, state, near, far, rims, source, *scalars
     )
     (sensitivity,) = kernel_call(nodes_kernel, [((6, 1, NODE_DEV), F32)], [pltpu.VMEM((bricks, 128), F32)])(
         arrived, after

time: 52.8 us -> 52.7 us (level)
  no operation moved by 1% of the time
where the time goes in v8:
time: 52.7 us; the launch traced here: 52.4 us
  starting transfers between devices  32.2 us (61%)
  waiting for transfers between devices  11.6 us (22%)
  Pallas kernels  6.2 us (12%)
  local copies, waits for them, and re-layouts  1.63 us (3%)
  between operations  0.79 us (1%)
    all_to_all x1, starting transfers between devices, body(): recv = lax.all_to_all(send, 'brick', 0, 0, tiled=True)  11.1 us
    all_to_all x1, starting transfers between devices, body(): arrived = lax.all_to_all(routed, 'brick', 0, 0, tiled=True)  10.4 us
    all_to_all x1, waiting for transfers between devices, body(): arrived = lax.all_to_all(routed, 'brick', 0, 0, tiled=True)  6.43 us
    ppermute x4, starting transfers between devices, planes_beside(): return (lax.ppermute(code, 'brick', near), lax.ppermute(code, 'brick', far))  5.63 us
    ppermute x2, starting transfers between devices, swapped(): lax.ppermute(rim, 'passage', [(i, (i + 1) % passes) for i in range(passes)])  5.06 us
    ppermute x2, waiting for transfers between devices, swapped(): lax.ppermute(rim, 'passage', [(i, (i + 1) % passes) for i in range(passes)])  3.31 us
    pallas_call x1, Pallas kernels, body(): kernel_call(functools.partial(first_kernel, phase), [(field, F32), (rim,...  1.7 us
    unnamed x18, local copies, waits for them, and re-layouts  1.63 us
  transfers between devices with their start and end apart: 8, of which 4 were waited for; matrix products, arithmetic and copies ran while one was open for 0% of the time, Pallas kernels for 5%

profile of v8, /device:TPU:1, one launch (start us, length us, event | category | flops | bytes accessed | tf_op | source)
XLA Modules:
  0.0 52.4 jit_solution(3082174143940252526)
XLA Ops:
  0.6 1.0 %copy-done.2 = bf16[1,25,64,128]{3,2,1,0:T(8,128)(2,1)S(1)} copy-done((bf16[1,25,64,128]{3,2,1,0:T(8,128)(2,1)S(1)}, bf16[1,25,64,128]{3,2,1,0:T(8,128)(2,1)}, u32[]{:S(2)}) %copy-start.2) | copy-done | bytes 409624
  1.6 1.1 %shard_map.104 = bf16[64,4,896]{2,1,0:T(4,128)(2,1)} custom-call(bf16[25,64,128]{2,1,0:T(8,128)(2,1)S(1)} %bitcast.17), custom_call_target="tpu_custom_call" | custom-call | tf_op jit(solution)/shard_map/pallas_call | solution.py:405
  2.7 0.0 copy-start.5
  2.7 11.1 %all-to-all-start = ((bf16[64,4,896]{2,1,0:T(4,128)(2,1)}), bf16[64,4,896]{2,1,0:T(4,128)(2,1)S(1)}, u32[]{:S(2)}, u32[]{:S(2)}) async-start(bf16[64,4,896]{2,1,0:T(4,128)(2,1)} %shard_map.104), calls=%async_computation | async-start | bytes 917504 | tf_op jit(solution)/shard_map/all_to_all | solution.py:410
  13.8 0.0 copy-start.6
  13.8 0.0 copy-start.7
  13.8 0.0 copy-start.8
  13.9 0.6 %copy-done.6 = f32[1,3,1,64]{3,2,1,0:T(1,128)S(1)} copy-done((f32[1,3,1,64]{3,2,1,0:T(1,128)S(1)}, f32[1,3,1,64]{3,2,1,0:T(1,128)}, u32[]{:S(2)}) %copy-start.6) | copy-done | bytes 792
  14.5 0.5 shard_map.105
  15.0 3.5 %collective-permute-start.1 = (s16[672,128]{1,0:T(8,128)(2,1)S(1)}, s16[672,128]{1,0:T(8,128)(2,1)S(1)}, u32[]{:S(2)}, u32[]{:S(2)}) collective-permute-start(s16[672,128]{1,0:T(8,128)(2,1)S(1)} %get-tuple-element.13), channel_id=1, source_target_pairs={{1,2},{2,1},{3,4},{4,3},{5,6},{6,5},{7,8},{8,7},{9,10},{10,9},{11,... | collective-permute-start | bytes 516104 | tf_op jit(solution)/shard_map/ppermute | solution.py:374
  18.5 0.1 collective-permute-start
  18.6 2.5 %collective-permute-start.2 = (f32[2,16,128]{2,1,0:T(8,128)S(1)}, f32[2,16,128]{2,1,0:T(8,128)S(1)}, u32[]{:S(2)}, u32[]{:S(2)}) collective-permute-start(f32[2,16,128]{2,1,0:T(8,128)S(1)} %get-tuple-element.14), channel_id=1, source_target_pairs={{0,64},{64,0},{1,65},{65,1},{2,66},{66,2},{3,67},{67,3},{4,68},{68... | collective-permute-start | bytes 49160 | tf_op jit(solution)/shard_map/ppermute | solution.py:378
  21.1 3.3 %collective-permute-done.2.rim_ref = f32[2,16,128]{2,1,0:T(8,128)S(1)} collective-permute-done((f32[2,16,128]{2,1,0:T(8,128)S(1)}, f32[2,16,128]{2,1,0:T(8,128)S(1)}, u32[]{:S(2)}, u32[]{:S(2)}) %collective-permute-start.2) | collective-permute-done | bytes 16416 | tf_op jit(solution)/shard_map/ppermute | solution.py:378
  24.5 0.6 %collective-permute-done.1.far_ref = s16[672,128]{1,0:T(8,128)(2,1)S(1)} collective-permute-done((s16[672,128]{1,0:T(8,128)(2,1)S(1)}, s16[672,128]{1,0:T(8,128)(2,1)S(1)}, u32[]{:S(2)}, u32[]{:S(2)}) %collective-permute-start.1) | collective-permute-done | bytes 172064 | tf_op jit(solution)/shard_map/ppermute | solution.py:374
  25.1 1.2 %all-to-all-done.recv_ref = bf16[64,4,896]{2,1,0:T(4,128)(2,1)S(1)} async-done(((bf16[64,4,896]{2,1,0:T(4,128)(2,1)}), bf16[64,4,896]{2,1,0:T(4,128)(2,1)S(1)}, u32[]{:S(2)}, u32[]{:S(2)}) %all-to-all-start) | async-done | bytes 458784 | tf_op jit(solution)/shard_map/all_to_all | solution.py:410
  26.3 1.7 %shard_map.106 = (f32[10,64,128]{2,1,0:T(8,128)S(1)}, f32[2,16,128]{2,1,0:T(8,128)S(1)}, s16[656,128]{1,0:T(8,128)(2,1)S(1)}, f32[64,128]{1,0:T(8,128)S(1)}) custom-call(bf16[64,4,896]{2,1,0:T(4,128)(2,1)S(1)} %all-to-all-done.recv_ref, f32[10,64,128]{2,1,0:T(8,128)S(1)} %bitcast.16, s16[672,128]{1,0:T(8,128)(2,1)S(1)} %collective-permute-done.near_ref, ...), custom_call_target="tpu_custom_call" | custom-call | tf_op jit(solution)/shard_map/pallas_call | solution.py:418
  28.0 2.5 %collective-permute-start.5 = (f32[2,16,128]{2,1,0:T(8,128)S(1)}, f32[2,16,128]{2,1,0:T(8,128)S(1)}, u32[]{:S(2)}, u32[]{:S(2)}) collective-permute-start(f32[2,16,128]{2,1,0:T(8,128)S(1)} %get-tuple-element.20), channel_id=1, source_target_pairs={{0,64},{64,0},{1,65},{65,1},{2,66},{66,2},{3,67},{67,3},{4,68},{68... | collective-permute-start | bytes 49160 | tf_op jit(solution)/shard_map/ppermute | solution.py:378
  30.5 1.9 %collective-permute-start.4 = (s16[656,128]{1,0:T(8,128)(2,1)S(1)}, s16[656,128]{1,0:T(8,128)(2,1)S(1)}, u32[]{:S(2)}, u32[]{:S(2)}) collective-permute-start(s16[656,128]{1,0:T(8,128)(2,1)S(1)} %get-tuple-element.19), channel_id=1, source_target_pairs={{1,2},{2,1},{3,4},{4,3},{5,6},{6,5},{7,8},{8,7},{9,10},{10,9},{11,... | collective-permute-start | bytes 503816 | tf_op jit(solution)/shard_map/ppermute | solution.py:374
  32.5 0.1 collective-permute-start.3
  32.6 0.7 %shard_map.108 = f32[64,1,128]{2,1,0:T(1,128)} custom-call(f32[64,128]{1,0:T(8,128)S(1)} %get-tuple-element.22.sum_ref, f32[2,16,128]{2,1,0:T(8,128)S(1)} %collective-permute-done.5.rim_ref, f32[4,64,128]{2,1,0:T(8,128)S(1)} %get-tuple-element.15.fields_ref, f32[64,128]{1,0:T(8,128)S(1)} %get-tuple-element.16.weight_ref, ...), custom_call_target="tpu_custom_call" | custom-call | flops 17179869184 | tf_op jit(solution)/shard_map/pallas_call | solution.py:425
  33.3 10.4 %all-to-all-start.1 = ((f32[64,1,128]{2,1,0:T(1,128)}), f32[64,1,128]{2,1,0:T(1,128)S(1)}, u32[]{:S(2)}, u32[]{:S(2)}) async-start(f32[64,1,128]{2,1,0:T(1,128)} %shard_map.108), calls=%async_computation.1 | async-start | bytes 65536 | tf_op jit(solution)/shard_map/all_to_all | solution.py:428
  43.7 1.3 %shard_map.107 = (f32[10,64,128]{2,1,0:T(8,128)}, f32[8,128]{1,0:T(8,128)S(1)}) custom-call(bf16[64,4,896]{2,1,0:T(4,128)(2,1)S(1)} %all-to-all-done.recv_ref, f32[10,64,128]{2,1,0:T(8,128)S(1)} %get-tuple-element.18.u_ref, s16[656,128]{1,0:T(8,128)(2,1)S(1)} %collective-permute-done.3.near_ref, s16[656,128]{1,0:T(8,128)(2,1)S(1)} %collective-permute-done.4.far_ref, ...), custom_call_target="tpu_custom_call" | custom-call | tf_op jit(solution)/shard_map/pallas_call | solution.py:430
  45.0 6.4 %all-to-all-done.1.recv_ref = f32[64,1,128]{2,1,0:T(1,128)S(1)} async-done(((f32[64,1,128]{2,1,0:T(1,128)}), f32[64,1,128]{2,1,0:T(1,128)S(1)}, u32[]{:S(2)}, u32[]{:S(2)}) %all-to-all-start.1) | async-done | bytes 32800 | tf_op jit(solution)/shard_map/all_to_all | solution.py:428
  51.4 1.0 %shard_map.109 = f32[6,1,256]{2,1,0:T(1,128)} custom-call(f32[64,1,128]{2,1,0:T(1,128)S(1)} %all-to-all-done.1.recv_ref, f32[8,128]{1,0:T(8,128)S(1)} %get-tuple-element.23.after_ref), custom_call_target="tpu_custom_call" | custom-call | tf_op jit(solution)/shard_map/pallas_call | solution.py:437
  (16 shorter events, 0.0 us)
Async XLA Ops:
  0.6 1.0 %copy-start.2 = (bf16[1,25,64,128]{3,2,1,0:T(8,128)(2,1)S(1)}, bf16[1,25,64,128]{3,2,1,0:T(8,128)(2,1)}, u32[]{:S(2)}) copy-start(bf16[1,25,64,128]{3,2,1,0:T(8,128)(2,1)} %param.9) | copy-start | bytes 1228804
  2.7 11.1 %copy-start = (f32[1,10,1,64,128]{4,3,2,1,0:T(8,128)S(1)}, f32[1,10,1,64,128]{4,3,2,1,0:T(8,128)}, u32[]{:S(2)}) copy-start(f32[1,10,1,64,128]{4,3,2,1,0:T(8,128)} %param.11) | copy-start | bytes 983044
  2.7 11.2 %copy-start.1 = (f32[1,10,1,64,128]{4,3,2,1,0:T(8,128)S(1)}, f32[1,10,1,64,128]{4,3,2,1,0:T(8,128)}, u32[]{:S(2)}) copy-start(f32[1,10,1,64,128]{4,3,2,1,0:T(8,128)} %param.10) | copy-start | bytes 983044
  2.7 11.2 %copy-start.3 = (f32[1,1,64,128]{3,2,1,0:T(8,128)S(1)}, f32[1,1,64,128]{3,2,1,0:T(8,128)}, u32[]{:S(2)}) copy-start(f32[1,1,64,128]{3,2,1,0:T(8,128)} %param.12) | copy-start | bytes 98308
  2.7 11.2 %copy-start.4 = (f32[1,1,64,128]{3,2,1,0:T(8,128)S(1)}, f32[1,1,64,128]{3,2,1,0:T(8,128)}, u32[]{:S(2)}) copy-start(f32[1,1,64,128]{3,2,1,0:T(8,128)} %param.13) | copy-start | bytes 98308
  2.7 11.2 %copy-start.5 = (f32[1,1,64,128]{3,2,1,0:T(8,128)S(1)}, f32[1,1,64,128]{3,2,1,0:T(8,128)}, u32[]{:S(2)}) copy-start(f32[1,1,64,128]{3,2,1,0:T(8,128)} %param.14) | copy-start | bytes 98308
  2.7 23.6 %all-to-all-start = ((bf16[64,4,896]{2,1,0:T(4,128)(2,1)}), bf16[64,4,896]{2,1,0:T(4,128)(2,1)S(1)}, u32[]{:S(2)}, u32[]{:S(2)}) async-start(bf16[64,4,896]{2,1,0:T(4,128)(2,1)} %shard_map.104), calls=%async_computation | async-start | bytes 917504 | tf_op jit(solution)/shard_map/all_to_all | solution.py:410
  13.8 0.7 %copy-start.6 = (f32[1,3,1,64]{3,2,1,0:T(1,128)S(1)}, f32[1,3,1,64]{3,2,1,0:T(1,128)}, u32[]{:S(2)}) copy-start(f32[1,3,1,64]{3,2,1,0:T(1,128)} %param.15) | copy-start | bytes 2308
  13.8 0.7 %copy-start.7 = (s32[1,64,1]{1,2,0:T(1,128)S(1)}, s32[1,64,1]{1,2,0:T(1,128)}, u32[]{:S(2)}) copy-start(s32[1,64,1]{1,2,0:T(1,128)} %param.16) | copy-start | bytes 772
  13.8 0.7 %copy-start.8 = (s32[1,64]{1,0:T(1,128)S(1)}, s32[1,64]{1,0:T(1,128)}, u32[]{:S(2)}) copy-start(s32[1,64]{1,0:T(1,128)} %slot_ref.1) | copy-start | bytes 772
  15.0 10.1 %collective-permute-start.1 = (s16[672,128]{1,0:T(8,128)(2,1)S(1)}, s16[672,128]{1,0:T(8,128)(2,1)S(1)}, u32[]{:S(2)}, u32[]{:S(2)}) collective-permute-start(s16[672,128]{1,0:T(8,128)(2,1)S(1)} %get-tuple-element.13), channel_id=1, source_target_pairs={{1,2},{2,1},{3,4},{4,3},{5,6},{6,5},{7,8},{8,7},{9,10},{10,9},{11,... | collective-permute-start | bytes 516104 | tf_op jit(solution)/shard_map/ppermute | solution.py:374
  18.5 6.5 %collective-permute-start = (s16[672,128]{1,0:T(8,128)(2,1)S(1)}, s16[672,128]{1,0:T(8,128)(2,1)S(1)}, u32[]{:S(2)}, u32[]{:S(2)}) collective-permute-start(s16[672,128]{1,0:T(8,128)(2,1)S(1)} %get-tuple-element.13), channel_id=1, source_target_pairs={{0,1},{1,0},{2,3},{3,2},{4,5},{5,4},{6,7},{7,6},{8,9},{9,8},{10,11... | collective-permute-start | bytes 516104 | tf_op jit(solution)/shard_map/ppermute | solution.py:374
  18.6 5.8 %collective-permute-start.2 = (f32[2,16,128]{2,1,0:T(8,128)S(1)}, f32[2,16,128]{2,1,0:T(8,128)S(1)}, u32[]{:S(2)}, u32[]{:S(2)}) collective-permute-start(f32[2,16,128]{2,1,0:T(8,128)S(1)} %get-tuple-element.14), channel_id=1, source_target_pairs={{0,64},{64,0},{1,65},{65,1},{2,66},{66,2},{3,67},{67,3},{4,68},{68... | collective-permute-start | bytes 49160 | tf_op jit(solution)/shard_map/ppermute | solution.py:378
  28.0 4.6 %collective-permute-start.5 = (f32[2,16,128]{2,1,0:T(8,128)S(1)}, f32[2,16,128]{2,1,0:T(8,128)S(1)}, u32[]{:S(2)}, u32[]{:S(2)}) collective-permute-start(f32[2,16,128]{2,1,0:T(8,128)S(1)} %get-tuple-element.20), channel_id=1, source_target_pairs={{0,64},{64,0},{1,65},{65,1},{2,66},{66,2},{3,67},{67,3},{4,68},{68... | collective-permute-start | bytes 49160 | tf_op jit(solution)/shard_map/ppermute | solution.py:378
  30.5 13.2 %collective-permute-start.4 = (s16[656,128]{1,0:T(8,128)(2,1)S(1)}, s16[656,128]{1,0:T(8,128)(2,1)S(1)}, u32[]{:S(2)}, u32[]{:S(2)}) collective-permute-start(s16[656,128]{1,0:T(8,128)(2,1)S(1)} %get-tuple-element.19), channel_id=1, source_target_pairs={{1,2},{2,1},{3,4},{4,3},{5,6},{6,5},{7,8},{8,7},{9,10},{10,9},{11,... | collective-permute-start | bytes 503816 | tf_op jit(solution)/shard_map/ppermute | solution.py:374
  32.5 11.3 %collective-permute-start.3 = (s16[656,128]{1,0:T(8,128)(2,1)S(1)}, s16[656,128]{1,0:T(8,128)(2,1)S(1)}, u32[]{:S(2)}, u32[]{:S(2)}) collective-permute-start(s16[656,128]{1,0:T(8,128)(2,1)S(1)} %get-tuple-element.19), channel_id=1, source_target_pairs={{0,1},{1,0},{2,3},{3,2},{4,5},{5,4},{6,7},{7,6},{8,9},{9,8},{10,11... | collective-permute-start | bytes 503816 | tf_op jit(solution)/shard_map/ppermute | solution.py:374
  33.3 18.2 %all-to-all-start.1 = ((f32[64,1,128]{2,1,0:T(1,128)}), f32[64,1,128]{2,1,0:T(1,128)S(1)}, u32[]{:S(2)}, u32[]{:S(2)}) async-start(f32[64,1,128]{2,1,0:T(1,128)} %shard_map.108), calls=%async_computation.1 | async-start | bytes 65536 | tf_op jit(solution)/shard_map/all_to_all | solution.py:428
